TPU v7x, 32 devices: a whole 2x2x4 slice. The times are simulated.
32 devices in a mesh: page: 4 (over x, core), blk: 8 (over z, y).
Axes of the slice: x: 2, y: 2, z: 4, core: 2. Of those that a mesh axis runs over, the one named last changes fastest.
Arguments:
- visual_in: bfloat16 [4608, 768], P(('page', 'blk')), may hold values from -6 to 6
- question_in: bfloat16 [4096, 768], P('page'), may hold values from -6 to 6
- segment_ids: int32 [4, 1024], P('page'), may hold values from 0 to 5, never falling along the last dimension, each value on 1 to 512 neighbouring positions
- regions: int32 [4608], P(('page', 'blk')), may hold values from 0 to 3
- rel_index: int32 [144, 144], replicated, may hold values from 0 to 528
- rel_table: float32 [12, 529], replicated, may hold values from -3 to 3
- window_project: bfloat16 [1769472], P(('page', 'blk')), may hold values from -0.21875 to 0.21875
- window_output: bfloat16 [589824], P(('page', 'blk')), may hold values from -0.875 to 0.875
- causal_project: bfloat16 [1769472], P(('page', 'blk')), may hold values from -0.21875 to 0.21875
- causal_output: bfloat16 [589824], P(('page', 'blk')), may hold values from -1.25 to 1.25
- reader_query: bfloat16 [589824], P(('page', 'blk')), may hold values from -0.4375 to 0.4375
- reader_pair: bfloat16 [1179648], P(('page', 'blk')), may hold values from -0.21875 to 0.21875
- reader_output: bfloat16 [589824], P(('page', 'blk')), may hold values from -1.75 to 1.75
- viewer_query: bfloat16 [589824], P(('page', 'blk')), may hold values from -0.3125 to 0.3125
- viewer_pair: bfloat16 [1179648], P(('page', 'blk')), may hold values from -0.21875 to 0.21875
- viewer_output: bfloat16 [589824], P(('page', 'blk')), may hold values from -1.75 to 1.75
- visual_up: bfloat16 [2359296], P(('page', 'blk')), may hold values from -0.21875 to 0.21875
- visual_down: bfloat16 [2359296], P(('page', 'blk')), may hold values from -0.15625 to 0.15625
- question_up: bfloat16 [2359296], P(('page', 'blk')), may hold values from -0.21875 to 0.21875
- question_down: bfloat16 [2359296], P(('page', 'blk')), may hold values from -0.15625 to 0.15625
- norm_gains: bfloat16 [4608], P(('page', 'blk')), may hold values from 0.5 to 1.5
- norm_shifts: bfloat16 [4608], P(('page', 'blk')), may hold values from -1 to 1
- visual_cot: bfloat16 [4608, 768], P(('page', 'blk')), may hold values from -6 to 6
- question_cot: bfloat16 [4096, 768], P('page'), may hold values from -6 to 6
Outputs:
- visual_out: bfloat16 [4608, 768], P(('page', 'blk'))
- question_out: bfloat16 [4096, 768], P('page')
- visual_delta: float32 [4608, 768], P(('page', 'blk'))
- question_delta: float32 [4096, 768], P('page')
- table_delta: float32 [12, 529], replicated
- delta_window_project: float32 [1769472], P(('page', 'blk'))
- delta_window_output: float32 [589824], P(('page', 'blk'))
- delta_causal_project: float32 [1769472], P(('page', 'blk'))
- delta_causal_output: float32 [589824], P(('page', 'blk'))
- delta_reader_query: float32 [589824], P(('page', 'blk'))
- delta_reader_pair: float32 [1179648], P(('page', 'blk'))
- delta_reader_output: float32 [589824], P(('page', 'blk'))
- delta_viewer_query: float32 [589824], P(('page', 'blk'))
- delta_viewer_pair: float32 [1179648], P(('page', 'blk'))
- delta_viewer_output: float32 [589824], P(('page', 'blk'))
- delta_visual_up: float32 [2359296], P(('page', 'blk'))
- delta_visual_down: float32 [2359296], P(('page', 'blk'))
- delta_question_up: float32 [2359296], P(('page', 'blk'))
- delta_question_down: float32 [2359296], P(('page', 'blk'))
- delta_norm_gains: float32 [4608], P(('page', 'blk'))
- delta_norm_shifts: float32 [4608], P(('page', 'blk'))
- delta_question_shift: float32 [768], replicated
Inputs may be any that keep to these rules, and one draw needn't show every extreme that they name: `segment_ids`: within a page question numbers never fall along the tokens, each question has 1 to 512 tokens and one has exactly that many.
All inputs are finite; a program needn't handle non-finite values.
Results may differ from a plain program's by a relative error of at most 0.025.
Values may be sent and summed in bfloat16 or wider, within the bound.
No kernel may reach another device: no remote copies, remote signals or barrier semaphores. Data moves between devices by JAX's collectives and lax.ppermute only.
A program may use at most 384 MiB of HBM per device.

v0:
```python
import jax
import jax.numpy as jnp
from jax import lax
from jax.sharding import PartitionSpec as P

D = 768
HEADS = 12
HEAD_DIM = 64
FF = 3072
Q_LEN = 1024
WIN = 144
RELS = 529


EPS = 1e-05
NEG = -1000000000.0


def matrix_shapes():
    return (
        (D, 3 * D),
        (D, D),
        (D, 3 * D),
        (D, D),
        (D, D),
        (D, 2 * D),
        (D, D),
        (D, D),
        (D, 2 * D),
        (D, D),
        (D, FF),
        (FF, D),
        (D, FF),
        (FF, D),
        (6, D),
        (6, D),
    )


def product(left, right):
    return jnp.dot(left, right, preferred_element_type=jnp.float32)


def times_transposed(left, right):
    return lax.dot_general(
        left, right, (((1,), (1,)), ((), ())), preferred_element_type=jnp.float32
    )


def transposed_times(left, right):
    return lax.dot_general(
        left, right, (((0,), (0,)), ((), ())), preferred_element_type=jnp.float32
    )


def normalize(rows, gain, shift):
    mean = jnp.mean(rows, axis=-1, keepdims=True)
    centred = rows - mean
    spread = jnp.mean(centred * centred, axis=-1, keepdims=True)
    return centred * lax.rsqrt(spread + EPS) * gain + shift


def smooth(values):
    return jax.nn.gelu(values, approximate=False)


def split_heads(rows):
    return rows.reshape(rows.shape[0], HEADS, HEAD_DIM)


def local_scores(queries, keys, extra):
    raw = jnp.einsum("bnhe,bmhe->bhnm", queries, keys, preferred_element_type=jnp.float32)
    return raw * HEAD_DIM ** (-0.5) + extra


def local_attend(queries, keys, values, extra):
    shares = jax.nn.softmax(local_scores(queries, keys, extra), axis=-1)
    return jnp.einsum(
        "bhnm,bmhe->bnhe", shares.astype(jnp.bfloat16), values, preferred_element_type=jnp.float32
    )


def local_backward(queries, keys, values, extra, back_out):
    shares = jax.nn.softmax(local_scores(queries, keys, extra), axis=-1)
    back_values = jnp.einsum(
        "bhnm,bnhe->bmhe", shares.astype(jnp.bfloat16), back_out, preferred_element_type=jnp.float32
    )
    back_shares = jnp.einsum(
        "bnhe,bmhe->bhnm", back_out, values, preferred_element_type=jnp.float32
    )
    inner = jnp.sum(shares * back_shares, axis=-1, keepdims=True)
    back_scores = (shares * (back_shares - inner)).astype(jnp.bfloat16)
    back_queries = jnp.einsum(
        "bhnm,bmhe->bnhe", back_scores, keys, preferred_element_type=jnp.float32
    ) * HEAD_DIM ** (-0.5)
    back_keys = jnp.einsum(
        "bhnm,bnhe->bmhe", back_scores, queries, preferred_element_type=jnp.float32
    ) * HEAD_DIM ** (-0.5)
    return (back_queries, back_keys, back_values, back_scores)


def key_partial(queries, keys, values):
    scores = jnp.einsum(
        "nhe,mhe->nhm", queries, keys, preferred_element_type=jnp.float32
    ) * HEAD_DIM ** (-0.5)
    top = jnp.max(scores, axis=-1)
    expo = jnp.exp(scores - top[..., None])
    total = jnp.sum(expo, axis=-1)
    part = jnp.einsum(
        "nhm,mhe->nhe", expo.astype(jnp.bfloat16), values, preferred_element_type=jnp.float32
    )
    return (top, total, part.reshape(part.shape[0], -1))


def combine(first, second):
    top = jnp.maximum(first[0], second[0])
    left = jnp.exp(first[0] - top)
    right = jnp.exp(second[0] - top)
    total = first[1] * left + second[1] * right
    part = split_heads(first[2]) * left[..., None] + split_heads(second[2]) * right[..., None]
    return (top, total, part.reshape(part.shape[0], -1))


def key_terms(queries, keys, values, log_total, inner, back_out):
    scores = jnp.einsum(
        "nhe,mhe->nhm", queries, keys, preferred_element_type=jnp.float32
    ) * HEAD_DIM ** (-0.5)
    top = jnp.max(scores, axis=-1)
    expo = jnp.exp(scores - top[..., None])
    factor = jnp.exp(top - log_total)
    back_part = (back_out.astype(jnp.float32) * factor[..., None]).astype(jnp.bfloat16)
    back_expo = jnp.einsum("nhe,mhe->nhm", back_part, values, preferred_element_type=jnp.float32)
    shares = jnp.exp(scores - log_total[..., None])
    back_scores = (expo * back_expo - shares * inner[..., None]).astype(jnp.bfloat16)
    return (expo, back_part, back_scores)


def key_query_backward(queries, keys, values, log_total, inner, back_out):
    unused, unused_part, back_scores = key_terms(queries, keys, values, log_total, inner, back_out)
    return jnp.einsum(
        "nhm,mhe->nhe", back_scores, keys, preferred_element_type=jnp.float32
    ) * HEAD_DIM ** (-0.5)


def key_side_backward(queries, keys, values, log_total, inner, back_out):
    expo, back_part, back_scores = key_terms(queries, keys, values, log_total, inner, back_out)
    back_values = jnp.einsum(
        "nhm,nhe->mhe", expo.astype(jnp.bfloat16), back_part, preferred_element_type=jnp.float32
    )
    back_keys = jnp.einsum(
        "nhm,nhe->mhe", back_scores, queries, preferred_element_type=jnp.float32
    ) * HEAD_DIM ** (-0.5)
    back_queries = jnp.einsum(
        "nhm,mhe->nhe", back_scores, keys, preferred_element_type=jnp.float32
    ) * HEAD_DIM ** (-0.5)
    return (back_queries, back_keys, back_values)


def feed_forward(rows, gain, shift, up_weight, down_weight):
    normed, norm_pull = jax.vjp(normalize, rows, gain, shift)
    normed_low = normed.astype(jnp.bfloat16)
    upward = product(normed_low, up_weight)
    active, gelu_pull = jax.vjp(smooth, upward)
    active_low = active.astype(jnp.bfloat16)
    return (rows + product(active_low, down_weight), (norm_pull, normed_low, gelu_pull, active_low))


def feed_back(back_rows, kept, up_weight, down_weight):
    norm_pull, normed_low, gelu_pull, active_low = kept
    branch = back_rows.astype(jnp.bfloat16)
    delta_down = transposed_times(active_low, branch)
    back_active = times_transposed(branch, down_weight)
    (back_up,) = gelu_pull(back_active)
    back_up_low = back_up.astype(jnp.bfloat16)
    delta_up = transposed_times(normed_low, back_up_low)
    back_normed = times_transposed(back_up_low, up_weight)
    back_in, delta_gain, delta_shift = norm_pull(back_normed)
    return (back_rows + back_in, delta_up, delta_down, delta_gain, delta_shift)


def body(
    visual_in,
    question_in,
    segment_ids,
    regions,
    rel_index,
    rel_table,
    window_project,
    window_output,
    causal_project,
    causal_output,
    reader_query,
    reader_pair,
    reader_output,
    viewer_query,
    viewer_pair,
    viewer_output,
    visual_up,
    visual_down,
    question_up,
    question_down,
    norm_gains,
    norm_shifts,
    visual_cot,
    question_cot,
):
    blocks = lax.axis_size("blk")
    share = Q_LEN // blocks
    first = lax.axis_index("blk") * share
    rows_here = visual_in.shape[0]
    gathered = (
        lax.all_gather(window_project, ("page", "blk"), axis=0, tiled=True),
        lax.all_gather(window_output, ("page", "blk"), axis=0, tiled=True),
        lax.all_gather(causal_project, ("page", "blk"), axis=0, tiled=True),
        lax.all_gather(causal_output, ("page", "blk"), axis=0, tiled=True),
        lax.all_gather(reader_query, ("page", "blk"), axis=0, tiled=True),
        lax.all_gather(reader_pair, ("page", "blk"), axis=0, tiled=True),
        lax.all_gather(reader_output, ("page", "blk"), axis=0, tiled=True),
        lax.all_gather(viewer_query, ("page", "blk"), axis=0, tiled=True),
        lax.all_gather(viewer_pair, ("page", "blk"), axis=0, tiled=True),
        lax.all_gather(viewer_output, ("page", "blk"), axis=0, tiled=True),
        lax.all_gather(visual_up, ("page", "blk"), axis=0, tiled=True),
        lax.all_gather(visual_down, ("page", "blk"), axis=0, tiled=True),
        lax.all_gather(question_up, ("page", "blk"), axis=0, tiled=True),
        lax.all_gather(question_down, ("page", "blk"), axis=0, tiled=True),
        lax.all_gather(norm_gains, ("page", "blk"), axis=0, tiled=True),
        lax.all_gather(norm_shifts, ("page", "blk"), axis=0, tiled=True),
    )
    (
        window_weight,
        window_exit,
        causal_weight,
        causal_exit,
        reader_weight,
        reader_pair_weight,
        reader_exit,
        viewer_weight,
        viewer_pair_weight,
        viewer_exit,
        visual_raise,
        visual_lower,
        question_raise,
        question_lower,
        gain_rows,
        shift_rows,
    ) = [piece.reshape(shape) for piece, shape in zip(gathered, matrix_shapes())]
    gains = gain_rows.astype(jnp.float32)
    shifts = shift_rows.astype(jnp.float32)
    visual = visual_in.astype(jnp.float32)
    question_own = lax.dynamic_slice_in_dim(question_in, first, share, 0).astype(jnp.float32)
    marks_all = segment_ids[0]
    marks_own = lax.dynamic_slice_in_dim(marks_all, first, share, 0)
    win_norm, win_pull = jax.vjp(normalize, visual, gains[0], shifts[0])
    win_low = win_norm.astype(jnp.bfloat16)
    win_proj = product(win_low, window_weight).astype(jnp.bfloat16)
    windows = rows_here // WIN

    def as_windows(part):
        return part.reshape(windows, WIN, HEADS, HEAD_DIM)

    win_query = as_windows(win_proj[:, :D])
    win_keys = as_windows(win_proj[:, D : 2 * D])
    win_values = as_windows(win_proj[:, 2 * D :])
    labels = regions.reshape(windows, WIN)
    bias = rel_table[:, rel_index]
    win_extra = bias[None] + jnp.where(labels[:, :, None] == labels[:, None, :], 0.0, NEG)[:, None]
    win_attn = (
        local_attend(win_query, win_keys, win_values, win_extra).reshape(-1, D).astype(jnp.bfloat16)
    )
    visual_one = visual + product(win_attn, window_exit)
    self_norm, self_pull = jax.vjp(normalize, question_own, gains[1], shifts[1])
    self_low = self_norm.astype(jnp.bfloat16)
    self_query = product(self_low, causal_weight[:, :D]).astype(jnp.bfloat16)
    every_low = normalize(question_in.astype(jnp.float32), gains[1], shifts[1]).astype(jnp.bfloat16)
    self_pair = product(every_low, causal_weight[:, D:]).astype(jnp.bfloat16)
    own_place = first + jnp.arange(share)
    place = jnp.arange(Q_LEN)
    causal = (marks_own[:, None] == marks_all[None, :]) & (place[None, :] <= own_place[:, None])
    self_extra = jnp.where(causal, 0.0, NEG)[None, None]
    self_keys = split_heads(self_pair[:, :D])[None]
    self_values = split_heads(self_pair[:, D:])[None]
    self_heads = split_heads(self_query)[None]
    self_attn = (
        local_attend(self_heads, self_keys, self_values, self_extra)[0]
        .reshape(share, D)
        .astype(jnp.bfloat16)
    )
    question_one = question_own + product(self_attn, causal_exit)
    cross_norm, cross_pull = jax.vjp(normalize, question_one, gains[2], shifts[2])
    cross_low = cross_norm.astype(jnp.bfloat16)
    vis_norm, vis_pull = jax.vjp(normalize, visual_one, gains[3], shifts[3])
    vis_low = vis_norm.astype(jnp.bfloat16)
    qv_query = product(cross_low, reader_weight).astype(jnp.bfloat16)
    vq_pair = product(cross_low, viewer_pair_weight).astype(jnp.bfloat16)
    qv_query_all, vq_pair_all = (
        lax.all_gather(qv_query, "blk", axis=0, tiled=True),
        lax.all_gather(vq_pair, "blk", axis=0, tiled=True),
    )
    qv_pair = product(vis_low, reader_pair_weight).astype(jnp.bfloat16)
    vq_query = product(vis_low, viewer_weight).astype(jnp.bfloat16)
    start_state = (
        jnp.full((share, HEADS), NEG, jnp.float32),
        jnp.zeros((share, HEADS), jnp.float32),
        jnp.zeros((share, D), jnp.float32),
    )
    state = start_state
    stacked = lax.all_gather(qv_pair, "blk", axis=0, tiled=True).reshape(-1, rows_here, 2 * D)

    def fold_one_block(carry, block):
        found = key_partial(
            split_heads(qv_query), split_heads(block[:, :D]), split_heads(block[:, D:])
        )
        return (combine(carry, found), None)

    state, unused = lax.scan(fold_one_block, state, stacked)
    top, total, part = state
    log_total = top + jnp.log(total)
    qv_attn = split_heads(part) / total[..., None]
    qv_flat = qv_attn.reshape(share, D).astype(jnp.bfloat16)
    question_two = question_one + product(qv_flat, reader_exit)
    vq_keys = split_heads(vq_pair_all[:, :D])[None]
    vq_values = split_heads(vq_pair_all[:, D:])[None]
    vq_heads = split_heads(vq_query)[None]
    vq_attn = local_attend(vq_heads, vq_keys, vq_values, 0.0)[0].reshape(-1, D).astype(jnp.bfloat16)
    visual_two = visual_one + product(vq_attn, viewer_exit)
    visual_three, visual_kept = feed_forward(
        visual_two, gains[4], shifts[4], visual_raise, visual_lower
    )
    question_three, question_kept = feed_forward(
        question_two, gains[5], shifts[5], question_raise, question_lower
    )
    question_out = lax.all_gather(question_three.astype(jnp.bfloat16), "blk", axis=0, tiled=True)
    back_visual_two, delta_visual_up, delta_visual_down, gain_visual_mlp, shift_visual_mlp = (
        feed_back(visual_cot.astype(jnp.float32), visual_kept, visual_raise, visual_lower)
    )
    question_cot_own = lax.dynamic_slice_in_dim(question_cot, first, share, 0).astype(jnp.float32)
    (
        back_question_two,
        delta_question_up,
        delta_question_down,
        gain_question_mlp,
        shift_question_mlp,
    ) = feed_back(question_cot_own, question_kept, question_raise, question_lower)
    vq_branch = back_visual_two.astype(jnp.bfloat16)
    delta_viewer_output = transposed_times(vq_attn, vq_branch)
    back_vq_attn = times_transposed(vq_branch, viewer_exit).astype(jnp.bfloat16)
    vq_back_query, vq_back_keys, vq_back_values, unused = local_backward(
        vq_heads, vq_keys, vq_values, 0.0, split_heads(back_vq_attn)[None]
    )
    qv_branch = back_question_two.astype(jnp.bfloat16)
    delta_reader_output = transposed_times(qv_flat, qv_branch)
    back_qv_attn = times_transposed(qv_branch, reader_exit).astype(jnp.bfloat16)
    inner_own = jnp.sum(split_heads(back_qv_attn.astype(jnp.float32)) * qv_attn, axis=-1)
    back_rows_all, log_all, inner_all = (
        lax.all_gather(back_qv_attn.astype(jnp.float32), "blk", axis=0, tiled=True),
        lax.all_gather(log_total, "blk", axis=0, tiled=True),
        lax.all_gather(inner_own, "blk", axis=0, tiled=True),
    )
    qv_back_query, qv_back_keys, qv_back_values = key_side_backward(
        split_heads(qv_query_all),
        split_heads(qv_pair[:, :D]),
        split_heads(qv_pair[:, D:]),
        log_all,
        inner_all,
        split_heads(back_rows_all.astype(jnp.bfloat16)),
    )
    viewer_pair_partial = jnp.concatenate(
        [vq_back_keys[0].reshape(Q_LEN, D), vq_back_values[0].reshape(Q_LEN, D)], 1
    )
    own_back_heads = split_heads(back_qv_attn)
    carry = jnp.zeros((share, HEADS, HEAD_DIM), jnp.float32)
    stacked = lax.all_gather(qv_pair, "blk", axis=0, tiled=True).reshape(-1, rows_here, 2 * D)

    def back_one_block(running, block):
        found = key_query_backward(
            split_heads(qv_query),
            split_heads(block[:, :D]),
            split_heads(block[:, D:]),
            log_total,
            inner_own,
            own_back_heads,
        )
        return (running + found, None)

    carry, unused_rows = lax.scan(back_one_block, carry, stacked)
    query_sum = carry.reshape(share, D)
    pair_sum = lax.psum_scatter(viewer_pair_partial, "blk", scatter_dimension=0, tiled=True)
    vq_pair_back = pair_sum.astype(jnp.bfloat16)
    qv_query_back = query_sum.astype(jnp.bfloat16)
    delta_reader_query = transposed_times(cross_low, qv_query_back)
    delta_viewer_pair = transposed_times(cross_low, vq_pair_back)
    back_cross = times_transposed(qv_query_back, reader_weight) + times_transposed(
        vq_pair_back, viewer_pair_weight
    )
    back_cross_in, gain_cross, shift_cross = cross_pull(back_cross)
    back_question_one = back_question_two + back_cross_in
    qv_pair_back = jnp.concatenate(
        [qv_back_keys.reshape(-1, D), qv_back_values.reshape(-1, D)], 1
    ).astype(jnp.bfloat16)
    vq_query_back = vq_back_query[0].reshape(-1, D).astype(jnp.bfloat16)
    delta_reader_pair = transposed_times(vis_low, qv_pair_back)
    delta_viewer_query = transposed_times(vis_low, vq_query_back)
    back_vis = times_transposed(qv_pair_back, reader_pair_weight) + times_transposed(
        vq_query_back, viewer_weight
    )
    back_vis_in, gain_vis, shift_vis = vis_pull(back_vis)
    back_visual_one = back_visual_two + back_vis_in
    self_branch = back_question_one.astype(jnp.bfloat16)
    delta_causal_output = transposed_times(self_attn, self_branch)
    back_self_attn = times_transposed(self_branch, causal_exit).astype(jnp.bfloat16)
    self_back_query, self_back_keys, self_back_values, unused = local_backward(
        self_heads, self_keys, self_values, self_extra, split_heads(back_self_attn)[None]
    )
    pair_partial = jnp.concatenate(
        [self_back_keys[0].reshape(Q_LEN, D), self_back_values[0].reshape(Q_LEN, D)], 1
    )
    pair_own = lax.psum_scatter(pair_partial, "blk", scatter_dimension=0, tiled=True)
    self_back = jnp.concatenate([self_back_query[0].reshape(share, D), pair_own], 1).astype(
        jnp.bfloat16
    )
    delta_causal_project = transposed_times(self_low, self_back)
    back_self_in, gain_self, shift_self = self_pull(times_transposed(self_back, causal_weight))
    back_question = back_question_one + back_self_in
    win_branch = back_visual_one.astype(jnp.bfloat16)
    delta_window_output = transposed_times(win_attn, win_branch)
    back_win_attn = times_transposed(win_branch, window_exit).astype(jnp.bfloat16)
    win_back_query, win_back_keys, win_back_values, win_back_scores = local_backward(
        win_query, win_keys, win_values, win_extra, as_windows(back_win_attn)
    )
    win_back = jnp.concatenate(
        [
            win_back_query.reshape(-1, D),
            win_back_keys.reshape(-1, D),
            win_back_values.reshape(-1, D),
        ],
        1,
    ).astype(jnp.bfloat16)
    delta_window_project = transposed_times(win_low, win_back)
    back_win_in, gain_win, shift_win = win_pull(times_transposed(win_back, window_weight))
    back_visual = back_visual_one + back_win_in
    table_local = jnp.sum(win_back_scores.astype(jnp.float32), axis=0).reshape(HEADS, -1)
    table_part = jax.ops.segment_sum(table_local.T, rel_index.reshape(-1), num_segments=RELS).T
    gain_delta = jnp.stack(
        [gain_win, gain_self, gain_cross, gain_vis, gain_visual_mlp, gain_question_mlp]
    )
    shift_delta = jnp.stack(
        [shift_win, shift_self, shift_cross, shift_vis, shift_visual_mlp, shift_question_mlp]
    )
    summed = (
        lax.psum_scatter(
            delta_window_project.reshape(-1), ("page", "blk"), scatter_dimension=0, tiled=True
        ),
        lax.psum_scatter(
            delta_window_output.reshape(-1), ("page", "blk"), scatter_dimension=0, tiled=True
        ),
        lax.psum_scatter(
            delta_causal_project.reshape(-1), ("page", "blk"), scatter_dimension=0, tiled=True
        ),
        lax.psum_scatter(
            delta_causal_output.reshape(-1), ("page", "blk"), scatter_dimension=0, tiled=True
        ),
        lax.psum_scatter(
            delta_reader_query.reshape(-1), ("page", "blk"), scatter_dimension=0, tiled=True
        ),
        lax.psum_scatter(
            delta_reader_pair.reshape(-1), ("page", "blk"), scatter_dimension=0, tiled=True
        ),
        lax.psum_scatter(
            delta_reader_output.reshape(-1), ("page", "blk"), scatter_dimension=0, tiled=True
        ),
        lax.psum_scatter(
            delta_viewer_query.reshape(-1), ("page", "blk"), scatter_dimension=0, tiled=True
        ),
        lax.psum_scatter(
            delta_viewer_pair.reshape(-1), ("page", "blk"), scatter_dimension=0, tiled=True
        ),
        lax.psum_scatter(
            delta_viewer_output.reshape(-1), ("page", "blk"), scatter_dimension=0, tiled=True
        ),
        lax.psum_scatter(
            delta_visual_up.reshape(-1), ("page", "blk"), scatter_dimension=0, tiled=True
        ),
        lax.psum_scatter(
            delta_visual_down.reshape(-1), ("page", "blk"), scatter_dimension=0, tiled=True
        ),
        lax.psum_scatter(
            delta_question_up.reshape(-1), ("page", "blk"), scatter_dimension=0, tiled=True
        ),
        lax.psum_scatter(
            delta_question_down.reshape(-1), ("page", "blk"), scatter_dimension=0, tiled=True
        ),
        lax.psum_scatter(gain_delta.reshape(-1), ("page", "blk"), scatter_dimension=0, tiled=True),
        lax.psum_scatter(shift_delta.reshape(-1), ("page", "blk"), scatter_dimension=0, tiled=True),
    )
    table_delta, question_shift = lax.psum((table_part, shift_question_mlp), ("page", "blk"))
    question_delta = lax.all_gather(back_question, "blk", axis=0, tiled=True)
    return (
        visual_three.astype(jnp.bfloat16),
        question_out,
        back_visual,
        question_delta,
        table_delta,
        summed[0],
        summed[1],
        summed[2],
        summed[3],
        summed[4],
        summed[5],
        summed[6],
        summed[7],
        summed[8],
        summed[9],
        summed[10],
        summed[11],
        summed[12],
        summed[13],
        summed[14],
        summed[15],
        question_shift,
    )


def solution(mesh):
    in_specs = (
        P(("page", "blk"), None),
        P("page", None),
        P("page", None),
        P(("page", "blk")),
        P(),
        P(),
        P(("page", "blk")),
        P(("page", "blk")),
        P(("page", "blk")),
        P(("page", "blk")),
        P(("page", "blk")),
        P(("page", "blk")),
        P(("page", "blk")),
        P(("page", "blk")),
        P(("page", "blk")),
        P(("page", "blk")),
        P(("page", "blk")),
        P(("page", "blk")),
        P(("page", "blk")),
        P(("page", "blk")),
        P(("page", "blk")),
        P(("page", "blk")),
        P(("page", "blk"), None),
        P("page", None),
    )
    out_specs = (
        P(("page", "blk"), None),
        P("page", None),
        P(("page", "blk"), None),
        P("page", None),
        P(),
        P(("page", "blk")),
        P(("page", "blk")),
        P(("page", "blk")),
        P(("page", "blk")),
        P(("page", "blk")),
        P(("page", "blk")),
        P(("page", "blk")),
        P(("page", "blk")),
        P(("page", "blk")),
        P(("page", "blk")),
        P(("page", "blk")),
        P(("page", "blk")),
        P(("page", "blk")),
        P(("page", "blk")),
        P(("page", "blk")),
        P(("page", "blk")),
        P(),
    )
    return jax.shard_map(body, mesh=mesh, in_specs=in_specs, out_specs=out_specs, check_vma=False)
```

profile of v0, /device:TPU:0, one launch (start us, length us, event | category | flops | bytes accessed | tf_op | source)
XLA Modules:
  0.0 2665.5 jit_solution(18006951241829797062)
XLA Ops:
  15.8 42.4 %all-reduce.20 = (bf16[4608]{0:T(1024)(128)(2,1)S(1)}, bf16[4608]{0:T(1024)(128)(2,1)S(1)}) all-reduce(bf16[4608]{0:T(1024)(128)(2,1)S(1)} %dynamic-update-slice, bf16[4608]{0:T(1024)(128)(2,1)S(1)} %dynamic-update-slice.1), channel_id=1, replica_groups=mesh['page'=4,'blk'=8] {'page','blk'}, use_global_device_ids=true, to_apply=%add | all-reduce | flops 9216 | bytes 36864
  70.5 56.7 %all-gather.29.cloned.1.call-done = bf16[1179648]{0:T(1024)(128)(2,1)} async-done(((bf16[36864]{0:T(1024)(128)(2,1)}), bf16[1179648]{0:T(1024)(128)(2,1)}) %all-gather.29.cloned.1.call-update) | async-done | bytes 2359312 | tf_op jit(solution)/shard_map/all_gather | solution.py:220
  131.7 57.4 %all-gather.25.cloned.1.call-done = bf16[1769472]{0:T(1024)(128)(2,1)} async-done(((bf16[55296]{0:T(1024)(128)(2,1)}), bf16[1769472]{0:T(1024)(128)(2,1)}) %all-gather.25.cloned.1.call-update) | async-done | bytes 3538960 | tf_op jit(solution)/shard_map/all_gather | solution.py:214
  231.8 38.9 %gather_fusion = f32[20736,12]{1,0:T(8,128)} fusion(f32[12,529]{0,1:T(8,128)S(1)} %copy.125, s32[21504]{0:T(1024)S(1)} %pad_clamp_fusion), kind=kCustom, calls=%fused_computation | custom fusion | bytes 2073600 | tf_op jit(solution)/shard_map/gather | solution.py:265
  287.9 12.9 all-gather.33.cloned.1.call-done
  304.2 52.5 %all-gather.35.cloned.1.call-done = bf16[589824]{0:T(1024)(128)(2,1)} async-done(((bf16[18432]{0:T(1024)(128)(2,1)}), bf16[589824]{0:T(1024)(128)(2,1)}) %all-gather.35.cloned.1.call-update) | async-done | bytes 1179664 | tf_op jit(solution)/shard_map/all_gather | solution.py:221
  360.1 55.8 %all-gather.41.cloned.1.call-done = bf16[1179648]{0:T(1024)(128)(2,1)} async-done(((bf16[36864]{0:T(1024)(128)(2,1)}), bf16[1179648]{0:T(1024)(128)(2,1)}) %all-gather.41.cloned.1.call-update) | async-done | bytes 2359312 | tf_op jit(solution)/shard_map/all_gather | solution.py:217
  421.4 56.4 %all-gather.21.cloned.1.call-done = bf16[1769472]{0:T(1024)(128)(2,1)} async-done(((bf16[55296]{0:T(1024)(128)(2,1)}), bf16[1769472]{0:T(1024)(128)(2,1)}) %all-gather.21.cloned.1.call-update) | async-done | bytes 3538960 | tf_op jit(solution)/shard_map/all_gather | solution.py:212
  502.0 41.3 %all-gather.37.cloned.1.call-done = bf16[2359296]{0:T(1024)(128)(2,1)} async-done(((bf16[73728]{0:T(1024)(128)(2,1)}), bf16[2359296]{0:T(1024)(128)(2,1)}) %all-gather.37.cloned.1.call-update) | async-done | bytes 4718608 | tf_op jit(solution)/shard_map/all_gather | solution.py:222
  551.5 57.1 %all-gather.39.cloned.1.call-done = bf16[2359296]{0:T(1024)(128)(2,1)} async-done(((bf16[73728]{0:T(1024)(128)(2,1)}), bf16[2359296]{0:T(1024)(128)(2,1)}) %all-gather.39.cloned.1.call-update) | async-done | bytes 4718608 | tf_op jit(solution)/shard_map/all_gather | solution.py:223
  617.8 52.8 %all-gather.31.cloned.1.call-done = bf16[1024,1536]{1,0:T(8,128)(2,1)} async-done(((bf16[128,1536]{1,0:T(8,128)(2,1)}), bf16[1024,1536]{1,0:T(8,128)(2,1)}) %all-gather.31.cloned.1.call-update) | async-done | bytes 3145744 | tf_op jit(solution)/shard_map/all_gather | solution.py:297
  728.8 53.5 %all-gather.47.cloned.1.call-done = bf16[589824]{0:T(1024)(128)(2,1)} async-done(((bf16[18432]{0:T(1024)(128)(2,1)}), bf16[589824]{0:T(1024)(128)(2,1)}) %all-gather.47.cloned.1.call-update) | async-done | bytes 1179664 | tf_op jit(solution)/shard_map/all_gather | solution.py:218
  786.7 60.9 %all-gather.49.cloned.1.call-done = bf16[2359296]{0:T(1024)(128)(2,1)} async-done(((bf16[73728]{0:T(1024)(128)(2,1)}), bf16[2359296]{0:T(1024)(128)(2,1)}) %all-gather.49.cloned.1.call-update) | async-done | bytes 4718608 | tf_op jit(solution)/shard_map/all_gather | solution.py:224
  855.8 57.1 %all-gather.51.cloned.1.call-done = bf16[2359296]{0:T(1024)(128)(2,1)} async-done(((bf16[73728]{0:T(1024)(128)(2,1)}), bf16[2359296]{0:T(1024)(128)(2,1)}) %all-gather.51.cloned.1.call-update) | async-done | bytes 4718608 | tf_op jit(solution)/shard_map/all_gather | solution.py:225
  922.1 56.8 %all-gather.43.cloned.1.call-done = bf16[1152,1536]{1,0:T(8,128)(2,1)} async-done(((bf16[144,1536]{1,0:T(8,128)(2,1)}), bf16[1152,1536]{1,0:T(8,128)(2,1)}) %all-gather.43.cloned.1.call-update) | async-done | bytes 3538960 | tf_op jit(solution)/shard_map/all_gather | solution.py:307
  986.6 17.1 while.26
  1023.1 37.0 %while.27 = (s32[]{:T(128)}, f32[128,12,64]{0,2,1:T(8,128)}, bf16[8,144,1536]{1,2,0:T(8,128)(2,1)}, bf16[128,768]{0,1:T(8,128)(2,1)S(1)}, bf16[128,12,64]{0,2,1:...) while((s32[]{:T(128)}, f32[128,12,64]{0,2,1:T(8,128)}, ...), condition=%wide.region_38.39_spmd.clone, body=%wide.region_36.38_spmd.clone.sunk | while | flops 87293952 | bytes 8577195 | solution.py:385
  1061.2 38.1 %reduce-scatter.3.cloned.1.call-done = f32[128,1536]{0,1:T(8,128)} async-done(((f32[1024,1536]{0,1:T(8,128)}), f32[128,1536]{0,1:T(8,128)}) %reduce-scatter.3.cloned.1.call-update) | async-done | bytes 786448 | tf_op jit(solution)/shard_map/reduce_scatter | solution.py:387
  1122.8 22.4 all-gather.55.cloned.1.call-done
  1243.3 30.9 %all_gather.94 = f32[1024,12]{0,1:T(8,128)S(1)} all-gather(f32[128,12]{0,1:T(8,128)S(1)} %get-tuple-element.691), channel_id=1, replica_groups=mesh['page'=4,'blk'=8] {'blk'}, dimensions={0}, use_global_device_ids=true | all-gather | bytes 55296 | tf_op jit(solution)/shard_map/all_gather | solution.py:356
  1274.3 31.4 %all_gather.95 = f32[1024,12]{0,1:T(8,128)S(1)} all-gather(f32[128,12]{0,1:T(8,128)S(1)} %copy-done.127), channel_id=1, replica_groups=mesh['page'=4,'blk'=8] {'blk'}, dimensions={0}, use_global_device_ids=true | all-gather | bytes 55296 | tf_op jit(solution)/shard_map/all_gather | solution.py:357
  1421.1 112.5 %scatter_custom_fusion = f32[529,12]{1,0:T(8,128)S(1)} fusion(s32[20736]{0:T(1024)} %reshape.883, f32[20736,12]{1,0:T(8,128)} %copy.152, f32[]{:T(128)} %constant.64.clone.1), kind=kCustom, calls=%fused_computation.259 | custom fusion | flops 248832 | bytes 25904 | tf_op jit(solution)/shard_map/scatter-add | solution.py:442
  1536.0 47.2 %all-reduce.18 = (f32[12,529]{0,1:T(8,128)S(1)}, f32[4608]{0:T(1024)S(1)}, f32[4608]{0:T(1024)S(1)}, f32[768]{0:T(1024)}) all-reduce(f32[12,529]{0,1:T(8,128)S(1)} %bitcast.394, f32[4608]{0:T(1024)S(1)} %reshape.863, f32[4608]{0:T(1024)S(1)} %reshape.870, f32[768]{0:T(1024)S(1)} %copy-done.123), channel_id=1, replica_groups=mesh['page'=4,'blk'=8] {'page','blk'}, use_global_device_ids=true, to_apply=%region_47.48 | all-reduce | flops 16332 | bytes 130656 | tf_op jit(solution)/shard_map/psum | solution.py:495
  1585.3 1047.9 %all-reduce.23.cloned.1.call-done = (f32[1769472]{0:T(1024)}, f32[589824]{0:T(1024)}, f32[1769472]{0:T(1024)}, f32[589824]{0:T(1024)}, f32[589824]{0:T(1024)}, /...) async-done(((f32[1769472]{0:T(1024)}, f32[589824]{0:T(1024)}, ...) | async-done | bytes 75497488
  (785 shorter events, 564.5 us)
Async XLA Ops:
  7.2 60.7 %all-gather.27.cloned.1.call-start = ((), (), s32[]{:S(2)}) async-start(), calls=%async_computation.5 | async-start | bytes 1216512 | tf_op jit(solution)/shard_map/all_gather | solution.py:215
  7.9 119.2 %all-gather.29.cloned.1.call-start = ((), (), s32[]{:S(2)}) async-start(), calls=%async_computation.6 | async-start | bytes 2433024 | tf_op jit(solution)/shard_map/all_gather | solution.py:220
  8.7 180.5 %all-gather.25.cloned.1.call-start = ((), (), s32[]{:S(2)}) async-start(), calls=%async_computation.4 | async-start | bytes 3649536 | tf_op jit(solution)/shard_map/all_gather | solution.py:214
  9.4 275.2 %all-gather.23.cloned.1.call-start = ((), (), s32[]{:S(2)}) async-start(), calls=%async_computation.3 | async-start | bytes 1216512 | tf_op jit(solution)/shard_map/all_gather | solution.py:213
  10.0 290.9 %all-gather.33.cloned.1.call-start = ((), (), s32[]{:S(2)}) async-start(), calls=%async_computation.8 | async-start | bytes 1216512 | tf_op jit(solution)/shard_map/all_gather | solution.py:219
  10.6 346.1 %all-gather.35.cloned.1.call-start = ((), (), s32[]{:S(2)}) async-start(), calls=%async_computation.9 | async-start | bytes 1216512 | tf_op jit(solution)/shard_map/all_gather | solution.py:221
  11.2 404.7 %all-gather.41.cloned.1.call-start = ((), (), s32[]{:S(2)}) async-start(), calls=%async_computation.12 | async-start | bytes 2433024 | tf_op jit(solution)/shard_map/all_gather | solution.py:217
  11.9 465.9 %all-gather.21.cloned.1.call-start = ((), (), s32[]{:S(2)}) async-start(), calls=%async_computation.2 | async-start | bytes 3649536 | tf_op jit(solution)/shard_map/all_gather | solution.py:212
  12.7 530.6 %all-gather.37.cloned.1.call-start = ((), (), s32[]{:S(2)}) async-start(), calls=%async_computation.10 | async-start | bytes 4866048 | tf_op jit(solution)/shard_map/all_gather | solution.py:222
  13.4 595.2 %all-gather.39.cloned.1.call-start = ((), (), s32[]{:S(2)}) async-start(), calls=%async_computation.11 | async-start | bytes 4866048 | tf_op jit(solution)/shard_map/all_gather | solution.py:223
  14.0 656.6 %all-gather.31.cloned.1.call-start = ((), (), s32[]{:S(2)}) async-start(), calls=%async_computation.7 | async-start | bytes 3538944 | tf_op jit(solution)/shard_map/all_gather | solution.py:297
  66.3 417.9 %copy-start.101 = (f32[768]{0:T(1024)}, f32[768]{0:T(1024)S(1)}, u32[]{:S(2)}) copy-start(f32[768]{0:T(1024)S(1)} %get-tuple-element.351) | copy-start | bytes 9220
  228.9 497.3 %all-gather.45.cloned.1.call-start = ((), (), s32[]{:S(2)}) async-start(), calls=%async_computation.14 | async-start | bytes 1216512 | tf_op jit(solution)/shard_map/all_gather | solution.py:216
  229.5 552.8 %all-gather.47.cloned.1.call-start = ((), (), s32[]{:S(2)}) async-start(), calls=%async_computation.15 | async-start | bytes 1216512 | tf_op jit(solution)/shard_map/all_gather | solution.py:218
  230.2 617.4 %all-gather.49.cloned.1.call-start = ((), (), s32[]{:S(2)}) async-start(), calls=%async_computation.16 | async-start | bytes 4866048 | tf_op jit(solution)/shard_map/all_gather | solution.py:224
  230.8 682.1 %all-gather.51.cloned.1.call-start = ((), (), s32[]{:S(2)}) async-start(), calls=%async_computation.17 | async-start | bytes 4866048 | tf_op jit(solution)/shard_map/all_gather | solution.py:225
  231.4 747.5 %all-gather.43.cloned.1.call-start = ((), (), s32[]{:S(2)}) async-start(), calls=%async_computation.13 | async-start | bytes 3981312 | tf_op jit(solution)/shard_map/all_gather | solution.py:307
  501.4 597.8 %reduce-scatter.3.cloned.1.call-start = ((), (), s32[]{:S(2)}) async-start(), calls=%async_computation.21 | async-start | bytes 7077888 | tf_op jit(solution)/shard_map/reduce_scatter | solution.py:387
  713.4 431.8 %all-gather.55.cloned.1.call-start = ((), (), s32[]{:S(2)}) async-start(), calls=%async_computation.19 | async-start | bytes 1769472 | tf_op jit(solution)/shard_map/all_gather | solution.py:296
  786.6 519.1 %all-gather.57.cloned.1.call-start = ((), (), s32[]{:S(2)}) async-start(), calls=%async_computation.20 | async-start | bytes 1769472 | tf_op jit(solution)/shard_map/all_gather | solution.py:355
  1023.0 298.4 %reduce-scatter.5.cloned.1.call-start = ((), (), s32[]{:S(2)}) async-start(), calls=%async_computation.22 | async-start | bytes 7077888 | tf_op jit(solution)/shard_map/reduce_scatter | solution.py:417
  1117.2 416.4 %all-gather.53.cloned.1.call-start = ((), (), s32[]{:S(2)}) async-start(), calls=%async_computation.18 | async-start | bytes 1769472 | tf_op jit(solution)/shard_map/all_gather | solution.py:332
  1209.9 375.4 %all-gather.59.cloned.1.call-start = ((), (), s32[]{:S(2)}) async-start(), calls=%async_computation.23 | async-start | bytes 3538944 | tf_op jit(solution)/shard_map/all_gather | solution.py:496
  1330.6 1302.6 %all-reduce.23.cloned.1.call-start = ((), (), s32[]{:S(2)}) async-start(), calls=%async_computation.24 | async-start | bytes 150994944
  (200 other events, 2953.5 us)
Sparse Core Ops, SparseCore 0:
  10.9 56.8 all-gather.26
  70.8 56.3 all-gather.28
  130.1 59.0 all-gather.24
  192.0 52.8 all-gather.22
  247.6 53.1 all-gather.32
  303.6 53.0 all-gather.34
  359.6 56.1 all-gather.40
  418.8 59.0 all-gather.20
  480.8 62.4 all-gather.36
  546.1 62.4 all-gather.38
  611.3 59.2 all-gather.30
  673.4 52.7 all-gather.44
  729.1 53.1 all-gather.46
  785.0 62.5 all-gather.48
  850.3 62.4 all-gather.50
  914.9 63.9 all-gather.42
  982.4 116.8 reduce-scatter.2
  1101.9 43.3 all-gather.54
  1147.4 42.9 all-gather.56
  1193.9 117.3 reduce-scatter.4
  1314.1 44.1 all-gather.52
  1360.5 59.2 all-gather.58
  1426.2 1206.9 all-reduce.22
where the time goes:
time: 2680 us; the launch traced here: 2670 us
  waiting for transfers between devices  1800 us (67%)
  local copies, waits for them, and re-layouts  345 us (13%)
  matrix products  202 us (8%)
  blocking collectives  152 us (6%)
  other arithmetic  146 us (5%)
    unnamed x24, waiting for transfers between devices  1060 us
    scatter-add x1, other arithmetic, body(): jax.ops.segment_sum(table_local.T, rel_index.reshape(-1), num_segments=RELS)  112 us
    reshape x14, local copies, waits for them, and re-layouts, body(): piece.reshape(shape)  77.5 us
    unnamed x398, local copies, waits for them, and re-layouts  68.3 us
    all_gather x1, waiting for transfers between devices, body(): lax.all_gather(question_up, ('page', 'blk'), axis=0, tiled=True)  60.9 us
    all_gather x1, waiting for transfers between devices, body(): lax.all_gather(causal_project, ('page', 'blk'), axis=0, tiled=True)  57.4 us
    all_gather x1, waiting for transfers between devices, body(): lax.all_gather(question_down, ('page', 'blk'), axis=0, tiled=True)  57.1 us
    all_gather x1, waiting for transfers between devices, body(): lax.all_gather(visual_down, ('page', 'blk'), axis=0, tiled=True)  57.1 us
  transfers between devices with their start and end apart: 23, of which 18 were waited for; matrix products, arithmetic and copies ran while one was open for 24% of the time, Pallas kernels for 0%

commit v1 on v0

v1 whole, which is shorter than its diff:
```python
import functools

import jax
import jax.numpy as jnp
from jax import lax
from jax.experimental import pallas as pl
from jax.experimental.pallas import tpu as pltpu
from jax.sharding import PartitionSpec as P

D = 768
HEADS = 12
HEAD_DIM = 64
FF = 3072
Q_LEN = 1024
WIN = 144
RELS = 529
LONGEST = Q_LEN // 2
LANES = 128
PAIRS = D // LANES
RELS_PAD = 640

EPS = 1e-05
NEG = -1000000000.0
SCALE = HEAD_DIM ** (-0.5)
MIB = 1 << 20


def product(left, right):
    return jnp.dot(left, right, preferred_element_type=jnp.float32)


def times_transposed(left, right):
    return lax.dot_general(
        left, right, (((1,), (1,)), ((), ())), preferred_element_type=jnp.float32
    )


def transposed_times(left, right):
    return lax.dot_general(
        left, right, (((0,), (0,)), ((), ())), preferred_element_type=jnp.float32
    )


def low(values):
    return values.astype(jnp.bfloat16)


def normalize(rows, gain, shift):
    mean = jnp.mean(rows, axis=-1, keepdims=True)
    centred = rows - mean
    spread = jnp.mean(centred * centred, axis=-1, keepdims=True)
    return centred * lax.rsqrt(spread + EPS) * gain + shift


def smooth(values):
    return jax.nn.gelu(values, approximate=False)


def ring_order(blocks):
    return tuple(range(0, blocks, 2)) + tuple(range(blocks - 1, 0, -2))


def ring_seat(blk, blocks):
    return jnp.where(blk % 2 == 0, blk // 2, blocks - 1 - blk // 2)


def ring_place(seat, blocks):
    seat = lax.rem(seat + 2 * blocks, blocks)
    return jnp.where(seat < blocks // 2, 2 * seat, 2 * (blocks - 1 - seat) + 1)


def forward_hop(blocks):
    order = ring_order(blocks)
    return [(order[i], order[(i + 1) % blocks]) for i in range(blocks)]


def backward_hop(blocks):
    return [(there, here) for here, there in forward_hop(blocks)]


def swap_far(values):
    return lax.ppermute(values, "page", [(i, i ^ 2) for i in range(4)])


def swap_core(values):
    return lax.ppermute(values, "page", [(i, i ^ 1) for i in range(4)])


OFFSETS = (0, -1, 1, -2, 2, -3, 3, 4)


def ring_pieces(own, blocks):
    ahead, behind = forward_hop(blocks), backward_hop(blocks)
    half = own.shape[0] // 2
    pieces = {0: own}
    one, two = own, own
    for step in (1, 2, 3):
        one = lax.ppermute(one, "blk", ahead)
        two = lax.ppermute(two, "blk", behind)
        pieces[-step], pieces[step] = one, two
    pieces["first"] = lax.ppermute(one[:half], "blk", ahead)
    pieces["second"] = lax.ppermute(two[half:], "blk", behind)
    return pieces


def ring_reduce(chunk, blocks):
    ahead, behind = forward_hop(blocks), backward_hop(blocks)
    most = chunk(4)
    half = most.shape[0] // 2
    one = lax.ppermute(low(most[:half]), "blk", ahead).astype(jnp.float32)
    two = lax.ppermute(low(most[half:]), "blk", behind).astype(jnp.float32)
    blank = jnp.zeros(one.shape, jnp.float32)
    one, two = jnp.concatenate([one, blank]), jnp.concatenate([blank, two])
    for step in (3, 2, 1):
        one = lax.ppermute(low(chunk(step) + one), "blk", ahead).astype(jnp.float32)
        two = lax.ppermute(low(chunk(-step) + two), "blk", behind).astype(jnp.float32)
    return chunk(0) + one + two


def whole_block(array):
    blank = (0,) * len(array.shape)
    return pl.BlockSpec(array.shape, lambda i, where: blank)


def assemble_kernel(plan, count, where_ref, *refs):
    pieces, outs = refs[:count], refs[count:]
    for piece, (index, first, core) in zip(pieces, plan):
        start = 0
        for out in outs:
            width = out.shape[-1]
            for number in range(piece.shape[0]):
                target = (first + number, where_ref[core], where_ref[index])
                out[target] = piece[number, :, start : start + width]
            start += width


def assemble(own, other, splits, core, seat, blocks):
    rows = own[0].shape[1]
    places = [ring_place(seat + k, blocks) for k in OFFSETS]
    where = jnp.stack([core, 1 - core] + places).astype(jnp.int32)
    pieces, plan = [], []
    for side, group in ((0, own), (1, other)):
        for number, offset in enumerate(OFFSETS):
            if offset == 4:
                pieces += [group["first"], group["second"]]
                plan += [(2 + number, 0, side), (2 + number, 1, side)]
            else:
                pieces.append(group[offset])
                plan.append((2 + number, 0, side))
    outs = [jax.ShapeDtypeStruct((2, 2, blocks, rows, width), jnp.bfloat16) for width in splits]
    found = pl.pallas_call(
        functools.partial(assemble_kernel, plan, len(pieces)),
        out_shape=outs,
        grid_spec=pltpu.PrefetchScalarGridSpec(
            num_scalar_prefetch=1,
            grid=(1,),
            in_specs=[whole_block(item) for item in pieces],
            out_specs=[whole_block(item) for item in outs],
        ),
        compiler_params=pltpu.CompilerParams(vmem_limit_bytes=32 * MIB),
        cost_estimate=pl.CostEstimate(
            flops=0, bytes_accessed=16 * blocks * rows * sum(splits), transcendentals=0
        ),
    )(where, *pieces)
    return [item.reshape(4 * blocks * rows, -1) for item in found]


def place_kernel(plan, where_ref, *refs):
    pieces, out = refs[:-1], refs[-1]
    for piece, (index, first, last) in zip(pieces, plan):
        out[where_ref[index], first:last] = piece[...].astype(out.dtype)


def gather_seats(own, seat, blocks, dtype):
    rows = own.shape[0]
    if blocks != 8:
        stacked = lax.all_gather(own, "blk", axis=0)
        ordered = jnp.stack([stacked[i] for i in ring_order(blocks)])
        return ordered.reshape(blocks * rows, -1).astype(dtype)
    found = ring_pieces(own, blocks)
    where = jnp.stack([lax.rem(seat + k + blocks, blocks) for k in OFFSETS]).astype(jnp.int32)
    pieces, plan = [], []
    for number, offset in enumerate(OFFSETS):
        if offset == 4:
            pieces += [found["first"], found["second"]]
            plan += [(number, 0, rows // 2), (number, rows // 2, rows)]
        else:
            pieces.append(found[offset])
            plan.append((number, 0, rows))
    out = jax.ShapeDtypeStruct((blocks,) + own.shape, dtype)
    placed = pl.pallas_call(
        functools.partial(place_kernel, plan),
        out_shape=out,
        grid_spec=pltpu.PrefetchScalarGridSpec(
            num_scalar_prefetch=1,
            grid=(1,),
            in_specs=[whole_block(item) for item in pieces],
            out_specs=whole_block(out),
        ),
        compiler_params=pltpu.CompilerParams(vmem_limit_bytes=24 * MIB),
        cost_estimate=pl.CostEstimate(
            flops=0, bytes_accessed=4 * blocks * own.size, transcendentals=0
        ),
    )(where, *pieces)
    return placed.reshape(blocks * rows, -1)


def bias_kernel(table_ref, index_ref, out_ref):
    def one(i, carry):
        row = index_ref[pl.ds(i, 1), :]
        marks = lax.broadcasted_iota(jnp.int32, (RELS_PAD, WIN), 0) == row
        hot = low(jnp.where(marks, 1.0, 0.0))
        both = jnp.dot(table_ref[...], hot, preferred_element_type=jnp.float32)
        out_ref[i] = both[:16] + both[16:]
        return carry

    lax.fori_loop(0, WIN, one, 0, unroll=4)


def window_bias(rel_table, rel_index):
    table = jnp.pad(rel_table, ((0, 16 - HEADS), (0, RELS_PAD - RELS)))
    coarse = lax.reduce_precision(table, 8, 7)
    both = low(jnp.concatenate([coarse, table - coarse]))
    found = pl.pallas_call(
        bias_kernel,
        out_shape=jax.ShapeDtypeStruct((WIN, 16, WIN), jnp.float32),
        cost_estimate=pl.CostEstimate(
            flops=64 * RELS_PAD * WIN * WIN, bytes_accessed=4 * 17 * WIN * WIN, transcendentals=0
        ),
    )(both, rel_index)
    return found[:, :HEADS].transpose(1, 0, 2)


def table_kernel(scores_ref, index_ref, out_ref):
    def one(i, total):
        row = index_ref[pl.ds(i, 1), :]
        marks = lax.broadcasted_iota(jnp.int32, (RELS_PAD, WIN), 0) == row
        hot = low(jnp.where(marks, 1.0, 0.0))
        return total + times_transposed(scores_ref[i], hot)

    out_ref[...] = lax.fori_loop(
        0, WIN, one, jnp.zeros((2 * HEADS, RELS_PAD), jnp.float32), unroll=4
    )


def table_sums(back_scores, rel_index):
    rows = back_scores.reshape(2 * HEADS, WIN, WIN).transpose(1, 0, 2)
    found = pl.pallas_call(
        table_kernel,
        out_shape=jax.ShapeDtypeStruct((2 * HEADS, RELS_PAD), jnp.float32),
        cost_estimate=pl.CostEstimate(
            flops=48 * RELS_PAD * WIN * WIN, bytes_accessed=52 * WIN * WIN, transcendentals=0
        ),
    )(rows, rel_index)
    return jnp.sum(found.reshape(HEADS, 2, RELS_PAD), axis=1)[:, :RELS]


def head_lanes(side):
    lane = lax.broadcasted_iota(jnp.int32, (1, LANES), 1)
    return (lane < HEAD_DIM) if side == 0 else (lane >= HEAD_DIM)


def attend_pair(query, keys, values, extras):
    result, logs = None, None
    for side in (0, 1):
        mine = head_lanes(side)
        one = jnp.where(mine, query * SCALE, 0).astype(jnp.bfloat16)
        scores = times_transposed(one, keys) + extras[side]
        top = jnp.max(scores, axis=-1, keepdims=True)
        expo = jnp.exp(scores - top)
        total = jnp.sum(expo, axis=-1, keepdims=True)
        found = product(low(expo), values) / total
        log_total = jnp.broadcast_to(top + jnp.log(total), found.shape)
        result = found if side == 0 else jnp.where(mine, found, result)
        logs = log_total if side == 0 else jnp.where(mine, log_total, logs)
    return low(result), logs


def pair_backward(query, keys, values, extras, logs, back_out):
    back_query, back_keys, back_values, kept = None, None, None, []
    for side in (0, 1):
        mine = head_lanes(side)
        one = jnp.where(mine, query * SCALE, 0).astype(jnp.bfloat16)
        back_one = jnp.where(mine, back_out, 0).astype(jnp.bfloat16)
        scores = times_transposed(one, keys) + extras[side]
        first = side * HEAD_DIM
        shares = jnp.exp(scores - logs[:, first : first + 1])
        back_shares = times_transposed(back_one, values)
        inner = jnp.sum(shares * back_shares, axis=-1, keepdims=True)
        back_scores = low(shares * (back_shares - inner))
        found = product(back_scores, keys) * SCALE
        found_keys = transposed_times(back_scores, one)
        found_values = transposed_times(low(shares), back_one)
        kept.append(back_scores)
        if side == 0:
            back_query, back_keys, back_values = found, found_keys, found_values
        else:
            back_query = jnp.where(mine, found, back_query)
            back_keys, back_values = back_keys + found_keys, back_values + found_values
    return low(back_query), low(back_keys), low(back_values), kept


def question_extra(role_ref, qid, kid):
    shape = (qid.shape[0], kid.shape[1])
    row = lax.broadcasted_iota(jnp.int32, shape, 0) + role_ref[1]
    column = lax.broadcasted_iota(jnp.int32, shape, 1)
    return jnp.where((qid == kid) & (column <= row), 0.0, NEG)


def window_extras(bias_ref, qid, kid):
    same = jnp.where(qid == kid, 0.0, NEG)
    return [bias_ref[0] + same, bias_ref[1] + same]


def self_forward_kernel(
    role_ref, q_ref, k_ref, v_ref, bias_ref, qid_ref, kid_ref, o_ref, log_ref
):
    rows = q_ref.shape[1]

    @pl.when(role_ref[0] == 0)
    def question():
        for s in (0, 1):
            extra = question_extra(role_ref, qid_ref[s], kid_ref[s])
            o_ref[s], log_ref[s] = attend_pair(q_ref[s], k_ref[s], v_ref[s], [extra, extra])

    @pl.when(role_ref[0] != 0)
    def visual():
        for s in (0, 1):
            extras = window_extras(bias_ref, qid_ref[s], kid_ref[s, :, :rows])
            o_ref[s], log_ref[s] = attend_pair(
                q_ref[s], k_ref[s, :rows], v_ref[s, :rows], extras
            )


def self_backward_kernel(
    role_ref,
    q_ref,
    k_ref,
    v_ref,
    bias_ref,
    qid_ref,
    kid_ref,
    log_ref,
    back_ref,
    dq_ref,
    dk_ref,
    dv_ref,
    ds_ref,
):
    rows = q_ref.shape[1]

    @pl.when(role_ref[0] == 0)
    def question():
        ds_ref[...] = jnp.zeros_like(ds_ref)
        for s in (0, 1):
            extra = question_extra(role_ref, qid_ref[s], kid_ref[s])
            dq_ref[s], dk_ref[s], dv_ref[s], unused = pair_backward(
                q_ref[s], k_ref[s], v_ref[s], [extra, extra], log_ref[s], back_ref[s]
            )

    @pl.when(role_ref[0] != 0)
    def visual():
        dk_ref[...] = jnp.zeros_like(dk_ref)
        dv_ref[...] = jnp.zeros_like(dv_ref)
        for s in (0, 1):
            extras = window_extras(bias_ref, qid_ref[s], kid_ref[s, :, :rows])
            dq_ref[s], found_keys, found_values, kept = pair_backward(
                q_ref[s], k_ref[s, :rows], v_ref[s, :rows], extras, log_ref[s], back_ref[s]
            )
            dk_ref[s, :rows] = found_keys
            dv_ref[s, :rows] = found_values
            ds_ref[0, s] = kept[0]
            ds_ref[1, s] = kept[1]


def self_specs(rows, span):
    query = pl.BlockSpec((2, rows, LANES), lambda h, role: (0, 0, h))
    keys = pl.BlockSpec((2, span, LANES), lambda h, role: (0, 0, h))
    values = pl.BlockSpec((2, span, LANES), lambda h, role: (0, 0, h + PAIRS))
    bias = pl.BlockSpec((2, rows, rows), lambda h, role: (h, 0, 0))
    qid = pl.BlockSpec((2, rows, 1), lambda h, role: (0, 0, 0))
    kid = pl.BlockSpec((2, 1, span), lambda h, role: (0, 0, 0))
    return query, keys, values, bias, qid, kid


def self_forward(role, query, pair, bias, qid, kid):
    rows, span = query.shape[1], pair.shape[1]
    specs = self_specs(rows, span)
    return pl.pallas_call(
        self_forward_kernel,
        out_shape=[
            jax.ShapeDtypeStruct((2, rows, D), jnp.bfloat16),
            jax.ShapeDtypeStruct((2, rows, D), jnp.float32),
        ],
        grid_spec=pltpu.PrefetchScalarGridSpec(
            num_scalar_prefetch=1, grid=(PAIRS,), in_specs=list(specs), out_specs=[specs[0]] * 2
        ),
        compiler_params=pltpu.CompilerParams(vmem_limit_bytes=24 * MIB),
        cost_estimate=pl.CostEstimate(
            flops=16 * rows * span * D, bytes_accessed=12 * span * D, transcendentals=0
        ),
    )(role, query, pair, pair, bias, qid, kid)


def self_backward(role, query, pair, bias, qid, kid, logs, back_out):
    rows, span = query.shape[1], pair.shape[1]
    specs = self_specs(rows, span)
    return pl.pallas_call(
        self_backward_kernel,
        out_shape=[
            jax.ShapeDtypeStruct((2, rows, D), jnp.bfloat16),
            jax.ShapeDtypeStruct((2, span, D), jnp.bfloat16),
            jax.ShapeDtypeStruct((2, span, D), jnp.bfloat16),
            jax.ShapeDtypeStruct((HEADS, 2, rows, rows), jnp.bfloat16),
        ],
        grid_spec=pltpu.PrefetchScalarGridSpec(
            num_scalar_prefetch=1,
            grid=(PAIRS,),
            in_specs=list(specs) + [specs[0]] * 2,
            out_specs=[
                specs[0],
                specs[1],
                specs[1],
                pl.BlockSpec((2, 2, rows, rows), lambda h, role: (h, 0, 0, 0)),
            ],
        ),
        compiler_params=pltpu.CompilerParams(vmem_limit_bytes=24 * MIB),
        cost_estimate=pl.CostEstimate(
            flops=40 * rows * span * D, bytes_accessed=16 * span * D, transcendentals=0
        ),
    )(role, query, pair, pair, bias, qid, kid, logs, back_out)


def cross_forward_kernel(q_ref, k_ref, v_ref, extra_ref, o_ref, log_ref):
    extra = extra_ref[...]
    o_ref[...], log_ref[...] = attend_pair(
        q_ref[...], k_ref[...], v_ref[...], [extra, extra]
    )


def cross_backward_kernel(
    q_ref, k_ref, v_ref, extra_ref, log_ref, back_ref, dq_ref, dk_ref, dv_ref
):
    extra = extra_ref[...]
    dq_ref[...], dk_ref[...], dv_ref[...], unused = pair_backward(
        q_ref[...], k_ref[...], v_ref[...], [extra, extra], log_ref[...], back_ref[...]
    )


def cross_specs(rows, span):
    query = pl.BlockSpec((rows, LANES), lambda h: (0, h))
    keys = pl.BlockSpec((span, LANES), lambda h: (0, h))
    values = pl.BlockSpec((span, LANES), lambda h: (0, h + PAIRS))
    extra = pl.BlockSpec((1, span), lambda h: (0, 0))
    return query, keys, values, extra


def cross_limit(span):
    return (24 if span <= 2048 else 60) * MIB


def cross_forward(query, pair, extra):
    rows, span = query.shape[0], pair.shape[0]
    specs = cross_specs(rows, span)
    return pl.pallas_call(
        cross_forward_kernel,
        out_shape=[
            jax.ShapeDtypeStruct((rows, D), jnp.bfloat16),
            jax.ShapeDtypeStruct((rows, D), jnp.float32),
        ],
        grid=(PAIRS,),
        in_specs=list(specs),
        out_specs=[specs[0]] * 2,
        compiler_params=pltpu.CompilerParams(vmem_limit_bytes=cross_limit(span)),
        cost_estimate=pl.CostEstimate(
            flops=16 * rows * span * D, bytes_accessed=4 * span * D, transcendentals=0
        ),
    )(query, pair, pair, extra)


def cross_backward(query, pair, extra, logs, back_out):
    rows, span = query.shape[0], pair.shape[0]
    specs = cross_specs(rows, span)
    return pl.pallas_call(
        cross_backward_kernel,
        out_shape=[
            jax.ShapeDtypeStruct((rows, D), jnp.bfloat16),
            jax.ShapeDtypeStruct((span, D), jnp.bfloat16),
            jax.ShapeDtypeStruct((span, D), jnp.bfloat16),
        ],
        grid=(PAIRS,),
        in_specs=list(specs) + [specs[0]] * 2,
        out_specs=[specs[0], specs[1], specs[1]],
        compiler_params=pltpu.CompilerParams(vmem_limit_bytes=cross_limit(span)),
        cost_estimate=pl.CostEstimate(
            flops=40 * rows * span * D, bytes_accessed=8 * span * D, transcendentals=0
        ),
    )(query, pair, pair, extra, logs, back_out)


def body(
    visual_in,
    question_in,
    segment_ids,
    regions,
    rel_index,
    rel_table,
    window_project,
    window_output,
    causal_project,
    causal_output,
    reader_query,
    reader_pair,
    reader_output,
    viewer_query,
    viewer_pair,
    viewer_output,
    visual_up,
    visual_down,
    question_up,
    question_down,
    norm_gains,
    norm_shifts,
    visual_cot,
    question_cot,
):
    blocks = lax.axis_size("blk")
    share = Q_LEN // blocks
    rows = visual_in.shape[0]
    page, blk = lax.axis_index("page"), lax.axis_index("blk")
    asks, core = page < 2, page % 2
    seat = ring_seat(blk, blocks)
    early = -(-(LONGEST - 1) // share)
    reach = min(Q_LEN, share * (early + 1))
    span = reach + rows - share
    first = jnp.clip((seat - early) * share, 0, Q_LEN - reach)
    inset = jnp.where(asks, seat * share - first, 0)
    cut = D // (4 * blocks)

    def own_of(question_side, visual_side):
        return jnp.where(asks, question_side, visual_side)

    def trade(question_side, visual_side):
        got = swap_far(own_of(visual_side, question_side))
        kept = own_of(question_side, visual_side)
        return jnp.stack([own_of(kept, got), own_of(got, kept)])

    def gather_weight(question_side, visual_side, splits):
        both = trade(question_side, visual_side)
        if blocks == 8:
            pieces = ring_pieces(both, blocks)
            other = {key: swap_core(item) for key, item in pieces.items()}
            return assemble(pieces, other, splits, core, seat, blocks)
        here = lax.all_gather(both, "blk", axis=0)
        there = swap_core(here)
        pair = jnp.where(core == 0, jnp.stack([here, there]), jnp.stack([there, here]))
        whole = pair.transpose(2, 0, 1, 3, 4).reshape(4 * blocks * both.shape[1], -1)
        places = [sum(splits[:i]) for i in range(len(splits))]
        return [whole[:, at : at + width] for at, width in zip(places, splits)]

    def pad_rows(values, total):
        return jnp.pad(values, ((0, total - values.shape[0]),) + ((0, 0),) * (values.ndim - 1))

    def block_of(flat, columns):
        return flat.reshape(-1, columns)

    norms = jnp.pad(jnp.concatenate([norm_gains, norm_shifts]), (0, cut * LANES - 2 * norm_gains.size))
    norms = norms.reshape(cut, LANES)
    self_query_weight, self_pair_weight, self_exit, norm_rows = gather_weight(
        jnp.concatenate([block_of(causal_project, 3 * D), block_of(causal_output, D), norms], 1),
        jnp.concatenate([block_of(window_project, 3 * D), block_of(window_output, D), norms], 1),
        (D, 2 * D, D, LANES),
    )
    slots = trade(
        pad_rows(lax.dynamic_slice_in_dim(question_in, first, reach, 0), span),
        pad_rows(visual_in, span),
    )
    marks = trade(segment_ids[0], jnp.pad(regions, (0, Q_LEN - rows)))
    cross_query_weight, cross_pair_weight, cross_exit = gather_weight(
        jnp.concatenate(
            [block_of(reader_query, D), block_of(reader_pair, 2 * D), block_of(reader_output, D)], 1
        ),
        jnp.concatenate(
            [block_of(viewer_query, D), block_of(viewer_pair, 2 * D), block_of(viewer_output, D)], 1
        ),
        (D, 2 * D, D),
    )
    (raise_weight,) = gather_weight(block_of(question_up, FF), block_of(visual_up, FF), (FF,))
    (lower_weight,) = gather_weight(block_of(question_down, D), block_of(visual_down, D), (D,))
    cot = trade(
        pad_rows(lax.dynamic_slice_in_dim(question_cot, seat * share, share, 0), rows), visual_cot
    ).astype(jnp.float32)
    norm_flat = norm_rows.reshape(4 * blocks, -1)[:, : 2 * norm_gains.size].astype(jnp.float32)
    gains = norm_flat[:, : norm_gains.size].reshape(6, D)
    shifts = norm_flat[:, norm_gains.size :].reshape(6, D)
    bias = window_bias(rel_table, rel_index)

    role = jnp.stack([jnp.where(asks, 0, 1), inset]).astype(jnp.int32)
    key_marks = own_of(
        jnp.pad(
            lax.dynamic_slice_in_dim(marks, first, reach, 1),
            ((0, 0), (0, span - reach)),
            constant_values=-2,
        ),
        marks[:, :span],
    )[:, None, :]
    row_marks = own_of(
        jnp.pad(
            lax.dynamic_slice_in_dim(marks, seat * share, share, 1),
            ((0, 0), (0, rows - share)),
            constant_values=-1,
        ),
        marks[:, :rows],
    )[:, :, None]
    own = lax.dynamic_slice_in_dim(slots, inset, rows, 1).astype(jnp.float32)
    self_gain, self_shift = own_of(gains[1], gains[0]), own_of(shifts[1], shifts[0])
    self_norm, self_pull = jax.vjp(normalize, own, self_gain, self_shift)
    self_low = low(self_norm).reshape(2 * rows, D)
    every_low = low(normalize(slots.astype(jnp.float32), self_gain, self_shift))
    every_low = every_low.reshape(2 * span, D)
    self_query = low(product(self_low, self_query_weight)).reshape(2, rows, D)
    self_pair = low(product(every_low, self_pair_weight)).reshape(2, span, 2 * D)
    self_attn, self_logs = self_forward(role, self_query, self_pair, bias, row_marks, key_marks)
    self_attn = self_attn.reshape(2 * rows, D)
    rows_one = own + product(self_attn, self_exit).reshape(2, rows, D)

    cross_gain, cross_shift = own_of(gains[2], gains[3]), own_of(shifts[2], shifts[3])
    cross_norm, cross_pull = jax.vjp(normalize, rows_one, cross_gain, cross_shift)
    cross_low = low(cross_norm)
    sent = swap_far(cross_low)

    def all_blocks(piece):
        if blocks != 8:
            return lax.all_gather(piece, "blk", axis=0, tiled=True)
        found = ring_pieces(piece, blocks)
        ordered = [found[k] for k in OFFSETS[:-1]] + [found["first"], found["second"]]
        return jnp.concatenate(ordered)

    def sum_blocks(partial):
        if blocks != 8:
            return lax.psum_scatter(partial, "blk", scatter_dimension=0, tiled=True)

        def chunk(k):
            at = OFFSETS.index(k) * rows
            return partial[at : at + rows]

        return ring_reduce(chunk, blocks)

    sources = [all_blocks(sent[s]) for s in (0, 1)]
    cross_query = low(product(cross_low.reshape(2 * rows, D), cross_query_weight))
    cross_query = cross_query.reshape(2, rows, D)
    column = jnp.arange(blocks * rows) % rows
    cross_extra = own_of(0.0, jnp.where(column < share, 0.0, NEG))[None]
    cross_pairs = [low(product(source, cross_pair_weight)) for source in sources]
    cross_found = [cross_forward(cross_query[s], cross_pairs[s], cross_extra) for s in (0, 1)]
    cross_attn = jnp.concatenate([found[0] for found in cross_found])
    rows_two = rows_one + product(cross_attn, cross_exit).reshape(2, rows, D)

    mlp_gain, mlp_shift = own_of(gains[5], gains[4]), own_of(shifts[5], shifts[4])
    mlp_norm, mlp_pull = jax.vjp(normalize, rows_two, mlp_gain, mlp_shift)
    mlp_low = low(mlp_norm).reshape(2 * rows, D)
    active, smooth_pull = jax.vjp(smooth, product(mlp_low, raise_weight))
    active_low = low(active)
    rows_three = rows_two + product(active_low, lower_weight).reshape(2, rows, D)
    mlp_branch = low(cot).reshape(2 * rows, D)
    (back_raise,) = smooth_pull(times_transposed(mlp_branch, lower_weight))
    back_raise = low(back_raise)
    delta_lower = low(transposed_times(active_low, mlp_branch))
    delta_raise = low(transposed_times(mlp_low, back_raise))
    back_mlp = times_transposed(back_raise, raise_weight).reshape(2, rows, D)
    back_mlp_in, gain_mlp, shift_mlp = mlp_pull(back_mlp)
    back_two = cot + back_mlp_in

    def sum_weight(parts):
        height = parts[0].shape[0] // (4 * blocks)
        views = [part.reshape(2, 2, blocks, height, -1) for part in parts]

        def pick(side):
            return [
                lax.dynamic_index_in_dim(view, side, 1, keepdims=False) for view in views
            ]

        got = [swap_core(item) for item in pick(1 - core)]

        if blocks == 8:

            def chunk(k):
                place = ring_place(seat + k, blocks)
                both = []
                for view, item in zip(views, got):
                    mine = lax.dynamic_slice(
                        view, (0, core, place, 0, 0), (2, 1, 1) + view.shape[3:]
                    ).reshape(2, height, -1)
                    theirs = lax.dynamic_index_in_dim(item, place, 1, keepdims=False)
                    both.append(mine.astype(jnp.float32) + theirs.astype(jnp.float32))
                return jnp.concatenate(both, -1)

            total = ring_reduce(chunk, blocks)
        else:
            kept = jnp.concatenate(
                [a.astype(jnp.float32) + b.astype(jnp.float32) for a, b in zip(pick(core), got)], -1
            )
            total = lax.psum_scatter(kept, "blk", scatter_dimension=1, tiled=True)
            total = total.reshape(2, height, -1)
        mine, away = own_of(total[0], total[1]), own_of(total[1], total[0])
        came = swap_far(low(away)).astype(jnp.float32)
        return own_of(mine, came), own_of(came, mine)

    lower_sums = sum_weight([delta_lower])
    raise_sums = sum_weight([delta_raise])

    cross_branch = low(back_two).reshape(2 * rows, D)
    delta_cross_exit = low(transposed_times(cross_attn, cross_branch))
    back_attn = low(times_transposed(cross_branch, cross_exit)).reshape(2, rows, D)
    cross_back = [
        cross_backward(
            cross_query[s], cross_pairs[s], cross_extra, cross_found[s][1], back_attn[s]
        )
        for s in (0, 1)
    ]
    key_half, value_half = cross_pair_weight[:, :D], cross_pair_weight[:, D:]
    back_sent = []
    for unused, found_keys, found_values in cross_back:
        partial = times_transposed(found_keys, key_half) + times_transposed(found_values, value_half)
        back_sent.append(sum_blocks(partial))
    back_query = jnp.concatenate([found[0] for found in cross_back])
    back_cross = times_transposed(back_query, cross_query_weight).reshape(2, rows, D)
    back_cross = back_cross + swap_far(low(jnp.stack(back_sent))).astype(jnp.float32)
    back_cross_in, gain_cross, shift_cross = cross_pull(back_cross)
    back_one = back_two + back_cross_in
    all_sources = jnp.concatenate(sources)
    delta_cross_keys = low(
        transposed_times(all_sources, jnp.concatenate([found[1] for found in cross_back]))
    )
    delta_cross_values = low(
        transposed_times(all_sources, jnp.concatenate([found[2] for found in cross_back]))
    )
    delta_cross_query = low(transposed_times(cross_low.reshape(2 * rows, D), back_query))
    cross_sums = sum_weight(
        [delta_cross_query, delta_cross_keys, delta_cross_values, delta_cross_exit]
    )

    self_branch = low(back_one).reshape(2 * rows, D)
    delta_self_exit = low(transposed_times(self_attn, self_branch))
    back_attn = low(times_transposed(self_branch, self_exit)).reshape(2, rows, D)
    back_query, back_keys, back_values, back_scores = self_backward(
        role, self_query, self_pair, bias, row_marks, key_marks, self_logs, back_attn
    )
    back_query = back_query.reshape(2 * rows, D)
    back_keys, back_values = back_keys.reshape(2 * span, D), back_values.reshape(2 * span, D)
    delta_self_query = low(transposed_times(self_low, back_query))
    delta_self_keys = low(transposed_times(every_low, back_keys))
    delta_self_values = low(transposed_times(every_low, back_values))
    self_sums = sum_weight(
        [delta_self_query, delta_self_keys, delta_self_values, delta_self_exit]
    )
    back_every = times_transposed(back_keys, self_pair_weight[:, :D])
    back_every = back_every + times_transposed(back_values, self_pair_weight[:, D:])
    back_every = back_every.reshape(2, span, D)

    def for_earlier(j):
        at = jnp.maximum(inset - j * share, 0)
        found = lax.dynamic_slice_in_dim(back_every, at, share, 1)
        return jnp.where(asks & (seat >= j), found, 0.0)

    order = ring_order(blocks)
    earlier_hop = [(order[i], order[i - 1]) for i in range(1, blocks)]
    running = for_earlier(early)
    for j in range(early - 1, -1, -1):
        running = lax.ppermute(low(running), "blk", earlier_hop).astype(jnp.float32) + for_earlier(j)
    back_self = times_transposed(back_query, self_query_weight).reshape(2, rows, D) + own_of(
        jnp.pad(running, ((0, 0), (0, rows - share), (0, 0))), back_every[:, :rows]
    )
    back_self_in, gain_self, shift_self = self_pull(back_self)
    back_in = back_one + back_self_in

    blank = jnp.zeros((D,), jnp.float32)
    gain_delta = [
        own_of(blank, gain_self),
        own_of(gain_self, blank),
        own_of(gain_cross, blank),
        own_of(blank, gain_cross),
        own_of(blank, gain_mlp),
        own_of(gain_mlp, blank),
    ]
    shift_delta = [
        own_of(blank, shift_self),
        own_of(shift_self, blank),
        own_of(shift_cross, blank),
        own_of(blank, shift_cross),
        own_of(blank, shift_mlp),
        own_of(shift_mlp, blank),
    ]
    table_part = table_sums(back_scores, rel_index)
    small = jnp.concatenate(gain_delta + shift_delta + [table_part.reshape(-1)])
    size = small.size
    small = jnp.pad(small, (0, LANES * LANES - size)).reshape(LANES, LANES)
    small = small + swap_core(small)
    small = small + swap_far(small)
    bit = 1
    while bit < blocks:
        small = small + lax.ppermute(small, "blk", [(i, i ^ bit) for i in range(blocks)])
        bit *= 2
    small = small.reshape(-1)
    at = (page * blocks + blk) * norm_gains.size
    delta_gains = lax.dynamic_slice_in_dim(small, at, norm_gains.size, 0)
    delta_shifts = lax.dynamic_slice_in_dim(small, 6 * D + at, norm_gains.size, 0)
    table_delta = small[12 * D : size].reshape(HEADS, RELS)
    question_shift = small[11 * D : 12 * D]

    def home(values):
        got = swap_far(own_of(values[1], values[0]))
        kept = own_of(values[0], values[1])
        return own_of(kept, got)[:share], own_of(got, kept)

    question_rows, visual_out = home(low(rows_three))
    question_out = gather_seats(question_rows, seat, blocks, jnp.bfloat16)
    question_back, visual_back = home(low(back_in))
    question_delta = gather_seats(question_back, seat, blocks, jnp.float32)

    def cuts(sums, widths):
        places = [sum(widths[:i]) for i in range(len(widths))]
        return [
            [side[:, at : at + width].reshape(-1) for at, width in zip(places, widths)]
            for side in sums
        ]

    causal, window = cuts(self_sums, (3 * D, D))
    reader, viewer = cuts(cross_sums, (D, 2 * D, D))
    return (
        visual_out,
        question_out,
        visual_back.astype(jnp.float32),
        question_delta,
        table_delta,
        window[0],
        window[1],
        causal[0],
        causal[1],
        reader[0],
        reader[1],
        reader[2],
        viewer[0],
        viewer[1],
        viewer[2],
        raise_sums[1].reshape(-1),
        lower_sums[1].reshape(-1),
        raise_sums[0].reshape(-1),
        lower_sums[0].reshape(-1),
        delta_gains,
        delta_shifts,
        question_shift,
    )


def solution(mesh):
    split, by_page, flat, whole = P(("page", "blk"), None), P("page", None), P(("page", "blk")), P()
    in_specs = (split, by_page, by_page, flat, whole, whole) + (flat,) * 16 + (split, by_page)
    out_specs = (split, by_page, split, by_page, whole) + (flat,) * 16 + (whole,)
    return jax.shard_map(body, mesh=mesh, in_specs=in_specs, out_specs=out_specs, check_vma=False)
```

time: 2680 us -> 703 us (0.26)
  waiting for transfers between devices: 1800 us -> 208 us
  local copies, waits for them, and re-layouts: 345 us -> 63.7 us
  starting transfers between devices: 1.76 us -> 162 us
  blocking collectives: 152 us -> 0 us
  matrix products: 202 us -> 73.3 us
  Pallas kernels: 0 us -> 114 us
  other arithmetic: 146 us -> 68.1 us
    unnamed x24 -> x0, waiting for transfers between devices: 1060 us -> none
    all_gather x20 -> x0, waiting for transfers between devices: 707 us -> none  [the longest x1 60.9 us: body(): lax.all_gather(question_up, ('page', 'blk'), axis=0, tiled=True)]
    ppermute x0 -> x182, waiting for transfers between devices: none -> 208 us  [the longest x18 47.2 us: ring_reduce(): one = lax.ppermute(low(chunk(step) + one), 'blk', ahead).astype(jnp.float32)]
    ppermute x0 -> x182, starting transfers between devices: none -> 162 us  [the longest x24 29.8 us: ring_pieces(): one = lax.ppermute(one, 'blk', ahead)]
    reshape x40 -> x29, local copies, waits for them, and re-layouts: 148 us -> 22.9 us  [the longest x10 9.2 us: block_of(): return flat.reshape(-1, columns)]
    pallas_call x0 -> x14, Pallas kernels: none -> 114 us  [the longest x2 24.8 us: cross_backward(): pl.pallas_call(cross_backward_kernel, out_shape=[jax.ShapeDtypeStruct((ro...]
    scatter-add x1 -> x0, other arithmetic: 112 us -> none  [body(): jax.ops.segment_sum(table_local.T, rel_index.reshape(-1), num_segments=RELS)]
    dot_general x51 -> x0, matrix products: 75.5 us -> none  [the longest x8 12.8 us: key_query_backward(): jnp.einsum('nhm,mhe->nhe', back_scores, keys, preferred_element_type=jnp....]
  transfers between devices with their start and end apart: 23 -> 182, of which waited for: 18 -> 65; matrix products, arithmetic and copies ran while one was open for 24% -> 20% of each run, Pallas kernels for 0% -> 13%
where the time goes in v1:
time: 703 us; the launch traced here: 693 us
  waiting for transfers between devices  208 us (30%)
  starting transfers between devices  162 us (23%)
  Pallas kernels  114 us (16%)
  matrix products  73.3 us (10%)
  other arithmetic  68.1 us (10%)
  local copies, waits for them, and re-layouts  63.7 us (9%)
    ppermute x18, waiting for transfers between devices, ring_reduce(): one = lax.ppermute(low(chunk(step) + one), 'blk', ahead).astype(jnp.float32)  47.2 us
    ppermute x24, waiting for transfers between devices, ring_pieces(): one = lax.ppermute(one, 'blk', ahead)  45.3 us
    ppermute x24, waiting for transfers between devices, ring_pieces(): two = lax.ppermute(two, 'blk', behind)  38.3 us
    dot_general x10, matrix products, transposed_times(): lax.dot_general(left, right, (((0,), (0,)), ((), ())), preferred_element_...  30 us
    ppermute x24, starting transfers between devices, ring_pieces(): one = lax.ppermute(one, 'blk', ahead)  29.8 us
    convert_element_type x48, other arithmetic, low(): return values.astype(jnp.bfloat16)  28.2 us
    dot_general x12, matrix products, times_transposed(): lax.dot_general(left, right, (((1,), (1,)), ((), ())), preferred_element_...  26.3 us
    ppermute x18, starting transfers between devices, ring_reduce(): one = lax.ppermute(low(chunk(step) + one), 'blk', ahead).astype(jnp.float32)  25 us
  transfers between devices with their start and end apart: 182, of which 65 were waited for; matrix products, arithmetic and copies ran while one was open for 20% of the time, Pallas kernels for 13%

profile of v1, /device:TPU:0, one launch (start us, length us, event | category | flops | bytes accessed | tf_op | source)
XLA Modules:
  0.0 692.6 jit_solution(16577548692834148182)
XLA Ops:
  52.8 7.5 %collective-permute-done.75.refs_2_ = bf16[2,96,768]{2,1,0:T(8,128)(2,1)} collective-permute-done((bf16[2,96,768]{2,1,0:T(8,128)(2,1)S(1)}, bf16[2,96,768]{2,1,0:T(8,128)(2,1)}, u32[]{:S(2)}, u32[]{:S(2)}) %collective-permute-start.75) | collective-permute-done | bytes 294944 | tf_op jit(solution)/shard_map/ppermute | solution.py:99
  73.0 14.1 %shard_map.400 = f32[144,16,144]{2,1,0:T(8,128)} custom-call(bf16[32,640]{1,0:T(8,128)(2,1)} %pad_maximum_fusion.9.table_ref, s32[144,144]{1,0:T(8,128)} %index_ref.3), custom_call_target="tpu_custom_call" | custom-call | flops 849346560 | bytes 1410048 | tf_op jit(solution)/shard_map/pallas_call | solution.py:224
  92.6 6.9 %collective-permute-done.76.refs_3_ = bf16[2,96,768]{2,1,0:T(8,128)(2,1)} collective-permute-done((bf16[2,96,768]{2,1,0:T(8,128)(2,1)S(1)}, bf16[2,96,768]{2,1,0:T(8,128)(2,1)}, u32[]{:S(2)}, u32[]{:S(2)}) %collective-permute-start.76) | collective-permute-done | bytes 294944 | tf_op jit(solution)/shard_map/ppermute | solution.py:98
  116.2 6.2 collective-permute-done.26.refs_6_
  191.0 10.5 %shard_map.401 = (bf16[2,144,768]{2,1,0:T(8,128)(2,1)S(1)}, f32[2,144,768]{2,1,0:T(8,128)S(1)}) custom-call(s32[2]{0:T(128)S(1)} %pad_add_fusion.1.role_ref, bf16[2,144,768]{2,1,0:T(8,128)(2,1)S(1)} %bitcast.918, bf16[2,656,1536]{2,1,0:T(8,128)(2,1)S(1)} %bitcast.897, bf16[2,656,1536]{2,1,0:T(8,128)(2,1)S(1)} %bitcast.898, f32[12,144,144]{2,1,0:T(8,128)S(1)} %bitcast.901, ...), custom_call_target="tpu_custom_call" | custom-call | flops 1160773632 | bytes 6045696 | tf_op jit(solution)/shard_map/pallas_call | solution.py:389
  203.3 11.7 %collective-permute-done.38 = bf16[2,144,768]{2,1,0:T(8,128)(2,1)S(1)} collective-permute-done((bf16[2,144,768]{2,1,0:T(8,128)(2,1)S(1)}, bf16[2,144,768]{2,1,0:T(8,128)(2,1)S(1)}, u32[]{:S(2)}, u32[]{:S(2)}) %collective-permute-start.38) | collective-permute-done | bytes 442400 | tf_op jit(solution)/shard_map/ppermute | solution.py:82
  253.9 7.0 %shard_map.403 = (bf16[144,768]{1,0:T(8,128)(2,1)S(1)}, f32[144,768]{1,0:T(8,128)S(1)}) custom-call(bf16[144,768]{1,0:T(8,128)(2,1)S(1)} %get-tuple-element.187.q_ref, bf16[1152,1536]{1,0:T(8,128)(2,1)S(1)} %convolution_convert_fusion.1.k_ref.v_ref, bf16[1152,1536]{1,0:T(8,128)(2,1)S(1)} %convolution_convert_fusion.1.k_ref.v_ref, ...), custom_call_target="tpu_custom_call" | custom-call | flops 2038431744 | bytes 3538944 | tf_op jit(solution)/shard_map/pallas_call | solution.py:465
  264.5 7.0 %shard_map.404 = (bf16[144,768]{1,0:T(8,128)(2,1)S(1)}, f32[144,768]{1,0:T(8,128)S(1)}) custom-call(bf16[144,768]{1,0:T(8,128)(2,1)S(1)} %get-tuple-element.186.q_ref, bf16[1152,1536]{1,0:T(8,128)(2,1)S(1)} %convolution_convert_fusion.k_ref.v_ref, bf16[1152,1536]{1,0:T(8,128)(2,1)S(1)} %convolution_convert_fusion.k_ref.v_ref, ...), custom_call_target="tpu_custom_call" | custom-call | flops 2038431744 | bytes 3538944 | tf_op jit(solution)/shard_map/pallas_call | solution.py:465
  276.7 11.9 %add_convert_fusion = (bf16[288,3072]{1,0:T(8,128)(2,1)}, f32[288,3072]{1,0:T(8,128)}) fusion(f32[288,3072]{1,0:T(8,128)} %fusion.166, bf16[288,768]{1,0:T(8,128)(2,1)S(1)} %bitcast.994, bf16[3072,768]{1,0:T(8,128)(2,1)S(1)} %bitcast.909), kind=kOutput, calls=%fused_computation.26 | convolution fusion | flops 1422655488 | bytes 14008320 | tf_op jit(solution)/shard_map/dot_general | solution.py:33
  288.6 5.0 multiply_convert_fusion
  293.7 6.5 convolution_convert_fusion.3
  303.2 6.0 convolution_convert_fusion.4
  313.7 12.4 %shard_map.409 = (bf16[144,768]{1,0:T(8,128)(2,1)S(1)}, bf16[1152,768]{1,0:T(8,128)(2,1)S(1)}, bf16[1152,768]{1,0:T(8,128)(2,1)S(1)}) custom-call(bf16[144,768]{1,0:T(8,128)(2,1)S(1)} %get-tuple-element.186.q_ref, bf16[1152,1536]{1,0:T(8,128)(2,1)S(1)} %convolution_convert_fusion.k_ref.v_ref, bf16[1152,1536]{1,0:T(8,128)(2,1)S(1)} %convolution_convert_fusion.k_ref.v_ref, ...), custom_call_target="tpu_custom_call" | custom-call | flops 5096079360 | bytes 7077888 | tf_op jit(solution)/shard_map/pallas_call | solution.py:484
  331.3 12.5 %shard_map.408 = (bf16[144,768]{1,0:T(8,128)(2,1)S(1)}, bf16[1152,768]{1,0:T(8,128)(2,1)S(1)}, bf16[1152,768]{1,0:T(8,128)(2,1)S(1)}) custom-call(bf16[144,768]{1,0:T(8,128)(2,1)S(1)} %get-tuple-element.187.q_ref, bf16[1152,1536]{1,0:T(8,128)(2,1)S(1)} %convolution_convert_fusion.1.k_ref.v_ref, bf16[1152,1536]{1,0:T(8,128)(2,1)S(1)} %convolution_convert_fusion.1.k_ref.v_ref, ...), custom_call_target="tpu_custom_call" | custom-call | flops 5096079360 | bytes 7077888 | tf_op jit(solution)/shard_map/pallas_call | solution.py:484
  385.2 5.2 collective-permute-done.103
  402.3 10.3 %collective-permute-done.157 = bf16[1,24,3072]{2,1,0:T(8,128)(2,1)S(1)} collective-permute-done((bf16[1,24,3072]{2,1,0:T(8,128)(2,1)S(1)}, bf16[1,24,3072]{2,1,0:T(8,128)(2,1)S(1)}, u32[]{:S(2)}, u32[]{:S(2)}) %collective-permute-start.157) | collective-permute-done | bytes 147488 | tf_op jit(solution)/shard_map/ppermute | solution.py:111
  441.3 6.5 collective-permute-done.107
  450.1 7.2 %collective-permute-done.154 = bf16[2,24,3072]{2,1,0:T(8,128)(2,1)S(1)} collective-permute-done((bf16[2,24,3072]{2,1,0:T(8,128)(2,1)S(1)}, bf16[2,24,3072]{2,1,0:T(8,128)(2,1)S(1)}, u32[]{:S(2)}, u32[]{:S(2)}) %collective-permute-start.154) | collective-permute-done | bytes 294944 | tf_op jit(solution)/shard_map/ppermute | solution.py:115
  460.2 5.3 collective-permute-done.159
  482.6 17.8 %shard_map.410 = (bf16[2,144,768]{2,1,0:T(8,128)(2,1)S(1)}, bf16[2,656,768]{2,1,0:T(8,128)(2,1)S(1)}, bf16[2,656,768]{2,1,0:T(8,128)(2,1)S(1)}, bf16[12,2,144,144]{3,2,1,0:T(8,128)(2,1)S(1)}) custom-call(s32[2]{0:T(128)S(1)} %pad_add_fusion.1.role_ref, bf16[2,144,768]{2,1,0:T(8,128)(2,1)S(1)} %bitcast.919, bf16[2,656,1536]{2,1,0:T(8,128)(2,1)S(1)} %bitcast.899, ...), custom_call_target="tpu_custom_call" | custom-call | flops 2901934080 | bytes 8060928 | tf_op jit(solution)/shard_map/pallas_call | solution.py:408
  513.5 19.7 %shard_map.412 = f32[24,640]{1,0:T(8,128)} custom-call(bf16[144,24,144]{2,1,0:T(8,128)(2,1)} %bitcast.962, s32[144,144]{1,0:T(8,128)} %index_ref.3), custom_call_target="tpu_custom_call" | custom-call | flops 637009920 | bytes 1078272 | tf_op jit(solution)/shard_map/pallas_call | solution.py:248
  585.1 6.2 collective-permute-done.164
  642.9 6.7 collective-permute-done.134
  668.4 5.6 collective-permute-done.125.refs_3_
  (882 shorter events, 472.9 us)
Async XLA Ops:
  6.1 28.2 %collective-permute-start.1 = (bf16[24,3200]{1,0:T(8,128)(2,1)}, bf16[24,3200]{1,0:T(8,128)(2,1)}, u32[]{:S(2)}, u32[]{:S(2)}) collective-permute-start(bf16[24,3200]{1,0:T(8,128)(2,1)} %broadcast_select_fusion.3), channel_id=1, source_target_pairs={{0,16},{8,24},{16,0},{24,8},{1,17},{9,25},{17,1},{25,9},{2,18},{10... | collective-permute-start | bytes 460808 | tf_op jit(solution)/shard_map/ppermute | solution.py:82
  9.7 25.7 %collective-permute-start.19 = (s32[1024]{0:T(1024)S(1)}, s32[1024]{0:T(1024)}, u32[]{:S(2)}, u32[]{:S(2)}) collective-permute-start(s32[1024]{0:T(1024)S(1)} %pad_select_fusion.2), channel_id=1, source_target_pairs={{0,16},{8,24},{16,0},{24,8},{1,17},{9,25},{17,1},{25,9},{2,18},{10... | collective-permute-start | bytes 12296 | tf_op jit(solution)/shard_map/ppermute | solution.py:82
  65.2 49.2 %collective-permute-start = (bf16[656,768]{1,0:T(8,128)(2,1)}, bf16[656,768]{1,0:T(8,128)(2,1)}, u32[]{:S(2)}, u32[]{:S(2)}) collective-permute-start(bf16[656,768]{1,0:T(8,128)(2,1)} %pad_select_fusion), channel_id=1, source_target_pairs={{0,16},{8,24},{16,0},{24,8},{1,17},{9,25},{17,1},{25,9},{2,18},{10... | collective-permute-start | bytes 3022856 | tf_op jit(solution)/shard_map/ppermute | solution.py:82
  67.5 22.7 %collective-permute-start.58 = (bf16[2,24,3072]{2,1,0:T(8,128)(2,1)}, bf16[2,24,3072]{2,1,0:T(8,128)(2,1)}, u32[]{:S(2)}, u32[]{:S(2)}) collective-permute-start(bf16[2,24,3072]{2,1,0:T(8,128)(2,1)} %collective-permute-done.56.refs_1_), channel_id=1, source_target_pairs={{0,2},{2,4},{4,6},{6,7},{7,5},{5,3},{3,1},{1,0},{8,10},{10,12},{12... | collective-permute-start | bytes 884744 | tf_op jit(solution)/shard_map/ppermute | solution.py:98
  302.6 60.7 %collective-permute-start.91 = (bf16[144,768]{1,0:T(8,128)(2,1)}, bf16[144,768]{1,0:T(8,128)(2,1)}, u32[]{:S(2)}, u32[]{:S(2)}) collective-permute-start(bf16[144,768]{1,0:T(8,128)(2,1)} %select_bitcast_fusion.7), channel_id=1, source_target_pairs={{0,16},{8,24},{16,0},{24,8},{1,17},{9,25},{17,1},{25,9},{2,18},{10... | collective-permute-start | bytes 663560 | tf_op jit(solution)/shard_map/ppermute | solution.py:82
  329.3 33.3 %collective-permute-start.109 = (bf16[72,768]{1,0:T(8,128)(2,1)S(1)}, bf16[72,768]{1,0:T(8,128)(2,1)S(1)}, u32[]{:S(2)}, u32[]{:S(2)}) collective-permute-start(bf16[72,768]{1,0:T(8,128)(2,1)S(1)} %get-tuple-element.165), channel_id=1, source_target_pairs={{0,2},{2,4},{4,6},{6,7},{7,5},{5,3},{3,1},{1,0},{8,10},{10,12},{12... | collective-permute-start | bytes 331784 | tf_op jit(solution)/shard_map/ppermute | solution.py:110
  330.9 48.0 %collective-permute-start.113 = (bf16[72,768]{1,0:T(8,128)(2,1)S(1)}, bf16[72,768]{1,0:T(8,128)(2,1)S(1)}, u32[]{:S(2)}, u32[]{:S(2)}) collective-permute-start(bf16[72,768]{1,0:T(8,128)(2,1)S(1)} %get-tuple-element.166), channel_id=1, source_target_pairs={{2,0},{4,2},{6,4},{7,6},{5,7},{3,5},{1,3},{0,1},{10,8},{12,10},{14... | collective-permute-start | bytes 331784 | tf_op jit(solution)/shard_map/ppermute | solution.py:111
  356.2 28.9 %collective-permute-start.105 = (bf16[72,768]{1,0:T(8,128)(2,1)S(1)}, bf16[72,768]{1,0:T(8,128)(2,1)S(1)}, u32[]{:S(2)}, u32[]{:S(2)}) collective-permute-start(bf16[72,768]{1,0:T(8,128)(2,1)S(1)} %get-tuple-element.164), channel_id=1, source_target_pairs={{2,0},{4,2},{6,4},{7,6},{5,7},{3,5},{1,3},{0,1},{10,8},{12,10},{14... | collective-permute-start | bytes 331784 | tf_op jit(solution)/shard_map/ppermute | solution.py:111
  362.6 29.4 %collective-permute-start.152 = (bf16[2,8,24,768]{3,2,0,1:T(8,128)(2,1)S(1)}, bf16[2,8,24,768]{3,2,0,1:T(8,128)(2,1)S(1)}, u32[]{:S(2)}, u32[]{:S(2)}) collective-permute-start(bf16[2,8,24,768]{3,2,0,1:T(8,128)(2,1)S(1)} %copy_bitcast_fusion.4), channel_id=1, source_target_pairs={{0,8},{8,0},{16,24},{24,16},{1,9},{9,1},{17,25},{25,17},{2,10},{10... | collective-permute-start | bytes 1769480 | tf_op jit(solution)/shard_map/ppermute | solution.py:86
  362.7 36.6 %collective-permute-start.151 = (bf16[2,8,24,768]{3,2,0,1:T(8,128)(2,1)S(1)}, bf16[2,8,24,768]{3,2,0,1:T(8,128)(2,1)S(1)}, u32[]{:S(2)}, u32[]{:S(2)}) collective-permute-start(bf16[2,8,24,768]{3,2,0,1:T(8,128)(2,1)S(1)} %copy_bitcast_fusion.5), channel_id=1, source_target_pairs={{0,8},{8,0},{16,24},{24,16},{1,9},{9,1},{17,25},{25,17},{2,10},{10... | collective-permute-start | bytes 1769480 | tf_op jit(solution)/shard_map/ppermute | solution.py:86
  396.1 166.6 %collective-permute-start.162 = (bf16[2,8,24,3072]{3,2,0,1:T(8,128)(2,1)}, bf16[2,8,24,3072]{3,2,0,1:T(8,128)(2,1)}, u32[]{:S(2)}, u32[]{:S(2)}) collective-permute-start(bf16[2,8,24,3072]{3,2,0,1:T(8,128)(2,1)} %copy_bitcast_fusion.1), channel_id=1, source_target_pairs={{0,8},{8,0},{16,24},{24,16},{1,9},{9,1},{17,25},{25,17},{2,10},{10... | collective-permute-start | bytes 7077896 | tf_op jit(solution)/shard_map/ppermute | solution.py:86
  397.7 22.4 %collective-permute-start.94 = (bf16[128,768]{1,0:T(8,128)(2,1)S(1)}, bf16[128,768]{1,0:T(8,128)(2,1)S(1)}, u32[]{:S(2)}, u32[]{:S(2)}) collective-permute-start(bf16[128,768]{1,0:T(8,128)(2,1)S(1)} %collective-permute-done.92.refs_1_), channel_id=1, source_target_pairs={{0,2},{2,4},{4,6},{6,7},{7,5},{5,3},{3,1},{1,0},{8,10},{10,12},{12... | collective-permute-start | bytes 589832 | tf_op jit(solution)/shard_map/ppermute | solution.py:98
  399.3 21.5 %collective-permute-start.95 = (bf16[128,768]{1,0:T(8,128)(2,1)S(1)}, bf16[128,768]{1,0:T(8,128)(2,1)S(1)}, u32[]{:S(2)}, u32[]{:S(2)}) collective-permute-start(bf16[128,768]{1,0:T(8,128)(2,1)S(1)} %collective-permute-done.93.refs_2_), channel_id=1, source_target_pairs={{2,0},{4,2},{6,4},{7,6},{5,7},{3,5},{1,3},{0,1},{10,8},{12,10},{14... | collective-permute-start | bytes 589832 | tf_op jit(solution)/shard_map/ppermute | solution.py:99
  399.7 22.4 %collective-permute-start.114 = (bf16[144,768]{1,0:T(8,128)(2,1)S(1)}, bf16[144,768]{1,0:T(8,128)(2,1)S(1)}, u32[]{:S(2)}, u32[]{:S(2)}) collective-permute-start(bf16[144,768]{1,0:T(8,128)(2,1)S(1)} %get-tuple-element.104), channel_id=1, source_target_pairs={{2,0},{4,2},{6,4},{7,6},{5,7},{3,5},{1,3},{0,1},{10,8},{12,10},{14... | collective-permute-start | bytes 663560 | tf_op jit(solution)/shard_map/ppermute | solution.py:116
  418.7 39.4 %collective-permute-start.112 = (bf16[144,768]{1,0:T(8,128)(2,1)S(1)}, bf16[144,768]{1,0:T(8,128)(2,1)S(1)}, u32[]{:S(2)}, u32[]{:S(2)}) collective-permute-start(bf16[144,768]{1,0:T(8,128)(2,1)S(1)} %get-tuple-element.103), channel_id=1, source_target_pairs={{0,2},{2,4},{4,6},{6,7},{7,5},{5,3},{3,1},{1,0},{8,10},{10,12},{12... | collective-permute-start | bytes 663560 | tf_op jit(solution)/shard_map/ppermute | solution.py:115
  435.7 33.4 %collective-permute-start.104 = (bf16[144,768]{1,0:T(8,128)(2,1)S(1)}, bf16[144,768]{1,0:T(8,128)(2,1)S(1)}, u32[]{:S(2)}, u32[]{:S(2)}) collective-permute-start(bf16[144,768]{1,0:T(8,128)(2,1)S(1)} %get-tuple-element.101), channel_id=1, source_target_pairs={{0,2},{2,4},{4,6},{6,7},{7,5},{5,3},{3,1},{1,0},{8,10},{10,12},{12... | collective-permute-start | bytes 663560 | tf_op jit(solution)/shard_map/ppermute | solution.py:115
  474.6 65.6 %collective-permute-start.161 = (bf16[24,3072]{1,0:T(8,128)(2,1)}, bf16[24,3072]{1,0:T(8,128)(2,1)}, u32[]{:S(2)}, u32[]{:S(2)}) collective-permute-start(bf16[24,3072]{1,0:T(8,128)(2,1)} %fusion.115), channel_id=1, source_target_pairs={{0,16},{8,24},{16,0},{24,8},{1,17},{9,25},{17,1},{25,9},{2,18},{10... | collective-permute-start | bytes 442376 | tf_op jit(solution)/shard_map/ppermute | solution.py:82
  510.3 31.5 %collective-permute-start.118 = (bf16[2,128,768]{2,1,0:T(8,128)(2,1)S(1)}, bf16[2,128,768]{2,1,0:T(8,128)(2,1)}, u32[]{:S(2)}, u32[]{:S(2)}) collective-permute-start(bf16[2,128,768]{2,1,0:T(8,128)(2,1)S(1)} %select_convert_fusion), channel_id=1, source_target_pairs={{2,0},{4,2},{6,4},{7,6},{5,7},{3,5},{1,3},{10,8},{12,10},{14,12},{... | collective-permute-start | bytes 1179656 | tf_op jit(solution)/shard_map/ppermute | solution.py:770
  566.1 41.4 %collective-permute-start.167 = (bf16[1,24,3072]{2,1,0:T(8,128)(2,1)S(1)}, bf16[1,24,3072]{2,1,0:T(8,128)(2,1)S(1)}, u32[]{:S(2)}, u32[]{:S(2)}) collective-permute-start(bf16[1,24,3072]{2,1,0:T(8,128)(2,1)S(1)} %get-tuple-element.193), channel_id=1, source_target_pairs={{2,0},{4,2},{6,4},{7,6},{5,7},{3,5},{1,3},{0,1},{10,8},{12,10},{14... | collective-permute-start | bytes 442376 | tf_op jit(solution)/shard_map/ppermute | solution.py:111
  569.6 46.1 %collective-permute-start.177 = (bf16[1,96,768]{2,1,0:T(8,128)(2,1)S(1)}, bf16[1,96,768]{2,1,0:T(8,128)(2,1)S(1)}, u32[]{:S(2)}, u32[]{:S(2)}) collective-permute-start(bf16[1,96,768]{2,1,0:T(8,128)(2,1)S(1)} %get-tuple-element.191), channel_id=1, source_target_pairs={{2,0},{4,2},{6,4},{7,6},{5,7},{3,5},{1,3},{0,1},{10,8},{12,10},{14... | collective-permute-start | bytes 442376 | tf_op jit(solution)/shard_map/ppermute | solution.py:111
  576.0 23.1 %collective-permute-start.120 = (bf16[2,128,768]{2,1,0:T(8,128)(2,1)S(1)}, bf16[2,128,768]{2,1,0:T(8,128)(2,1)S(1)}, u32[]{:S(2)}, u32[]{:S(2)}) collective-permute-start(bf16[2,128,768]{2,1,0:T(8,128)(2,1)S(1)} %add_convert_fusion.5), channel_id=1, source_target_pairs={{2,0},{4,2},{6,4},{7,6},{5,7},{3,5},{1,3},{10,8},{12,10},{14,12},{... | collective-permute-start | bytes 1179656 | tf_op jit(solution)/shard_map/ppermute | solution.py:770
  618.8 47.8 %collective-permute-start.166 = (bf16[2,24,3072]{2,1,0:T(8,128)(2,1)S(1)}, bf16[2,24,3072]{2,1,0:T(8,128)(2,1)}, u32[]{:S(2)}, u32[]{:S(2)}) collective-permute-start(bf16[2,24,3072]{2,1,0:T(8,128)(2,1)S(1)} %get-tuple-element.99), channel_id=1, source_target_pairs={{0,2},{2,4},{4,6},{6,7},{7,5},{5,3},{3,1},{1,0},{8,10},{10,12},{12... | collective-permute-start | bytes 884744 | tf_op jit(solution)/shard_map/ppermute | solution.py:115
  634.1 23.9 %collective-permute-start.169 = (bf16[2,24,3072]{2,1,0:T(8,128)(2,1)}, bf16[2,24,3072]{2,1,0:T(8,128)(2,1)}, u32[]{:S(2)}, u32[]{:S(2)}) collective-permute-start(bf16[2,24,3072]{2,1,0:T(8,128)(2,1)} %fusion.79), channel_id=1, source_target_pairs={{2,0},{4,2},{6,4},{7,6},{5,7},{3,5},{1,3},{0,1},{10,8},{12,10},{14... | collective-permute-start | bytes 884744 | tf_op jit(solution)/shard_map/ppermute | solution.py:116
  637.2 26.5 %collective-permute-start.179 = (bf16[2,96,768]{2,1,0:T(8,128)(2,1)S(1)}, bf16[2,96,768]{2,1,0:T(8,128)(2,1)}, u32[]{:S(2)}, u32[]{:S(2)}) collective-permute-start(bf16[2,96,768]{2,1,0:T(8,128)(2,1)S(1)} %fusion.64), channel_id=1, source_target_pairs={{2,0},{4,2},{6,4},{7,6},{5,7},{3,5},{1,3},{0,1},{10,8},{12,10},{14... | collective-permute-start | bytes 884744 | tf_op jit(solution)/shard_map/ppermute | solution.py:116
  (263 other events, 2441.8 us)

commit v2 on v1

v2 whole, which is shorter than its diff:
```python
import functools

import jax
import jax.numpy as jnp
from jax import lax
from jax.experimental import pallas as pl
from jax.experimental.pallas import tpu as pltpu
from jax.sharding import PartitionSpec as P

D = 768
HEADS = 12
HEAD_DIM = 64
FF = 3072
Q_LEN = 1024
WIN = 144
RELS = 529
LONGEST = Q_LEN // 2
LANES = 128
PAIRS = D // LANES
RELS_PAD = 640

EPS = 1e-05
NEG = -1000000000.0
SCALE = HEAD_DIM ** (-0.5)
MIB = 1 << 20


def product(left, right):
    return jnp.dot(left, right, preferred_element_type=jnp.float32)


def times_transposed(left, right):
    return lax.dot_general(
        left, right, (((1,), (1,)), ((), ())), preferred_element_type=jnp.float32
    )


def transposed_times(left, right):
    return lax.dot_general(
        left, right, (((0,), (0,)), ((), ())), preferred_element_type=jnp.float32
    )


def low(values):
    return values.astype(jnp.bfloat16)


def normalize(rows, gain, shift):
    mean = jnp.mean(rows, axis=-1, keepdims=True)
    centred = rows - mean
    spread = jnp.mean(centred * centred, axis=-1, keepdims=True)
    return centred * lax.rsqrt(spread + EPS) * gain + shift


def smooth(values):
    return jax.nn.gelu(values, approximate=False)


def ring_order(blocks):
    return tuple(range(0, blocks, 2)) + tuple(range(blocks - 1, 0, -2))


def ring_seat(blk, blocks):
    return jnp.where(blk % 2 == 0, blk // 2, blocks - 1 - blk // 2)


def ring_place(seat, blocks):
    seat = lax.rem(seat + 2 * blocks, blocks)
    return jnp.where(seat < blocks // 2, 2 * seat, 2 * (blocks - 1 - seat) + 1)


def forward_hop(blocks):
    order = ring_order(blocks)
    return [(order[i], order[(i + 1) % blocks]) for i in range(blocks)]


def backward_hop(blocks):
    return [(there, here) for here, there in forward_hop(blocks)]


def swap_far(values):
    return lax.ppermute(values, "far", [(0, 1), (1, 0)])


def swap_core(values):
    return lax.ppermute(values, "core", [(0, 1), (1, 0)])


OFFSETS = (0, -1, 1, -2, 2, -3, 3, 4)


class Gather:
    def __init__(self, own, blocks):
        self.hops = forward_hop(blocks), backward_hop(blocks)
        self.half = own.shape[0] // 2
        self.pieces, self.step, self.state = {0: own}, 0, (own, own)

    def send(self):
        one, two = self.state
        if self.step == 3:
            one, two = one[: self.half], two[self.half :]
        return lax.ppermute(one, "blk", self.hops[0]), lax.ppermute(two, "blk", self.hops[1])

    def receive(self, found):
        self.step, self.state = self.step + 1, found
        if self.step == 4:
            self.pieces["first"], self.pieces["second"] = found
        else:
            self.pieces[-self.step], self.pieces[self.step] = found


class Circle:
    def __init__(self, own, blocks):
        self.hops, self.left = forward_hop(blocks), blocks - 1
        self.pieces = [own]

    def send(self):
        return lax.ppermute(self.pieces[-1], "blk", self.hops)

    def receive(self, found):
        self.pieces.append(found)
        self.left -= 1


class Sum:
    def __init__(self, chunk, blocks):
        self.hops = forward_hop(blocks), backward_hop(blocks)
        self.chunk, self.step = chunk, 0
        most = chunk(4)
        half = most.shape[0] // 2
        self.state = lax.optimization_barrier((low(most[:half]), low(most[half:])))

    def send(self):
        one, two = self.state
        return lax.ppermute(one, "blk", self.hops[0]), lax.ppermute(two, "blk", self.hops[1])

    def receive(self, found):
        one, two = [item.astype(jnp.float32) for item in found]
        if self.step == 0:
            blank = jnp.zeros(one.shape, jnp.float32)
            one, two = jnp.concatenate([one, blank]), jnp.concatenate([blank, two])
        self.step += 1
        left = 4 - self.step
        if left == 0:
            self.total = self.chunk(0) + one + two
        else:
            self.state = low(self.chunk(left) + one), low(self.chunk(-left) + two)
            self.state = lax.optimization_barrier(self.state)


class Once:
    def __init__(self, send):
        self.send = send

    def receive(self, found):
        self.found = found


def phase(transfers, work=()):
    found = [item.send() for item in transfers]
    found, work = lax.optimization_barrier((found, work))
    for item, one in zip(transfers, found):
        item.receive(one)
    return work


def whole_block(array):
    blank = (0,) * len(array.shape)
    return pl.BlockSpec(array.shape, lambda i, where: blank)


def assemble_kernel(plan, count, where_ref, *refs):
    pieces, outs = refs[:count], refs[count:]
    for piece, (index, first, core) in zip(pieces, plan):
        start = 0
        for out in outs:
            width = out.shape[-1]
            for number in range(piece.shape[0]):
                target = (first + number, where_ref[core], where_ref[index])
                out[target] = piece[number, :, start : start + width]
            start += width


def assemble(own, other, splits, core, seat, blocks):
    rows = own[0].shape[1]
    places = [ring_place(seat + k, blocks) for k in OFFSETS]
    where = jnp.stack([core, 1 - core] + places).astype(jnp.int32)
    pieces, plan = [], []
    for side, group in ((0, own), (1, other)):
        for number, offset in enumerate(OFFSETS):
            if offset == 4:
                pieces += [group["first"], group["second"]]
                plan += [(2 + number, 0, side), (2 + number, 1, side)]
            else:
                pieces.append(group[offset])
                plan.append((2 + number, 0, side))
    outs = [jax.ShapeDtypeStruct((2, 2, blocks, rows, width), jnp.bfloat16) for width in splits]
    found = pl.pallas_call(
        functools.partial(assemble_kernel, plan, len(pieces)),
        out_shape=outs,
        grid_spec=pltpu.PrefetchScalarGridSpec(
            num_scalar_prefetch=1,
            grid=(1,),
            in_specs=[whole_block(item) for item in pieces],
            out_specs=[whole_block(item) for item in outs],
        ),
        compiler_params=pltpu.CompilerParams(vmem_limit_bytes=32 * MIB),
        cost_estimate=pl.CostEstimate(
            flops=0, bytes_accessed=16 * blocks * rows * sum(splits), transcendentals=0
        ),
    )(where, *pieces)
    return [item.reshape(4 * blocks * rows, -1) for item in found]


def place_kernel(plan, where_ref, *refs):
    pieces, out = refs[:-1], refs[-1]
    for piece, (index, first, last) in zip(pieces, plan):
        out[where_ref[index], first:last] = piece[...].astype(out.dtype)


def seats_in_order(found, seat, blocks, dtype):
    columns = found[0][2].shape[1]
    rows = max(piece.shape[0] for unused, also, piece in found)
    where = [lax.rem(seat + offset + blocks, blocks) for offset, unused, also in found]
    where = jnp.stack(where).astype(jnp.int32)
    pieces = [piece for unused, also, piece in found]
    plan = [(i, at, at + item[2].shape[0]) for i, item in enumerate(found) for at in [item[1]]]
    out = jax.ShapeDtypeStruct((blocks, rows, columns), dtype)
    placed = pl.pallas_call(
        functools.partial(place_kernel, plan),
        out_shape=out,
        grid_spec=pltpu.PrefetchScalarGridSpec(
            num_scalar_prefetch=1,
            grid=(1,),
            in_specs=[whole_block(item) for item in pieces],
            out_specs=whole_block(out),
        ),
        compiler_params=pltpu.CompilerParams(vmem_limit_bytes=24 * MIB),
        cost_estimate=pl.CostEstimate(
            flops=0, bytes_accessed=6 * blocks * rows * columns, transcendentals=0
        ),
    )(where, *pieces)
    return placed.reshape(blocks * rows, columns)


def bias_kernel(role_ref, table_ref, index_ref, out_ref):
    def one(i, carry):
        row = index_ref[pl.ds(i, 1), :]
        marks = lax.broadcasted_iota(jnp.int32, (RELS_PAD, WIN), 0) == row
        hot = low(jnp.where(marks, 1.0, 0.0))
        both = jnp.dot(table_ref[...], hot, preferred_element_type=jnp.float32)
        out_ref[i] = both[:16] + both[16:]
        return carry

    @pl.when(role_ref[0] != 0)
    def visual():
        lax.fori_loop(0, WIN, one, 0, unroll=4)

    @pl.when(role_ref[0] == 0)
    def question():
        out_ref[...] = jnp.zeros_like(out_ref)


def window_bias(role, rel_table, rel_index):
    table = jnp.pad(rel_table, ((0, 16 - HEADS), (0, RELS_PAD - RELS)))
    coarse = lax.reduce_precision(table, 8, 7)
    both = low(jnp.concatenate([coarse, table - coarse]))
    found = pl.pallas_call(
        bias_kernel,
        out_shape=jax.ShapeDtypeStruct((WIN, 16, WIN), jnp.float32),
        in_specs=[pl.BlockSpec(memory_space=pltpu.SMEM)] + [pl.BlockSpec()] * 2,
        cost_estimate=pl.CostEstimate(
            flops=64 * RELS_PAD * WIN * WIN, bytes_accessed=4 * 17 * WIN * WIN, transcendentals=0
        ),
    )(role, both, rel_index)
    return found[:, :HEADS].transpose(1, 0, 2)


def table_kernel(role_ref, scores_ref, index_ref, out_ref):
    def one(i, total):
        row = index_ref[pl.ds(i, 1), :]
        marks = lax.broadcasted_iota(jnp.int32, (RELS_PAD, WIN), 0) == row
        hot = low(jnp.where(marks, 1.0, 0.0))
        return total + times_transposed(scores_ref[i], hot)

    blank = jnp.zeros((2 * HEADS, RELS_PAD), jnp.float32)

    @pl.when(role_ref[0] != 0)
    def visual():
        out_ref[...] = lax.fori_loop(0, WIN, one, blank, unroll=4)

    @pl.when(role_ref[0] == 0)
    def question():
        out_ref[...] = blank


def table_sums(role, back_scores, rel_index):
    rows = back_scores.reshape(2 * HEADS, WIN, WIN).transpose(1, 0, 2)
    found = pl.pallas_call(
        table_kernel,
        out_shape=jax.ShapeDtypeStruct((2 * HEADS, RELS_PAD), jnp.float32),
        in_specs=[pl.BlockSpec(memory_space=pltpu.SMEM)] + [pl.BlockSpec()] * 2,
        cost_estimate=pl.CostEstimate(
            flops=48 * RELS_PAD * WIN * WIN, bytes_accessed=52 * WIN * WIN, transcendentals=0
        ),
    )(role, rows, rel_index)
    return jnp.sum(found.reshape(HEADS, 2, RELS_PAD), axis=1)[:, :RELS]


def head_lanes(side):
    lane = lax.broadcasted_iota(jnp.int32, (1, LANES), 1)
    return (lane < HEAD_DIM) if side == 0 else (lane >= HEAD_DIM)


def attend_pair(query, keys, values, extras):
    result, logs = None, None
    for side in (0, 1):
        mine = head_lanes(side)
        one = jnp.where(mine, query * SCALE, 0).astype(jnp.bfloat16)
        scores = times_transposed(one, keys) + extras[side]
        top = jnp.max(scores, axis=-1, keepdims=True)
        expo = jnp.exp(scores - top)
        total = jnp.sum(expo, axis=-1, keepdims=True)
        found = product(low(expo), values) / total
        log_total = jnp.broadcast_to(top + jnp.log(total), found.shape)
        result = found if side == 0 else jnp.where(mine, found, result)
        logs = log_total if side == 0 else jnp.where(mine, log_total, logs)
    return low(result), logs


def pair_backward(query, keys, values, extras, logs, back_out):
    back_query, back_keys, back_values, kept = None, None, None, []
    for side in (0, 1):
        mine = head_lanes(side)
        one = jnp.where(mine, query * SCALE, 0).astype(jnp.bfloat16)
        back_one = jnp.where(mine, back_out, 0).astype(jnp.bfloat16)
        scores = times_transposed(one, keys) + extras[side]
        first = side * HEAD_DIM
        shares = jnp.exp(scores - logs[:, first : first + 1])
        back_shares = times_transposed(back_one, values)
        inner = jnp.sum(shares * back_shares, axis=-1, keepdims=True)
        back_scores = low(shares * (back_shares - inner))
        found = product(back_scores, keys) * SCALE
        found_keys = transposed_times(back_scores, one)
        found_values = transposed_times(low(shares), back_one)
        kept.append(back_scores)
        if side == 0:
            back_query, back_keys, back_values = found, found_keys, found_values
        else:
            back_query = jnp.where(mine, found, back_query)
            back_keys, back_values = back_keys + found_keys, back_values + found_values
    return low(back_query), low(back_keys), low(back_values), kept


def question_extra(role_ref, qid, kid):
    shape = (qid.shape[0], kid.shape[1])
    row = lax.broadcasted_iota(jnp.int32, shape, 0) + role_ref[1]
    column = lax.broadcasted_iota(jnp.int32, shape, 1)
    return jnp.where((qid == kid) & (column <= row), 0.0, NEG)


def window_extras(bias_ref, qid, kid):
    same = jnp.where(qid == kid, 0.0, NEG)
    return [bias_ref[0] + same, bias_ref[1] + same]


def self_forward_kernel(
    role_ref, q_ref, k_ref, v_ref, bias_ref, qid_ref, kid_ref, o_ref, log_ref
):
    rows = q_ref.shape[1]

    @pl.when(role_ref[0] == 0)
    def question():
        for s in (0, 1):
            extra = question_extra(role_ref, qid_ref[s], kid_ref[s])
            o_ref[s], log_ref[s] = attend_pair(q_ref[s], k_ref[s], v_ref[s], [extra, extra])

    @pl.when(role_ref[0] != 0)
    def visual():
        for s in (0, 1):
            extras = window_extras(bias_ref, qid_ref[s], kid_ref[s, :, :rows])
            o_ref[s], log_ref[s] = attend_pair(
                q_ref[s], k_ref[s, :rows], v_ref[s, :rows], extras
            )


def self_backward_kernel(
    role_ref,
    q_ref,
    k_ref,
    v_ref,
    bias_ref,
    qid_ref,
    kid_ref,
    log_ref,
    back_ref,
    dq_ref,
    dk_ref,
    dv_ref,
    ds_ref,
):
    rows = q_ref.shape[1]

    @pl.when(role_ref[0] == 0)
    def question():
        ds_ref[...] = jnp.zeros_like(ds_ref)
        for s in (0, 1):
            extra = question_extra(role_ref, qid_ref[s], kid_ref[s])
            dq_ref[s], dk_ref[s], dv_ref[s], unused = pair_backward(
                q_ref[s], k_ref[s], v_ref[s], [extra, extra], log_ref[s], back_ref[s]
            )

    @pl.when(role_ref[0] != 0)
    def visual():
        dk_ref[...] = jnp.zeros_like(dk_ref)
        dv_ref[...] = jnp.zeros_like(dv_ref)
        for s in (0, 1):
            extras = window_extras(bias_ref, qid_ref[s], kid_ref[s, :, :rows])
            dq_ref[s], found_keys, found_values, kept = pair_backward(
                q_ref[s], k_ref[s, :rows], v_ref[s, :rows], extras, log_ref[s], back_ref[s]
            )
            dk_ref[s, :rows] = found_keys
            dv_ref[s, :rows] = found_values
            ds_ref[0, s] = kept[0]
            ds_ref[1, s] = kept[1]


def self_specs(rows, span):
    query = pl.BlockSpec((2, rows, LANES), lambda h, role: (0, 0, h))
    keys = pl.BlockSpec((2, span, LANES), lambda h, role: (0, 0, h))
    bias = pl.BlockSpec((2, rows, rows), lambda h, role: (h, 0, 0))
    qid = pl.BlockSpec((2, rows, 1), lambda h, role: (0, 0, 0))
    kid = pl.BlockSpec((2, 1, span), lambda h, role: (0, 0, 0))
    return query, keys, keys, bias, qid, kid


def self_forward(role, query, keys, values, bias, qid, kid):
    rows, span = query.shape[1], keys.shape[1]
    specs = self_specs(rows, span)
    return pl.pallas_call(
        self_forward_kernel,
        out_shape=[
            jax.ShapeDtypeStruct((2, rows, D), jnp.bfloat16),
            jax.ShapeDtypeStruct((2, rows, D), jnp.float32),
        ],
        grid_spec=pltpu.PrefetchScalarGridSpec(
            num_scalar_prefetch=1, grid=(PAIRS,), in_specs=list(specs), out_specs=[specs[0]] * 2
        ),
        compiler_params=pltpu.CompilerParams(vmem_limit_bytes=24 * MIB),
        cost_estimate=pl.CostEstimate(
            flops=16 * rows * span * D, bytes_accessed=12 * span * D, transcendentals=0
        ),
    )(role, query, keys, values, bias, qid, kid)


def self_backward(role, query, keys, values, bias, qid, kid, logs, back_out):
    rows, span = query.shape[1], keys.shape[1]
    specs = self_specs(rows, span)
    return pl.pallas_call(
        self_backward_kernel,
        out_shape=[
            jax.ShapeDtypeStruct((2, rows, D), jnp.bfloat16),
            jax.ShapeDtypeStruct((2, span, D), jnp.bfloat16),
            jax.ShapeDtypeStruct((2, span, D), jnp.bfloat16),
            jax.ShapeDtypeStruct((HEADS, 2, rows, rows), jnp.bfloat16),
        ],
        grid_spec=pltpu.PrefetchScalarGridSpec(
            num_scalar_prefetch=1,
            grid=(PAIRS,),
            in_specs=list(specs) + [specs[0]] * 2,
            out_specs=[
                specs[0],
                specs[1],
                specs[1],
                pl.BlockSpec((2, 2, rows, rows), lambda h, role: (h, 0, 0, 0)),
            ],
        ),
        compiler_params=pltpu.CompilerParams(vmem_limit_bytes=24 * MIB),
        cost_estimate=pl.CostEstimate(
            flops=40 * rows * span * D, bytes_accessed=16 * span * D, transcendentals=0
        ),
    )(role, query, keys, values, bias, qid, kid, logs, back_out)


def cross_forward_kernel(q_ref, k_ref, v_ref, extra_ref, o_ref, log_ref):
    extra = extra_ref[...]
    o_ref[0], log_ref[0] = attend_pair(q_ref[0], k_ref[0], v_ref[0], [extra, extra])


def cross_backward_kernel(
    q_ref, k_ref, v_ref, extra_ref, log_ref, back_ref, dq_ref, dk_ref, dv_ref
):
    extra = extra_ref[...]
    dq_ref[0], dk_ref[0], dv_ref[0], unused = pair_backward(
        q_ref[0], k_ref[0], v_ref[0], [extra, extra], log_ref[0], back_ref[0]
    )


def cross_specs(rows, span):
    query = pl.BlockSpec((1, rows, LANES), lambda s, h: (s, 0, h))
    keys = pl.BlockSpec((1, span, LANES), lambda s, h: (s, 0, h))
    extra = pl.BlockSpec((1, span), lambda s, h: (0, 0))
    return query, keys, keys, extra


def cross_limit(span):
    return (24 if span <= 2048 else 60) * MIB


def cross_forward(query, keys, values, extra):
    rows, span = query.shape[1], keys.shape[1]
    specs = cross_specs(rows, span)
    return pl.pallas_call(
        cross_forward_kernel,
        out_shape=[
            jax.ShapeDtypeStruct((2, rows, D), jnp.bfloat16),
            jax.ShapeDtypeStruct((2, rows, D), jnp.float32),
        ],
        grid=(2, PAIRS),
        in_specs=list(specs),
        out_specs=[specs[0]] * 2,
        compiler_params=pltpu.CompilerParams(vmem_limit_bytes=cross_limit(span)),
        cost_estimate=pl.CostEstimate(
            flops=32 * rows * span * D, bytes_accessed=8 * span * D, transcendentals=0
        ),
    )(query, keys, values, extra)


def cross_backward(query, keys, values, extra, logs, back_out):
    rows, span = query.shape[1], keys.shape[1]
    specs = cross_specs(rows, span)
    return pl.pallas_call(
        cross_backward_kernel,
        out_shape=[
            jax.ShapeDtypeStruct((2, rows, D), jnp.bfloat16),
            jax.ShapeDtypeStruct((2, span, D), jnp.bfloat16),
            jax.ShapeDtypeStruct((2, span, D), jnp.bfloat16),
        ],
        grid=(2, PAIRS),
        in_specs=list(specs) + [specs[0]] * 2,
        out_specs=[specs[0], specs[1], specs[1]],
        compiler_params=pltpu.CompilerParams(vmem_limit_bytes=cross_limit(span)),
        cost_estimate=pl.CostEstimate(
            flops=80 * rows * span * D, bytes_accessed=16 * span * D, transcendentals=0
        ),
    )(query, keys, values, extra, logs, back_out)


TILES = FF // D
HALF_ROOT = 0.5**0.5
BELL = (0.5 / 3.141592653589793) ** 0.5


def mlp_kernel(places, h_ref, g_ref, up_ref, down_ref, out_ref, back_ref, delta_ref, tile_ref):
    step = pl.program_id(0)
    far, core = step // 2, step % 2
    cut = delta_ref.shape[3]

    for place in range(places):
        for part in range(TILES):
            row = (place * TILES + part) * cut
            tile_ref[row : row + cut] = down_ref[part, place * cut : (place + 1) * cut]
    rows, branch, up, down = h_ref[...], g_ref[...], up_ref[0], tile_ref[...]
    upward = product(rows, up)
    lift = times_transposed(branch, down)
    chance = 0.5 * (1.0 + lax.erf(upward * HALF_ROOT))
    active = low(upward * chance)
    slope = chance + upward * jnp.exp(-0.5 * upward * upward) * BELL
    back_up = low(slope * lift)
    out, back = product(active, down), times_transposed(back_up, up)

    @pl.when(step == 0)
    def start():
        out_ref[...] = out
        back_ref[...] = back

    @pl.when(step > 0)
    def add():
        out_ref[...] += out
        back_ref[...] += back

    delta_up = low(transposed_times(rows, back_up))
    for side in range(2):
        for place in range(2 * places):
            row = (side * 2 * places + place) * cut
            delta_ref[place, step, side] = delta_up[row : row + cut]
    delta_down = low(transposed_times(active, branch))
    for place in range(places):
        for part in range(TILES):
            row = (place * TILES + part) * cut
            delta_ref[core * places + place, TILES + part, far] = delta_down[row : row + cut]


def mlp(rows, branch, weights, blocks):
    count = rows.shape[0]
    cut = D // (4 * blocks)
    resident = pl.BlockSpec((count, D), lambda i: (0, 0))
    shape = (2 * blocks, 2 * TILES, 2, cut, D)
    return pl.pallas_call(
        functools.partial(mlp_kernel, blocks),
        out_shape=[
            jax.ShapeDtypeStruct((count, D), jnp.float32),
            jax.ShapeDtypeStruct((count, D), jnp.float32),
            jax.ShapeDtypeStruct(shape, jnp.bfloat16),
        ],
        grid=(TILES,),
        in_specs=[
            resident,
            resident,
            pl.BlockSpec((1, D, D), lambda i: (4 + i, 0, 0)),
            pl.BlockSpec((TILES, D // TILES, D), lambda i: (2, i, 0)),
        ],
        out_specs=[resident, resident, pl.BlockSpec(shape, lambda i: (0, 0, 0, 0, 0))],
        scratch_shapes=[pltpu.VMEM((D, D), jnp.bfloat16)],
        compiler_params=pltpu.CompilerParams(vmem_limit_bytes=48 * MIB),
        cost_estimate=pl.CostEstimate(
            flops=12 * count * D * FF, bytes_accessed=8 * D * FF, transcendentals=0
        ),
    )(rows, branch, weights, weights)


def body(
    visual_in,
    question_in,
    segment_ids,
    regions,
    rel_index,
    rel_table,
    window_project,
    window_output,
    causal_project,
    causal_output,
    reader_query,
    reader_pair,
    reader_output,
    viewer_query,
    viewer_pair,
    viewer_output,
    visual_up,
    visual_down,
    question_up,
    question_down,
    norm_gains,
    norm_shifts,
    visual_cot,
    question_cot,
):
    blocks = lax.axis_size("blk")
    ringed = blocks == 8
    share = Q_LEN // blocks
    rows = visual_in.shape[0]
    far, core, blk = lax.axis_index("far"), lax.axis_index("core"), lax.axis_index("blk")
    asks = far == 0
    seat = ring_seat(blk, blocks)
    early = -(-(LONGEST - 1) // share)
    reach = min(Q_LEN, share * (early + 1))
    span = reach + rows - share
    first = jnp.clip((seat - early) * share, 0, Q_LEN - reach)
    inset = jnp.where(asks, seat * share - first, 0)
    role = jnp.stack([far, inset]).astype(jnp.int32)
    cut = D // (4 * blocks)

    def own_of(question_side, visual_side):
        return jnp.where(asks, question_side, visual_side)

    class Trade(Once):
        def __init__(self, question_side, visual_side):
            self.kept = own_of(question_side, visual_side)
            self.away = own_of(visual_side, question_side)

        def send(self):
            return swap_far(self.away)

        def receive(self, got):
            self.found = jnp.stack([own_of(self.kept, got), own_of(got, self.kept)])

    def pad_rows(values, total):
        return jnp.pad(values, ((0, total - values.shape[0]),) + ((0, 0),) * (values.ndim - 1))

    def block_of(flat, columns):
        return flat.reshape(-1, columns)

    def cross_squares(query, pair, out):
        pair = pair.reshape(cut, 2, D).transpose(1, 0, 2)
        return jnp.concatenate([query.reshape(1, cut, D), pair, out.reshape(1, cut, D)])

    def mlp_squares(up, down):
        up = up.reshape(cut, TILES, D).transpose(1, 0, 2)
        return jnp.concatenate([up, down.reshape(TILES, cut, D)])

    def matrices(ring, splits):
        if ringed:
            other = {key: swap_core(item) for key, item in ring.pieces.items()}
            return assemble(ring.pieces, other, splits, core, seat, blocks)
        here = lax.all_gather(ring, "blk", axis=0)
        there = swap_core(here)
        pair = jnp.where(core == 0, jnp.stack([here, there]), jnp.stack([there, here]))
        whole = pair.transpose(2, 0, 1, 3, 4).reshape(4 * blocks * ring.shape[1], -1)
        places = [sum(splits[:i]) for i in range(len(splits))]
        return [whole[:, at : at + width] for at, width in zip(places, splits)]

    def ring_of(own):
        return Gather(own, blocks) if ringed else own

    def step(rings, transfers=(), work=()):
        return phase((list(rings) if ringed else []) + list(transfers), work)

    norms = jnp.pad(jnp.concatenate([norm_gains, norm_shifts]), (0, cut * LANES - 2 * norm_gains.size))
    norms = norms.reshape(cut, LANES)
    self_shards = Trade(
        jnp.concatenate([block_of(causal_project, 3 * D), block_of(causal_output, D), norms], 1),
        jnp.concatenate([block_of(window_project, 3 * D), block_of(window_output, D), norms], 1),
    )
    phase([self_shards])
    self_ring = ring_of(self_shards.found)
    later_shards = Trade(
        jnp.concatenate(
            [
                cross_squares(reader_query, reader_pair, reader_output),
                mlp_squares(question_up, question_down),
            ]
        ),
        jnp.concatenate(
            [
                cross_squares(viewer_query, viewer_pair, viewer_output),
                mlp_squares(visual_up, visual_down),
            ]
        ),
    )
    step([self_ring], [later_shards])
    row_shards = Trade(
        pad_rows(lax.dynamic_slice_in_dim(question_in, first, reach, 0), span),
        pad_rows(visual_in, span),
    )
    marks = Trade(segment_ids[0], jnp.pad(regions, (0, Q_LEN - rows)))
    cot = Trade(
        pad_rows(lax.dynamic_slice_in_dim(question_cot, seat * share, share, 0), rows), visual_cot
    )
    later = step([self_ring], [], later_shards.found)
    later = later.transpose(1, 0, 2, 3).reshape(-1, cut, D)
    later = lax.all_gather(later, ("core", "blk"), axis=1, tiled=True).reshape(-1, D, D)
    bias = window_bias(role, rel_table, rel_index)
    bias = step([self_ring], [], bias)
    step([self_ring], [row_shards, marks])
    slots, marks = row_shards.found, marks.found
    key_marks = own_of(
        jnp.pad(
            lax.dynamic_slice_in_dim(marks, first, reach, 1),
            ((0, 0), (0, span - reach)),
            constant_values=-2,
        ),
        marks[:, :span],
    )[:, None, :]
    row_marks = own_of(
        jnp.pad(
            lax.dynamic_slice_in_dim(marks, seat * share, share, 1),
            ((0, 0), (0, rows - share)),
            constant_values=-1,
        ),
        marks[:, :rows],
    )[:, :, None]
    self_weights = matrices(self_ring, (D, D, D, D, LANES))
    self_query_weight, self_key_weight, self_value_weight, self_exit, norm_rows = self_weights
    norm_flat = norm_rows.reshape(4 * blocks, -1)[:, : 2 * norm_gains.size].astype(jnp.float32)
    gains = norm_flat[:, : norm_gains.size].reshape(6, D)
    shifts = norm_flat[:, norm_gains.size :].reshape(6, D)

    own = lax.dynamic_slice_in_dim(slots, inset, rows, 1).astype(jnp.float32)
    self_gain, self_shift = own_of(gains[1], gains[0]), own_of(shifts[1], shifts[0])
    self_norm, self_pull = jax.vjp(normalize, own, self_gain, self_shift)
    self_low = low(self_norm).reshape(2 * rows, D)
    every_low = low(normalize(slots.astype(jnp.float32), self_gain, self_shift))
    every_low = every_low.reshape(2 * span, D)
    self_query = low(product(self_low, self_query_weight)).reshape(2, rows, D)
    self_keys = low(product(every_low, self_key_weight)).reshape(2, span, D)
    self_values = low(product(every_low, self_value_weight)).reshape(2, span, D)
    self_attn, self_logs = self_forward(
        role, self_query, self_keys, self_values, bias, row_marks, key_marks
    )
    self_attn = self_attn.reshape(2 * rows, D)
    rows_one = own + product(self_attn, self_exit).reshape(2, rows, D)

    cross_gain, cross_shift = own_of(gains[2], gains[3]), own_of(shifts[2], shifts[3])
    cross_norm, cross_pull = jax.vjp(normalize, rows_one, cross_gain, cross_shift)
    cross_low = low(cross_norm)
    sent = Once(lambda: swap_far(cross_low))
    phase([sent])
    cross_weights = lax.optimization_barrier([later[i] for i in range(4)])
    cross_query_weight, cross_key_weight, cross_value_weight, cross_exit = cross_weights
    cross_query = low(product(cross_low.reshape(2 * rows, D), cross_query_weight))
    cross_query = cross_query.reshape(2, rows, D)
    source_ring = ring_of(sent.found)
    if ringed:
        for number in range(4):
            phase([source_ring] + ([cot] if number == 0 else []))
        pieces = [source_ring.pieces[k] for k in OFFSETS[:-1]]
        pieces.append(jnp.concatenate([source_ring.pieces["first"], source_ring.pieces["second"]]))
        sources = jnp.concatenate(pieces, axis=1)
    else:
        phase([cot])
        sources = lax.all_gather(sent.found, "blk", axis=1, tiled=True)
    sources = sources.reshape(-1, D)
    cot = cot.found
    column = jnp.arange(blocks * rows) % rows
    cross_extra = own_of(0.0, jnp.where(column < share, 0.0, NEG))[None]
    cross_keys = low(product(sources, cross_key_weight)).reshape(2, -1, D)
    cross_values = low(product(sources, cross_value_weight)).reshape(2, -1, D)
    cross_attn, cross_logs = cross_forward(cross_query, cross_keys, cross_values, cross_extra)
    cross_attn = cross_attn.reshape(2 * rows, D)
    rows_two = rows_one + product(cross_attn, cross_exit).reshape(2, rows, D)

    mlp_gain, mlp_shift = own_of(gains[5], gains[4]), own_of(shifts[5], shifts[4])
    mlp_norm, mlp_pull = jax.vjp(normalize, rows_two, mlp_gain, mlp_shift)
    mlp_low = low(mlp_norm).reshape(2 * rows, D)
    mlp_out, back_mlp, mlp_delta = mlp(mlp_low, cot.reshape(2 * rows, D), later, blocks)
    rows_three = rows_two + mlp_out.reshape(2, rows, D)
    back_mlp_in, gain_mlp, shift_mlp = mlp_pull(back_mlp.reshape(2, rows, D))
    back_two = cot.astype(jnp.float32) + back_mlp_in
    mlp_delta = mlp_delta.reshape(2 * blocks, -1, D)
    mlp_delta = lax.psum_scatter(mlp_delta, ("core", "blk"), scatter_dimension=0, tiled=True)

    class Owners(Once):
        def __init__(self, total):
            self.total = total

        def send(self):
            return swap_far(low(own_of(self.total[1], self.total[0])))

        def receive(self, came):
            mine = own_of(self.total[0], self.total[1]).astype(jnp.float32)
            came = came.astype(jnp.float32)
            self.found = own_of(mine, came), own_of(came, mine)

    class Home(Once):
        def __init__(self, values):
            self.values = values

        def send(self):
            return swap_far(own_of(self.values[1], self.values[0]))

        def receive(self, got):
            kept = own_of(self.values[0], self.values[1])
            self.found = own_of(kept, got)[:share], own_of(got, kept)

    home_out = Home(low(rows_three))

    def by_owner(parts):
        whole = jnp.stack([part.reshape(2, -1, D) for part in parts], 1)
        return whole.reshape(2, 4, -1, D).transpose(2, 1, 0, 3).reshape(2 * blocks * cut, 8, D)

    cross_branch = low(back_two).reshape(2 * rows, D)
    back_attn = low(times_transposed(cross_branch, cross_exit)).reshape(2, rows, D)
    back_query, back_keys, back_values = cross_backward(
        cross_query, cross_keys, cross_values, cross_extra, cross_logs, back_attn
    )
    back_query = back_query.reshape(2 * rows, D)
    back_keys, back_values = back_keys.reshape(-1, D), back_values.reshape(-1, D)
    back_sources = times_transposed(back_keys, cross_key_weight)
    back_sources = back_sources + times_transposed(back_values, cross_value_weight)
    back_sources = back_sources.reshape(2, -1, D)
    if ringed:

        def source_chunk(k):
            at = OFFSETS.index(k) * rows
            return back_sources[:, at : at + rows]

        back_sent = Sum(source_chunk, blocks)
        delta_cross_exit = low(transposed_times(cross_attn, cross_branch))
        delta_cross_query = low(transposed_times(cross_low.reshape(2 * rows, D), back_query))
        back_cross = times_transposed(back_query, cross_query_weight).reshape(2, rows, D)
        works = [
            (delta_cross_exit, delta_cross_query, back_cross),
            low(transposed_times(sources, back_keys)),
            low(transposed_times(sources, back_values)),
            (),
        ]
        extra = [[home_out], [], [], []]
        works = [phase([back_sent] + more, work) for work, more in zip(works, extra)]
        delta_cross_exit, delta_cross_query, back_cross = works[0]
        delta_cross_keys, delta_cross_values = works[1:3]
        back_sent = back_sent.total
    else:
        back_sent = lax.psum_scatter(back_sources, "blk", scatter_dimension=1, tiled=True)
        phase([home_out])
        delta_cross_exit = low(transposed_times(cross_attn, cross_branch))
        delta_cross_query = low(transposed_times(cross_low.reshape(2 * rows, D), back_query))
        back_cross = times_transposed(back_query, cross_query_weight).reshape(2, rows, D)
        delta_cross_keys = low(transposed_times(sources, back_keys))
        delta_cross_values = low(transposed_times(sources, back_values))
    returned = Once(lambda: swap_far(low(back_sent)))
    cross_delta = by_owner(
        [delta_cross_query, delta_cross_keys, delta_cross_values, delta_cross_exit]
    )
    cross_delta, mlp_delta = phase([returned], (cross_delta, mlp_delta))
    cross_delta = lax.psum_scatter(cross_delta, ("core", "blk"), scatter_dimension=0, tiled=True)
    back_cross = back_cross + returned.found.astype(jnp.float32)
    back_cross_in, gain_cross, shift_cross = cross_pull(back_cross)
    back_one = back_two + back_cross_in

    self_branch = low(back_one).reshape(2 * rows, D)
    back_attn = low(times_transposed(self_branch, self_exit)).reshape(2, rows, D)
    back_query, back_keys, back_values, back_scores = self_backward(
        role, self_query, self_keys, self_values, bias, row_marks, key_marks, self_logs, back_attn
    )
    back_query = back_query.reshape(2 * rows, D)
    back_keys, back_values = back_keys.reshape(2 * span, D), back_values.reshape(2 * span, D)
    back_every = times_transposed(back_keys, self_key_weight)
    back_every = back_every + times_transposed(back_values, self_value_weight)
    back_every = back_every.reshape(2, span, D)
    back_self = times_transposed(back_query, self_query_weight).reshape(2, rows, D)

    def for_earlier(j):
        at = jnp.maximum(inset - j * share, 0)
        found = lax.dynamic_slice_in_dim(back_every, at, share, 1)
        return jnp.where(asks & (seat >= j), found, 0.0)

    order = ring_order(blocks)
    earlier_hop = [(order[i], order[i - 1]) for i in range(1, blocks)]

    class Chain:
        def __init__(self):
            self.left, self.state = early, low(for_earlier(early))

        def send(self):
            return lax.ppermute(self.state, "blk", earlier_hop)

        def receive(self, found):
            self.left -= 1
            self.total = found.astype(jnp.float32) + for_earlier(self.left)
            self.state = low(self.total)

    chain = Chain()
    chain.state, back_query, back_keys, back_values = lax.optimization_barrier(
        (chain.state, back_query, back_keys, back_values)
    )
    self_parts = [
        low(transposed_times(self_low, back_query)),
        low(transposed_times(every_low, back_keys)),
        low(transposed_times(every_low, back_values)),
        low(transposed_times(self_attn, self_branch)),
    ]
    question_rows, visual_out = home_out.found
    out_ring = Circle(question_rows, blocks)
    outs = [out_ring] if ringed else []
    self_delta = jnp.stack(self_parts).reshape(4, 2, 2, blocks, cut, D)
    self_delta = phase([chain] + outs, self_delta)
    self_other = Once(
        lambda: swap_core(lax.dynamic_index_in_dim(self_delta, 1 - core, 2, keepdims=False))
    )
    table_part = table_sums(role, back_scores, rel_index)
    table_part = phase([chain, self_other] + outs, table_part)
    self_other = self_other.found
    if ringed:

        def self_chunk(k):
            place = ring_place(seat + k, blocks)
            mine = lax.dynamic_slice(
                self_delta, (0, 0, core, place, 0, 0), (4, 2, 1, 1, cut, D)
            ).reshape(4, 2, cut, D)
            theirs = lax.dynamic_index_in_dim(self_other, place, 2, keepdims=False)
            return mine.astype(jnp.float32) + theirs.astype(jnp.float32)

        self_sum = Sum(self_chunk, blocks)
        sums = [self_sum]
    else:
        kept = lax.dynamic_index_in_dim(self_delta, core, 2, keepdims=False)
        kept = kept.astype(jnp.float32) + self_other.astype(jnp.float32)
        self_total = lax.psum_scatter(kept, "blk", scatter_dimension=2, tiled=True)[:, :, 0]
        sums = []
    mlp_sums = Owners(mlp_delta.reshape(2 * TILES, 2, cut, D).transpose(1, 0, 2, 3))
    for number in range(early - 2):
        phase([chain] + outs + (sums if number < 2 else []))
    back_self = back_self + own_of(
        jnp.pad(chain.total, ((0, 0), (0, rows - share), (0, 0))), back_every[:, :rows]
    )
    back_self_in, gain_self, shift_self = self_pull(back_self)
    back_in = back_one + back_self_in

    blank = jnp.zeros((D,), jnp.float32)
    gain_delta = [
        own_of(blank, gain_self),
        own_of(gain_self, blank),
        own_of(gain_cross, blank),
        own_of(blank, gain_cross),
        own_of(blank, gain_mlp),
        own_of(gain_mlp, blank),
    ]
    shift_delta = [
        own_of(blank, shift_self),
        own_of(shift_self, blank),
        own_of(shift_cross, blank),
        own_of(blank, shift_cross),
        own_of(blank, shift_mlp),
        own_of(shift_mlp, blank),
    ]
    small = jnp.concatenate(gain_delta + shift_delta + [table_part.reshape(-1)])
    size = small.size
    small = jnp.pad(small, (0, LANES * LANES - size)).reshape(LANES, LANES)

    class Everywhere:
        def __init__(self, total):
            self.total, self.bit = total, 0
            self.bits = [("core", 1, 2), ("far", 1, 2)]
            self.bits += [("blk", 1 << i, blocks) for i in range(blocks.bit_length() - 1)]

        def send(self):
            axis, bit, count = self.bits[self.bit]
            return lax.ppermute(self.total, axis, [(i, i ^ bit) for i in range(count)])

        def receive(self, found):
            self.total, self.bit = self.total + found, self.bit + 1

    small = Everywhere(small)
    home_back = Home(low(back_in))
    cross_delta = phase([home_back, mlp_sums] + outs + sums, cross_delta)
    cross_sums = Owners(cross_delta.reshape(cut, 4, 2, D).transpose(2, 1, 0, 3))
    question_back, visual_back = home_back.found
    if ringed:
        back_ring = Gather(question_back, blocks)
        phase([back_ring, small] + outs + sums)
        self_total = self_sum.total
    self_sums = Owners(self_total.transpose(1, 0, 2, 3))
    if ringed:
        for number in range(3):
            more = (outs if out_ring.left else []) + [[], [cross_sums], [self_sums]][number]
            phase([back_ring, small] + more)
        found = [(k, 0, back_ring.pieces[k]) for k in OFFSETS[:-1]]
        found += [(4, 0, back_ring.pieces["first"]), (4, share // 2, back_ring.pieces["second"])]
        question_delta = seats_in_order(found, seat, blocks, jnp.float32)
        found = [(-k, 0, piece) for k, piece in enumerate(out_ring.pieces)]
        question_out = seats_in_order(found, seat, blocks, jnp.bfloat16)
    else:
        both = jnp.stack([question_rows, question_back])
        both = lax.all_gather(both, "blk", axis=0)
        both = jnp.concatenate([both[i] for i in ring_order(blocks)], 1)
        question_out, question_delta = both[0], both[1].astype(jnp.float32)
        phase([cross_sums, self_sums])
    while small.bit < len(small.bits):
        phase([small])
    small = small.total.reshape(-1)
    at = ((2 * far + core) * blocks + blk) * norm_gains.size
    delta_gains = lax.dynamic_slice_in_dim(small, at, norm_gains.size, 0)
    delta_shifts = lax.dynamic_slice_in_dim(small, 6 * D + at, norm_gains.size, 0)
    table_delta = small[12 * D : size].reshape(HEADS, RELS)
    question_shift = small[11 * D : 12 * D]

    def joined(side, start, stop):
        return side[start:stop].transpose(1, 0, 2).reshape(-1)

    causal, window = [[joined(side, 0, 3), joined(side, 3, 4)] for side in self_sums.found]
    reader, viewer = [
        [joined(side, 0, 1), joined(side, 1, 3), joined(side, 3, 4)] for side in cross_sums.found
    ]
    question_mlp, visual_mlp = [
        [joined(side, 0, TILES), side[TILES:].reshape(-1)] for side in mlp_sums.found
    ]
    return (
        visual_out,
        question_out,
        visual_back.astype(jnp.float32),
        question_delta,
        table_delta,
        window[0],
        window[1],
        causal[0],
        causal[1],
        reader[0],
        reader[1],
        reader[2],
        viewer[0],
        viewer[1],
        viewer[2],
        visual_mlp[0],
        visual_mlp[1],
        question_mlp[0],
        question_mlp[1],
        delta_gains,
        delta_shifts,
        question_shift,
    )


def solution(mesh):
    pages, blocks = mesh.devices.shape
    cut = jax.sharding.Mesh(
        mesh.devices.reshape(2, pages // 2, blocks), ("far", "core", "blk")
    )
    flat, whole, by_page = P(("far", "core", "blk")), P(), P(("far", "core"), None)
    split = P(("far", "core", "blk"), None)
    in_specs = (split, by_page, by_page, flat, whole, whole) + (flat,) * 16 + (split, by_page)
    out_specs = (split, by_page, split, by_page, whole) + (flat,) * 16 + (whole,)
    return jax.shard_map(body, mesh=cut, in_specs=in_specs, out_specs=out_specs, check_vma=False)
```

time: 703 us -> 599 us (0.85)
  waiting for transfers between devices: 208 us -> 163 us
  starting transfers between devices: 162 us -> 134 us
  matrix products: 73.3 us -> 53.8 us
  Pallas kernels: 114 us -> 97.1 us
  between operations: 3.98 us -> 16.8 us
    ppermute x182 -> x78, waiting for transfers between devices: 208 us -> 161 us  [the longest x20 73.5 us: send(): lax.ppermute(one, 'blk', self.hops[0])]
    ppermute x182 -> x78, starting transfers between devices: 162 us -> 133 us  [the longest x12 56.7 us: swap_far(): return lax.ppermute(values, 'far', [(0, 1), (1, 0)])]
    pallas_call x6 -> x5, Pallas kernels: 43.1 us -> 62.1 us  [the longest x1 24.8 us: cross_backward(): pl.pallas_call(cross_backward_kernel, out_shape=[jax.ShapeDtypeStruct((2,...]
    pallas_call x1, Pallas kernels: 19.7 us -> 2.23 us  [table_sums(): pl.pallas_call(table_kernel, out_shape=jax.ShapeDtypeStruct((2 * HEADS, R...]
    dot_general x10 -> x8, matrix products: 30 us -> 17.5 us  [transposed_times(): lax.dot_general(left, right, (((0,), (0,)), ((), ())), preferred_element_...]
    pallas_call x1, Pallas kernels: 14.1 us -> 2.54 us  [window_bias(): pl.pallas_call(bias_kernel, out_shape=jax.ShapeDtypeStruct((WIN, 16, WIN)...]
    dot_general x12 -> x8, matrix products: 26.3 us -> 16.2 us  [times_transposed(): lax.dot_general(left, right, (((1,), (1,)), ((), ())), preferred_element_...]
    squeeze x11 -> x1, local copies, waits for them, and re-layouts: 9.77 us -> 1.6 us  [body(): lax.dynamic_index_in_dim(self_delta, 1 - core, 2, keepdims=False)]
  transfers between devices with their start and end apart: 182 -> 81, of which waited for: 65 -> 38; matrix products, arithmetic and copies ran while one was open for 20% -> 24% of each run, Pallas kernels for 13% -> 11%
where the time goes in v2:
time: 599 us; the launch traced here: 592 us
  waiting for transfers between devices  163 us (27%)
  starting transfers between devices  134 us (22%)
  Pallas kernels  97.1 us (16%)
  local copies, waits for them, and re-layouts  63.7 us (11%)
  other arithmetic  63.3 us (11%)
  matrix products  53.8 us (9%)
  between operations  16.8 us (3%)
    ppermute x20, waiting for transfers between devices, send(): lax.ppermute(one, 'blk', self.hops[0])  73.5 us
    ppermute x12, starting transfers between devices, swap_far(): return lax.ppermute(values, 'far', [(0, 1), (1, 0)])  56.7 us
    ppermute x20, waiting for transfers between devices, send(): lax.ppermute(two, 'blk', self.hops[1])  45.2 us
    ppermute x20, starting transfers between devices, send(): lax.ppermute(one, 'blk', self.hops[0])  32.9 us
    ppermute x12, waiting for transfers between devices, swap_far(): return lax.ppermute(values, 'far', [(0, 1), (1, 0)])  27.3 us
    convert_element_type x20, other arithmetic, low(): return values.astype(jnp.bfloat16)  25.1 us
    pallas_call x1, Pallas kernels, cross_backward(): pl.pallas_call(cross_backward_kernel, out_shape=[jax.ShapeDtypeStruct((2,...  24.8 us
    unnamed x267, local copies, waits for them, and re-layouts  20.4 us
  transfers between devices with their start and end apart: 81, of which 38 were waited for; matrix products, arithmetic and copies ran while one was open for 24% of the time, Pallas kernels for 11%

profile of v2, /device:TPU:0, one launch (start us, length us, event | category | flops | bytes accessed | tf_op | source)
XLA Modules:
  0.0 591.9 jit_solution(5460459056937538295)
XLA Ops:
  28.7 8.4 %collective-permute-done.3 = bf16[12,24,768]{2,1,0:T(8,128)(2,1)S(1)} collective-permute-done((bf16[12,24,768]{2,1,0:T(8,128)(2,1)S(1)}, bf16[12,24,768]{2,1,0:T(8,128)(2,1)S(1)}, u32[]{:S(2)}, u32[]{:S(2)}) %collective-permute-start.3) | collective-permute-done | bytes 442400 | tf_op jit(solution)/shard_map/ppermute | solution.py:82
  65.1 10.8 %collective-permute-start.11 = (s32[1024]{0:T(1024)S(1)}, s32[1024]{0:T(1024)S(1)}, u32[]{:S(2)}, u32[]{:S(2)}) collective-permute-start(s32[1024]{0:T(1024)S(1)} %pad_select_fusion.3), channel_id=1, source_target_pairs={{0,16},{16,0},{1,17},{17,1},{2,18},{18,2},{3,19},{19,3},{4,20},{20... | collective-permute-start | bytes 12296 | tf_op jit(solution)/shard_map/ppermute | solution.py:82
  102.7 10.5 %shard_map.401 = (bf16[2,144,768]{2,1,0:T(8,128)(2,1)S(1)}, f32[2,144,768]{2,1,0:T(8,128)S(1)}) custom-call(s32[2]{0:T(128)S(1)} %copy-done.28, bf16[2,144,768]{2,1,0:T(8,128)(2,1)S(1)} %bitcast.361, bf16[2,656,768]{2,1,0:T(8,128)(2,1)S(1)} %bitcast.348, bf16[2,656,768]{2,1,0:T(8,128)(2,1)S(1)} %bitcast.350, f32[12,144,144]{2,1,0:T(8,128)S(1)} %bitcast.346, ...), custom_call_target="tpu_custom_call" | custom-call | flops 1160773632 | bytes 6045696 | tf_op jit(solution)/shard_map/pallas_call | solution.py:440
  114.5 5.2 collective-permute-start.21
  120.6 9.7 %collective-permute-done.21 = bf16[2,144,768]{2,1,0:T(8,128)(2,1)S(1)} collective-permute-done((bf16[2,144,768]{2,1,0:T(8,128)(2,1)S(1)}, bf16[2,144,768]{2,1,0:T(8,128)(2,1)S(1)}, u32[]{:S(2)}, u32[]{:S(2)}) %collective-permute-start.21) | collective-permute-done | bytes 442400 | tf_op jit(solution)/shard_map/ppermute | solution.py:82
  139.2 8.7 %collective-permute-done.22 = bf16[2,144,768]{2,1,0:T(8,128)(2,1)S(1)} collective-permute-done((bf16[2,144,768]{2,1,0:T(8,128)(2,1)S(1)}, bf16[2,144,768]{2,1,0:T(8,128)(2,1)S(1)}, u32[]{:S(2)}, u32[]{:S(2)}) %collective-permute-start.22) | collective-permute-done | bytes 442400 | tf_op jit(solution)/shard_map/ppermute | solution.py:102
  147.9 11.4 %collective-permute-done.23 = bf16[2,144,768]{2,1,0:T(8,128)(2,1)S(1)} collective-permute-done((bf16[2,144,768]{2,1,0:T(8,128)(2,1)S(1)}, bf16[2,144,768]{2,1,0:T(8,128)(2,1)S(1)}, u32[]{:S(2)}, u32[]{:S(2)}) %collective-permute-start.23) | collective-permute-done | bytes 442400 | tf_op jit(solution)/shard_map/ppermute | solution.py:102
  163.8 8.7 %collective-permute-done.25 = bf16[2,144,768]{2,1,0:T(8,128)(2,1)S(1)} collective-permute-done((bf16[2,144,768]{2,1,0:T(8,128)(2,1)S(1)}, bf16[2,144,768]{2,1,0:T(8,128)(2,1)S(1)}, u32[]{:S(2)}, u32[]{:S(2)}) %collective-permute-start.25) | collective-permute-done | bytes 442400 | tf_op jit(solution)/shard_map/ppermute | solution.py:102
  179.4 6.6 %collective-permute-done.27 = bf16[2,144,768]{2,1,0:T(8,128)(2,1)S(1)} collective-permute-done((bf16[2,144,768]{2,1,0:T(8,128)(2,1)S(1)}, bf16[2,144,768]{2,1,0:T(8,128)(2,1)S(1)}, u32[]{:S(2)}, u32[]{:S(2)}) %collective-permute-start.27) | collective-permute-done | bytes 442400 | tf_op jit(solution)/shard_map/ppermute | solution.py:102
  198.5 6.6 %convolution_convert_fusion.1 = bf16[2304,768]{1,0:T(8,128)(2,1)S(1)} fusion(bf16[2304,768]{1,0:T(8,128)(2,1)} %bitcast.46, bf16[768,768]{1,0:T(8,128)(2,1)S(1)} %bitcast.420), kind=kOutput, calls=%fused_computation.2 | convolution fusion | flops 2719678464 | bytes 8257536 | tf_op jit(solution)/shard_map/dot_general | solution.py:29
  205.2 6.2 %convolution_convert_fusion = bf16[2304,768]{1,0:T(8,128)(2,1)S(1)} fusion(bf16[2304,768]{1,0:T(8,128)(2,1)} %bitcast.46, bf16[768,768]{1,0:T(8,128)(2,1)S(1)} %bitcast.418), kind=kOutput, calls=%fused_computation.1 | convolution fusion | flops 2719678464 | bytes 8257536 | tf_op jit(solution)/shard_map/dot_general | solution.py:29
  212.0 14.2 %shard_map.402 = (bf16[2,144,768]{2,1,0:T(8,128)(2,1)S(1)}, f32[2,144,768]{2,1,0:T(8,128)S(1)}) custom-call(bf16[2,144,768]{2,1,0:T(8,128)(2,1)S(1)} %bitcast.378, bf16[2,1152,768]{2,1,0:T(8,128)(2,1)S(1)} %bitcast.369, bf16[2,1152,768]{2,1,0:T(8,128)(2,1)S(1)} %bitcast.371, f32[1,1152]{1,0:T(1,128)S(1)} %broadcast_select_fusion.7.extra_ref), custom_call_target="tpu_custom_call" | custom-call | flops 4076863488 | bytes 7077888 | tf_op jit(solution)/shard_map/pallas_call | solution.py:513
  227.8 18.1 %shard_map.403 = (f32[288,768]{1,0:T(8,128)S(1)}, f32[288,768]{1,0:T(8,128)S(1)}, bf16[16,8,2,24,768]{4,3,2,1,0:T(8,128)(2,1)}) custom-call(bf16[288,768]{1,0:T(8,128)(2,1)S(1)} %bitcast.359, bf16[288,768]{1,0:T(8,128)(2,1)S(1)} %bitcast.358, bf16[12,768,768]{2,1,0:T(8,128)(2,1)} %bitcast.413, bf16[12,768,768]{2,1,0:T(8,128)(2,1)} %bitcast.414), custom_call_target="tpu_custom_call" | custom-call | flops 8153726976 | bytes 18874368 | tf_op jit(solution)/shard_map/pallas_call | solution.py:599
  257.8 24.8 %shard_map.404 = (bf16[2,144,768]{2,1,0:T(8,128)(2,1)S(1)}, bf16[2,1152,768]{2,1,0:T(8,128)(2,1)S(1)}, bf16[2,1152,768]{2,1,0:T(8,128)(2,1)S(1)}) custom-call(bf16[2,144,768]{2,1,0:T(8,128)(2,1)S(1)} %bitcast.379, bf16[2,1152,768]{2,1,0:T(8,128)(2,1)S(1)} %bitcast.370, bf16[2,1152,768]{2,1,0:T(8,128)(2,1)S(1)} %bitcast.372, ...), custom_call_target="tpu_custom_call" | custom-call | flops 10192158720 | bytes 14155776 | tf_op jit(solution)/shard_map/pallas_call | solution.py:532
  298.8 8.1 %collective-permute-done.32 = bf16[1,144,768]{2,1,0:T(8,128)(2,1)S(1)} collective-permute-done((bf16[1,144,768]{2,1,0:T(8,128)(2,1)S(1)}, bf16[1,144,768]{2,1,0:T(8,128)(2,1)S(1)}, u32[]{:S(2)}, u32[]{:S(2)}) %collective-permute-start.32) | collective-permute-done | bytes 221216 | tf_op jit(solution)/shard_map/ppermute | solution.py:135
  309.3 5.1 bitcast_convert_fusion.2
  314.3 12.1 %collective-permute-done.34 = bf16[2,144,768]{2,1,0:T(8,128)(2,1)S(1)} collective-permute-done((bf16[2,144,768]{2,1,0:T(8,128)(2,1)S(1)}, bf16[2,144,768]{2,1,0:T(8,128)(2,1)S(1)}, u32[]{:S(2)}, u32[]{:S(2)}) %collective-permute-start.34) | collective-permute-done | bytes 442400 | tf_op jit(solution)/shard_map/ppermute | solution.py:135
  326.4 5.4 collective-permute-done.35
  339.3 6.8 %collective-permute-done.36 = bf16[2,144,768]{2,1,0:T(8,128)(2,1)S(1)} collective-permute-done((bf16[2,144,768]{2,1,0:T(8,128)(2,1)S(1)}, bf16[2,144,768]{2,1,0:T(8,128)(2,1)S(1)}, u32[]{:S(2)}, u32[]{:S(2)}) %collective-permute-start.36) | collective-permute-done | bytes 442400 | tf_op jit(solution)/shard_map/ppermute | solution.py:135
  351.7 12.5 %collective-permute-done.38 = bf16[2,144,768]{2,1,0:T(8,128)(2,1)S(1)} collective-permute-done((bf16[2,144,768]{2,1,0:T(8,128)(2,1)S(1)}, bf16[2,144,768]{2,1,0:T(8,128)(2,1)S(1)}, u32[]{:S(2)}, u32[]{:S(2)}) %collective-permute-start.38) | collective-permute-done | bytes 442400 | tf_op jit(solution)/shard_map/ppermute | solution.py:135
  364.2 8.4 %collective-permute-done.39 = bf16[2,144,768]{2,1,0:T(8,128)(2,1)S(1)} collective-permute-done((bf16[2,144,768]{2,1,0:T(8,128)(2,1)S(1)}, bf16[2,144,768]{2,1,0:T(8,128)(2,1)S(1)}, u32[]{:S(2)}, u32[]{:S(2)}) %collective-permute-start.39) | collective-permute-done | bytes 442400 | tf_op jit(solution)/shard_map/ppermute | solution.py:135
  387.6 17.3 %shard_map.405 = (bf16[2,144,768]{2,1,0:T(8,128)(2,1)S(1)}, bf16[2,656,768]{2,1,0:T(8,128)(2,1)S(1)}, bf16[2,656,768]{2,1,0:T(8,128)(2,1)S(1)}, bf16[12,2,144,144]{3,2,1,0:T(8,128)(2,1)S(1)}) custom-call(s32[2]{0:T(128)S(1)} %copy-done.29, bf16[2,144,768]{2,1,0:T(8,128)(2,1)S(1)} %bitcast.362, bf16[2,656,768]{2,1,0:T(8,128)(2,1)S(1)} %bitcast.349, ...), custom_call_target="tpu_custom_call" | custom-call | flops 2901934080 | bytes 8060928 | tf_op jit(solution)/shard_map/pallas_call | solution.py:459
  475.8 23.7 %collective-permute-start.55 = (bf16[8,24,768]{2,1,0:T(8,128)(2,1)}, bf16[8,24,768]{2,1,0:T(8,128)(2,1)}, u32[]{:S(2)}, u32[]{:S(2)}) collective-permute-start(bf16[8,24,768]{2,1,0:T(8,128)(2,1)} %fusion.48), channel_id=1, source_target_pairs={{0,16},{16,0},{1,17},{17,1},{2,18},{18,2},{3,19},{19,3},{4,20},{20... | collective-permute-start | bytes 884744 | tf_op jit(solution)/shard_map/ppermute | solution.py:82
  505.8 5.3 collective-permute-start.54
  (632 shorter events, 320.5 us)
Async XLA Ops:
  7.2 188.6 %all-gather.2.cloned.1.call-start = ((), (), s32[]{:S(2)}) async-start(), calls=%async_computation.2 | async-start | bytes 15040512 | tf_op jit(solution)/shard_map/all_gather | solution.py:741
  47.6 333.5 %reduce-scatter.5.cloned.1.call-start = ((), (), s32[]{:S(2)}) async-start(), calls=%async_computation.3 | async-start | bytes 10027008 | tf_op jit(solution)/shard_map/reduce_scatter | solution.py:820
  50.0 27.4 %collective-permute-start.10 = (bf16[656,768]{1,0:T(8,128)(2,1)}, bf16[656,768]{1,0:T(8,128)(2,1)}, u32[]{:S(2)}, u32[]{:S(2)}) collective-permute-start(bf16[656,768]{1,0:T(8,128)(2,1)} %pad_select_fusion), channel_id=1, source_target_pairs={{0,16},{16,0},{1,17},{17,1},{2,18},{18,2},{3,19},{19,3},{4,20},{20... | collective-permute-start | bytes 3022856 | tf_op jit(solution)/shard_map/ppermute | solution.py:82
  114.5 15.8 %collective-permute-start.21 = (bf16[2,144,768]{2,1,0:T(8,128)(2,1)S(1)}, bf16[2,144,768]{2,1,0:T(8,128)(2,1)S(1)}, u32[]{:S(2)}, u32[]{:S(2)}) collective-permute-start(bf16[2,144,768]{2,1,0:T(8,128)(2,1)S(1)} %add_convert_fusion.4), channel_id=1, source_target_pairs={{0,16},{16,0},{1,17},{17,1},{2,18},{18,2},{3,19},{19,3},{4,20},{20... | collective-permute-start | bytes 1327112 | tf_op jit(solution)/shard_map/ppermute | solution.py:82
  130.3 17.6 %collective-permute-start.22 = (bf16[2,144,768]{2,1,0:T(8,128)(2,1)S(1)}, bf16[2,144,768]{2,1,0:T(8,128)(2,1)S(1)}, u32[]{:S(2)}, u32[]{:S(2)}) collective-permute-start(bf16[2,144,768]{2,1,0:T(8,128)(2,1)S(1)} %collective-permute-done.21), channel_id=1, source_target_pairs={{0,2},{2,4},{4,6},{6,7},{7,5},{5,3},{3,1},{1,0},{8,10},{10,12},{12... | collective-permute-start | bytes 1327112 | tf_op jit(solution)/shard_map/ppermute | solution.py:102
  132.1 27.2 %collective-permute-start.23 = (bf16[2,144,768]{2,1,0:T(8,128)(2,1)S(1)}, bf16[2,144,768]{2,1,0:T(8,128)(2,1)S(1)}, u32[]{:S(2)}, u32[]{:S(2)}) collective-permute-start(bf16[2,144,768]{2,1,0:T(8,128)(2,1)S(1)} %collective-permute-done.21), channel_id=1, source_target_pairs={{2,0},{4,2},{6,4},{7,6},{5,7},{3,5},{1,3},{0,1},{10,8},{12,10},{14... | collective-permute-start | bytes 1327112 | tf_op jit(solution)/shard_map/ppermute | solution.py:102
  245.9 274.5 %reduce-scatter.7.cloned.1.call-start = ((), (), s32[]{:S(2)}) async-start(), calls=%async_computation.4 | async-start | bytes 5013504
  289.5 17.3 %collective-permute-start.32 = (bf16[1,144,768]{2,1,0:T(8,128)(2,1)S(1)}, bf16[1,144,768]{2,1,0:T(8,128)(2,1)S(1)}, u32[]{:S(2)}, u32[]{:S(2)}) collective-permute-start(bf16[1,144,768]{2,1,0:T(8,128)(2,1)S(1)} %get-tuple-element.181), channel_id=1, source_target_pairs={{2,0},{4,2},{6,4},{7,6},{5,7},{3,5},{1,3},{0,1},{10,8},{12,10},{14... | collective-permute-start | bytes 663560 | tf_op jit(solution)/shard_map/ppermute | solution.py:135
  307.0 19.4 %collective-permute-start.34 = (bf16[2,144,768]{2,1,0:T(8,128)(2,1)S(1)}, bf16[2,144,768]{2,1,0:T(8,128)(2,1)S(1)}, u32[]{:S(2)}, u32[]{:S(2)}) collective-permute-start(bf16[2,144,768]{2,1,0:T(8,128)(2,1)S(1)} %get-tuple-element.189), channel_id=1, source_target_pairs={{0,2},{2,4},{4,6},{6,7},{7,5},{5,3},{3,1},{1,0},{8,10},{10,12},{12... | collective-permute-start | bytes 1327112 | tf_op jit(solution)/shard_map/ppermute | solution.py:135
  308.0 23.8 %collective-permute-start.35 = (bf16[2,144,768]{2,1,0:T(8,128)(2,1)S(1)}, bf16[2,144,768]{2,1,0:T(8,128)(2,1)S(1)}, u32[]{:S(2)}, u32[]{:S(2)}) collective-permute-start(bf16[2,144,768]{2,1,0:T(8,128)(2,1)S(1)} %get-tuple-element.190), channel_id=1, source_target_pairs={{2,0},{4,2},{6,4},{7,6},{5,7},{3,5},{1,3},{0,1},{10,8},{12,10},{14... | collective-permute-start | bytes 1327112 | tf_op jit(solution)/shard_map/ppermute | solution.py:135
  346.3 17.9 %collective-permute-start.38 = (bf16[2,144,768]{2,1,0:T(8,128)(2,1)S(1)}, bf16[2,144,768]{2,1,0:T(8,128)(2,1)S(1)}, u32[]{:S(2)}, u32[]{:S(2)}) collective-permute-start(bf16[2,144,768]{2,1,0:T(8,128)(2,1)S(1)} %get-tuple-element.197), channel_id=1, source_target_pairs={{0,2},{2,4},{4,6},{6,7},{7,5},{5,3},{3,1},{1,0},{8,10},{10,12},{12... | collective-permute-start | bytes 1327112 | tf_op jit(solution)/shard_map/ppermute | solution.py:135
  346.4 26.2 %collective-permute-start.39 = (bf16[2,144,768]{2,1,0:T(8,128)(2,1)S(1)}, bf16[2,144,768]{2,1,0:T(8,128)(2,1)S(1)}, u32[]{:S(2)}, u32[]{:S(2)}) collective-permute-start(bf16[2,144,768]{2,1,0:T(8,128)(2,1)S(1)} %get-tuple-element.198), channel_id=1, source_target_pairs={{2,0},{4,2},{6,4},{7,6},{5,7},{3,5},{1,3},{0,1},{10,8},{12,10},{14... | collective-permute-start | bytes 1327112 | tf_op jit(solution)/shard_map/ppermute | solution.py:135
  374.3 42.5 %collective-permute-start.42 = (bf16[128,768]{1,0:T(8,128)(2,1)S(1)}, bf16[128,768]{1,0:T(8,128)(2,1)S(1)}, u32[]{:S(2)}, u32[]{:S(2)}) collective-permute-start(bf16[128,768]{1,0:T(8,128)(2,1)S(1)} %slice_select_fusion.3.refs_0_), channel_id=1, source_target_pairs={{0,2},{2,4},{4,6},{6,7},{7,5},{5,3},{3,1},{1,0},{8,10},{10,12},{12... | collective-permute-start | bytes 589832 | tf_op jit(solution)/shard_map/ppermute | solution.py:118
  421.4 19.3 %collective-permute-start.44 = (bf16[4,2,8,24,768]{4,3,0,1,2:T(8,128)(2,1)}, bf16[4,2,8,24,768]{4,3,0,1,2:T(8,128)(2,1)}, u32[]{:S(2)}, u32[]{:S(2)}) collective-permute-start(bf16[4,2,8,24,768]{4,3,0,1,2:T(8,128)(2,1)} %dynamic-slice_bitcast_fusion), channel_id=1, source_target_pairs={{0,8},{8,0},{1,9},{9,1},{2,10},{10,2},{3,11},{11,3},{4,12},{12,4},... | collective-permute-start | bytes 7077896 | tf_op jit(solution)/shard_map/ppermute | solution.py:86
  442.1 17.2 %collective-permute-start.46 = (bf16[2,128,768]{2,1,0:T(8,128)(2,1)S(1)}, bf16[2,128,768]{2,1,0:T(8,128)(2,1)S(1)}, u32[]{:S(2)}, u32[]{:S(2)}) collective-permute-start(bf16[2,128,768]{2,1,0:T(8,128)(2,1)S(1)} %add_convert_fusion.6), channel_id=1, source_target_pairs={{2,0},{4,2},{6,4},{7,6},{5,7},{3,5},{1,3},{10,8},{12,10},{14,12},{... | collective-permute-start | bytes 1179656 | tf_op jit(solution)/shard_map/ppermute | solution.py:925
  443.4 15.9 %collective-permute-start.47 = (bf16[128,768]{1,0:T(8,128)(2,1)}, bf16[128,768]{1,0:T(8,128)(2,1)S(1)}, u32[]{:S(2)}, u32[]{:S(2)}) collective-permute-start(bf16[128,768]{1,0:T(8,128)(2,1)} %collective-permute-done.45.refs_2_), channel_id=1, source_target_pairs={{0,2},{2,4},{4,6},{6,7},{7,5},{5,3},{3,1},{1,0},{8,10},{10,12},{12... | collective-permute-start | bytes 589832 | tf_op jit(solution)/shard_map/ppermute | solution.py:118
  461.5 39.0 %collective-permute-start.50 = (bf16[2,128,768]{2,1,0:T(8,128)(2,1)}, bf16[2,128,768]{2,1,0:T(8,128)(2,1)}, u32[]{:S(2)}, u32[]{:S(2)}) collective-permute-start(bf16[2,128,768]{2,1,0:T(8,128)(2,1)} %add_convert_fusion.5), channel_id=1, source_target_pairs={{2,0},{4,2},{6,4},{7,6},{5,7},{3,5},{1,3},{10,8},{12,10},{14,12},{... | collective-permute-start | bytes 1179656 | tf_op jit(solution)/shard_map/ppermute | solution.py:925
  465.0 35.5 %collective-permute-start.52 = (bf16[4,2,24,768]{3,2,0,1:T(8,128)(2,1)}, bf16[4,2,24,768]{3,2,0,1:T(8,128)(2,1)S(1)}, u32[]{:S(2)}, u32[]{:S(2)}) collective-permute-start(bf16[4,2,24,768]{3,2,0,1:T(8,128)(2,1)} %get-tuple-element.227), channel_id=1, source_target_pairs={{0,2},{2,4},{4,6},{6,7},{7,5},{5,3},{3,1},{1,0},{8,10},{10,12},{12... | collective-permute-start | bytes 884744 | tf_op jit(solution)/shard_map/ppermute | solution.py:135
  468.8 31.7 %collective-permute-start.53 = (bf16[4,2,24,768]{3,2,0,1:T(8,128)(2,1)}, bf16[4,2,24,768]{3,2,0,1:T(8,128)(2,1)}, u32[]{:S(2)}, u32[]{:S(2)}) collective-permute-start(bf16[4,2,24,768]{3,2,0,1:T(8,128)(2,1)} %get-tuple-element.228), channel_id=1, source_target_pairs={{2,0},{4,2},{6,4},{7,6},{5,7},{3,5},{1,3},{0,1},{10,8},{12,10},{14... | collective-permute-start | bytes 884744 | tf_op jit(solution)/shard_map/ppermute | solution.py:135
  474.0 26.5 %collective-permute-start.51 = (bf16[128,768]{1,0:T(8,128)(2,1)S(1)}, bf16[128,768]{1,0:T(8,128)(2,1)S(1)}, u32[]{:S(2)}, u32[]{:S(2)}) collective-permute-start(bf16[128,768]{1,0:T(8,128)(2,1)S(1)} %collective-permute-done.47.refs_3_), channel_id=1, source_target_pairs={{0,2},{2,4},{4,6},{6,7},{7,5},{5,3},{3,1},{1,0},{8,10},{10,12},{12... | collective-permute-start | bytes 589832 | tf_op jit(solution)/shard_map/ppermute | solution.py:118
  475.8 45.6 %collective-permute-start.55 = (bf16[8,24,768]{2,1,0:T(8,128)(2,1)}, bf16[8,24,768]{2,1,0:T(8,128)(2,1)}, u32[]{:S(2)}, u32[]{:S(2)}) collective-permute-start(bf16[8,24,768]{2,1,0:T(8,128)(2,1)} %fusion.48), channel_id=1, source_target_pairs={{0,16},{16,0},{1,17},{17,1},{2,18},{18,2},{3,19},{19,3},{4,20},{20... | collective-permute-start | bytes 884744 | tf_op jit(solution)/shard_map/ppermute | solution.py:82
  505.8 15.8 %collective-permute-start.54 = (bf16[144,768]{1,0:T(8,128)(2,1)}, bf16[144,768]{1,0:T(8,128)(2,1)S(1)}, u32[]{:S(2)}, u32[]{:S(2)}) collective-permute-start(bf16[144,768]{1,0:T(8,128)(2,1)} %select_bitcast_fusion.3), channel_id=1, source_target_pairs={{0,16},{16,0},{1,17},{17,1},{2,18},{18,2},{3,19},{19,3},{4,20},{20... | collective-permute-start | bytes 663560 | tf_op jit(solution)/shard_map/ppermute | solution.py:82
  521.5 19.0 %collective-permute-start.61 = (f32[128,128]{1,0:T(8,128)}, f32[128,128]{1,0:T(8,128)}, u32[]{:S(2)}, u32[]{:S(2)}) collective-permute-start(f32[128,128]{1,0:T(8,128)} %pad_bitcast_fusion), channel_id=1, source_target_pairs={{0,8},{8,0},{1,9},{9,1},{2,10},{10,2},{3,11},{11,3},{4,12},{12,4},... | collective-permute-start | bytes 196616 | tf_op jit(solution)/shard_map/ppermute | solution.py:1008
  541.4 24.3 %collective-permute-start.72 = (bf16[4,24,768]{2,1,0:T(8,128)(2,1)S(1)}, bf16[4,24,768]{2,1,0:T(8,128)(2,1)S(1)}, u32[]{:S(2)}, u32[]{:S(2)}) collective-permute-start(bf16[4,24,768]{2,1,0:T(8,128)(2,1)S(1)} %fusion.51), channel_id=1, source_target_pairs={{0,16},{16,0},{1,17},{17,1},{2,18},{18,2},{3,19},{19,3},{4,20},{20... | collective-permute-start | bytes 442376 | tf_op jit(solution)/shard_map/ppermute | solution.py:82
  (185 other events, 1743.3 us)
Sparse Core Ops, SparseCore 0:
  47.7 121.2 all-gather.1
  246.1 132.8 reduce-scatter.4
  424.3 96.0 reduce-scatter.6

commit v3 on v2

--- a/solution.py
+++ b/solution.py
@@ -17,7 +17,7 @@
 LONGEST = Q_LEN // 2
 LANES = 128
 PAIRS = D // LANES
-RELS_PAD = 640
+RELS_PAD = 544
 
 EPS = 1e-05
 NEG = -1000000000.0
@@ -89,50 +89,35 @@
 OFFSETS = (0, -1, 1, -2, 2, -3, 3, 4)
 
 
-class Gather:
-    def __init__(self, own, blocks):
-        self.hops = forward_hop(blocks), backward_hop(blocks)
+class Ring:
+    state = None
+    within = None
+
+
+class Gather(Ring):
+    def __init__(self, own):
         self.half = own.shape[0] // 2
         self.pieces, self.step, self.state = {0: own}, 0, (own, own)
-
-    def send(self):
-        one, two = self.state
-        if self.step == 3:
-            one, two = one[: self.half], two[self.half :]
-        return lax.ppermute(one, "blk", self.hops[0]), lax.ppermute(two, "blk", self.hops[1])
+        self.places = {0: (own, 0)}
 
     def receive(self, found):
-        self.step, self.state = self.step + 1, found
+        self.step += 1
         if self.step == 4:
             self.pieces["first"], self.pieces["second"] = found
+            self.places["first"], self.places["second"] = self.within
         else:
             self.pieces[-self.step], self.pieces[self.step] = found
-
-
-class Circle:
-    def __init__(self, own, blocks):
-        self.hops, self.left = forward_hop(blocks), blocks - 1
-        self.pieces = [own]
-
-    def send(self):
-        return lax.ppermute(self.pieces[-1], "blk", self.hops)
-
-    def receive(self, found):
-        self.pieces.append(found)
-        self.left -= 1
-
-
-class Sum:
-    def __init__(self, chunk, blocks):
-        self.hops = forward_hop(blocks), backward_hop(blocks)
+            self.places[-self.step], self.places[self.step] = self.within
+            one, two = found
+            self.state = (one[: self.half], two[self.half :]) if self.step == 3 else found
+
+
+class Sum(Ring):
+    def __init__(self, chunk):
         self.chunk, self.step = chunk, 0
         most = chunk(4)
         half = most.shape[0] // 2
-        self.state = lax.optimization_barrier((low(most[:half]), low(most[half:])))
-
-    def send(self):
-        one, two = self.state
-        return lax.ppermute(one, "blk", self.hops[0]), lax.ppermute(two, "blk", self.hops[1])
+        self.state = low(most[:half]), low(most[half:])
 
     def receive(self, found):
         one, two = [item.astype(jnp.float32) for item in found]
@@ -145,7 +130,6 @@
             self.total = self.chunk(0) + one + two
         else:
             self.state = low(self.chunk(left) + one), low(self.chunk(-left) + two)
-            self.state = lax.optimization_barrier(self.state)
 
 
 class Once:
@@ -157,10 +141,30 @@
 
 
 def phase(transfers, work=()):
-    found = [item.send() for item in transfers]
-    found, work = lax.optimization_barrier((found, work))
-    for item, one in zip(transfers, found):
+    rings = [item for item in transfers if isinstance(item, Ring)]
+    others = [item for item in transfers if not isinstance(item, Ring)]
+    states = lax.optimization_barrier([item.state for item in rings])
+    both = []
+    if rings:
+        blocks = lax.axis_size("blk")
+        for side, hop in ((0, forward_hop(blocks)), (1, backward_hop(blocks))):
+            parts = [state[side] for state in states]
+            both.append(
+                lax.ppermute(parts[0] if len(parts) == 1 else jnp.concatenate(parts), "blk", hop)
+            )
+    found = [item.send() for item in others]
+    both, found, work = lax.optimization_barrier((both, found, work))
+    for item, one in zip(others, found):
         item.receive(one)
+    starts = [0, 0]
+    for item, state in zip(rings, states):
+        pieces = []
+        item.within = [(both[side], starts[side]) for side in (0, 1)]
+        for side in (0, 1):
+            size = state[side].shape[0]
+            pieces.append(both[side][starts[side] : starts[side] + size])
+            starts[side] += size
+        item.receive(tuple(pieces) if len(rings) > 1 else tuple(both))
     return work
 
 
@@ -214,17 +218,20 @@
 
 def place_kernel(plan, where_ref, *refs):
     pieces, out = refs[:-1], refs[-1]
-    for piece, (index, first, last) in zip(pieces, plan):
-        out[where_ref[index], first:last] = piece[...].astype(out.dtype)
-
-
-def seats_in_order(found, seat, blocks, dtype):
-    columns = found[0][2].shape[1]
-    rows = max(piece.shape[0] for unused, also, piece in found)
-    where = [lax.rem(seat + offset + blocks, blocks) for offset, unused, also in found]
+    for piece, (index, start, first, last) in zip(pieces, plan):
+        found = piece[start : start + last - first]
+        out[where_ref[index], first:last] = found.astype(out.dtype)
+
+
+def seats_in_order(ring, far, seat, blocks, dtype):
+    rows, columns = ring.pieces[0].shape
+    found = [(k, ring.places[k], 0, rows) for k in OFFSETS[:-1]]
+    found += [(4, ring.places["first"], 0, rows // 2), (4, ring.places["second"], rows // 2, rows)]
+    where = [lax.rem(seat + item[0] + blocks, blocks) for item in found]
+    where = [jnp.where(far == 0, item, blocks - 1 - item) for item in where]
     where = jnp.stack(where).astype(jnp.int32)
-    pieces = [piece for unused, also, piece in found]
-    plan = [(i, at, at + item[2].shape[0]) for i, item in enumerate(found) for at in [item[1]]]
+    pieces = [item[1][0] for item in found]
+    plan = [(i, item[1][1], item[2], item[3]) for i, item in enumerate(found)]
     out = jax.ShapeDtypeStruct((blocks, rows, columns), dtype)
     placed = pl.pallas_call(
         functools.partial(place_kernel, plan),
@@ -243,9 +250,11 @@
     return placed.reshape(blocks * rows, columns)
 
 
-def bias_kernel(role_ref, table_ref, index_ref, out_ref):
+def bias_kernel(part, role_ref, table_ref, index_ref, out_ref):
+    count = out_ref.shape[0]
+
     def one(i, carry):
-        row = index_ref[pl.ds(i, 1), :]
+        row = index_ref[pl.ds(part * count + i, 1), :]
         marks = lax.broadcasted_iota(jnp.int32, (RELS_PAD, WIN), 0) == row
         hot = low(jnp.where(marks, 1.0, 0.0))
         both = jnp.dot(table_ref[...], hot, preferred_element_type=jnp.float32)
@@ -254,31 +263,30 @@
 
     @pl.when(role_ref[0] != 0)
     def visual():
-        lax.fori_loop(0, WIN, one, 0, unroll=4)
-
-    @pl.when(role_ref[0] == 0)
-    def question():
-        out_ref[...] = jnp.zeros_like(out_ref)
-
-
-def window_bias(role, rel_table, rel_index):
+        lax.fori_loop(0, count, one, 0, unroll=4)
+
+
+def window_bias(role, rel_table, rel_index, part, parts):
     table = jnp.pad(rel_table, ((0, 16 - HEADS), (0, RELS_PAD - RELS)))
     coarse = lax.reduce_precision(table, 8, 7)
     both = low(jnp.concatenate([coarse, table - coarse]))
-    found = pl.pallas_call(
-        bias_kernel,
-        out_shape=jax.ShapeDtypeStruct((WIN, 16, WIN), jnp.float32),
+    return pl.pallas_call(
+        functools.partial(bias_kernel, part),
+        out_shape=jax.ShapeDtypeStruct((WIN // parts, 16, WIN), jnp.float32),
         in_specs=[pl.BlockSpec(memory_space=pltpu.SMEM)] + [pl.BlockSpec()] * 2,
         cost_estimate=pl.CostEstimate(
-            flops=64 * RELS_PAD * WIN * WIN, bytes_accessed=4 * 17 * WIN * WIN, transcendentals=0
+            flops=64 * RELS_PAD * WIN * WIN // parts,
+            bytes_accessed=4 * 17 * WIN * WIN // parts,
+            transcendentals=0,
         ),
     )(role, both, rel_index)
-    return found[:, :HEADS].transpose(1, 0, 2)
-
-
-def table_kernel(role_ref, scores_ref, index_ref, out_ref):
+
+
+def table_kernel(part, role_ref, scores_ref, index_ref, out_ref):
+    count = scores_ref.shape[0]
+
     def one(i, total):
-        row = index_ref[pl.ds(i, 1), :]
+        row = index_ref[pl.ds(part * count + i, 1), :]
         marks = lax.broadcasted_iota(jnp.int32, (RELS_PAD, WIN), 0) == row
         hot = low(jnp.where(marks, 1.0, 0.0))
         return total + times_transposed(scores_ref[i], hot)
@@ -287,24 +295,29 @@
 
     @pl.when(role_ref[0] != 0)
     def visual():
-        out_ref[...] = lax.fori_loop(0, WIN, one, blank, unroll=4)
+        out_ref[...] = lax.fori_loop(0, count, one, blank, unroll=4)
 
     @pl.when(role_ref[0] == 0)
     def question():
         out_ref[...] = blank
 
 
-def table_sums(role, back_scores, rel_index):
-    rows = back_scores.reshape(2 * HEADS, WIN, WIN).transpose(1, 0, 2)
-    found = pl.pallas_call(
-        table_kernel,
+def table_sums(role, rows, rel_index, part, parts):
+    count = WIN // parts
+    return pl.pallas_call(
+        functools.partial(table_kernel, part),
         out_shape=jax.ShapeDtypeStruct((2 * HEADS, RELS_PAD), jnp.float32),
-        in_specs=[pl.BlockSpec(memory_space=pltpu.SMEM)] + [pl.BlockSpec()] * 2,
+        grid=(1,),
+        in_specs=[
+            pl.BlockSpec(memory_space=pltpu.SMEM),
+            pl.BlockSpec((count, 2 * HEADS, WIN), lambda i: (part, 0, 0)),
+            pl.BlockSpec((WIN, WIN), lambda i: (0, 0)),
+        ],
+        out_specs=pl.BlockSpec((2 * HEADS, RELS_PAD), lambda i: (0, 0)),
         cost_estimate=pl.CostEstimate(
-            flops=48 * RELS_PAD * WIN * WIN, bytes_accessed=52 * WIN * WIN, transcendentals=0
+            flops=48 * RELS_PAD * WIN * count, bytes_accessed=52 * WIN * count, transcendentals=0
         ),
     )(role, rows, rel_index)
-    return jnp.sum(found.reshape(HEADS, 2, RELS_PAD), axis=1)[:, :RELS]
 
 
 def head_lanes(side):
@@ -352,9 +365,9 @@
     return low(back_query), low(back_keys), low(back_values), kept
 
 
-def question_extra(role_ref, qid, kid):
+def question_extra(slot, role_ref, qid, kid):
     shape = (qid.shape[0], kid.shape[1])
-    row = lax.broadcasted_iota(jnp.int32, shape, 0) + role_ref[1]
+    row = lax.broadcasted_iota(jnp.int32, shape, 0) + role_ref[1 + slot]
     column = lax.broadcasted_iota(jnp.int32, shape, 1)
     return jnp.where((qid == kid) & (column <= row), 0.0, NEG)
 
@@ -372,7 +385,7 @@
     @pl.when(role_ref[0] == 0)
     def question():
         for s in (0, 1):
-            extra = question_extra(role_ref, qid_ref[s], kid_ref[s])
+            extra = question_extra(s, role_ref, qid_ref[s], kid_ref[s])
             o_ref[s], log_ref[s] = attend_pair(q_ref[s], k_ref[s], v_ref[s], [extra, extra])
 
     @pl.when(role_ref[0] != 0)
@@ -405,7 +418,7 @@
     def question():
         ds_ref[...] = jnp.zeros_like(ds_ref)
         for s in (0, 1):
-            extra = question_extra(role_ref, qid_ref[s], kid_ref[s])
+            extra = question_extra(s, role_ref, qid_ref[s], kid_ref[s])
             dq_ref[s], dk_ref[s], dv_ref[s], unused = pair_backward(
                 q_ref[s], k_ref[s], v_ref[s], [extra, extra], log_ref[s], back_ref[s]
             )
@@ -617,6 +630,42 @@
             flops=12 * count * D * FF, bytes_accessed=8 * D * FF, transcendentals=0
         ),
     )(rows, branch, weights, weights)
+
+
+def weight_kernel(places, *refs):
+    delta_ref = refs[-1]
+    cut = delta_ref.shape[3]
+    for number in range(len(refs) // 2):
+        delta = low(transposed_times(refs[2 * number][...], refs[2 * number + 1][...]))
+        for place in range(places):
+            delta_ref[place, number, 0] = delta[place * cut : (place + 1) * cut]
+
+
+def weight_gradients(pairs, blocks):
+    cut = D // (4 * blocks)
+    total = sum(rows.shape[0] for rows, unused in pairs)
+    if total > 8 * D:
+        parts = [low(transposed_times(rows, back)) for rows, back in pairs]
+        parts = jnp.stack([part.reshape(2, 2 * blocks, cut, D) for part in parts])
+        return parts.transpose(2, 0, 1, 3, 4)
+    specs, arrays = [], []
+    for rows, back in pairs:
+        specs.append(pl.BlockSpec((rows.shape[0], D // 2), lambda i: (0, i)))
+        specs.append(pl.BlockSpec(back.shape, lambda i: (0, 0)))
+        arrays += [rows, back]
+    return pl.pallas_call(
+        functools.partial(weight_kernel, 2 * blocks),
+        out_shape=jax.ShapeDtypeStruct((2 * blocks, len(pairs), 2, cut, D), jnp.bfloat16),
+        grid=(2,),
+        in_specs=specs,
+        out_specs=pl.BlockSpec(
+            (2 * blocks, len(pairs), 1, cut, D), lambda i: (0, 0, i, 0, 0)
+        ),
+        compiler_params=pltpu.CompilerParams(vmem_limit_bytes=32 * MIB),
+        cost_estimate=pl.CostEstimate(
+            flops=2 * total * D * D, bytes_accessed=4 * total * D, transcendentals=0
+        ),
+    )(*arrays)
 
 
 def body(
@@ -655,9 +704,12 @@
     early = -(-(LONGEST - 1) // share)
     reach = min(Q_LEN, share * (early + 1))
     span = reach + rows - share
-    first = jnp.clip((seat - early) * share, 0, Q_LEN - reach)
-    inset = jnp.where(asks, seat * share - first, 0)
-    role = jnp.stack([far, inset]).astype(jnp.int32)
+    turns = (seat, blocks - 1 - seat)
+    firsts = [jnp.clip((turn - early) * share, 0, Q_LEN - reach) for turn in turns]
+    insets = [jnp.where(far == 0, turn * share - at, 0) for turn, at in zip(turns, firsts)]
+    turn = jnp.where(far == 0, turns[0], turns[1])
+    first = jnp.where(far == 0, firsts[0], firsts[1])
+    role = jnp.stack([far] + insets).astype(jnp.int32)
     cut = D // (4 * blocks)
 
     def own_of(question_side, visual_side):
@@ -668,8 +720,11 @@
             self.kept = own_of(question_side, visual_side)
             self.away = own_of(visual_side, question_side)
 
+        def begin(self):
+            self.coming = swap_far(self.away)
+
         def send(self):
-            return swap_far(self.away)
+            return self.coming if hasattr(self, "coming") else swap_far(self.away)
 
         def receive(self, got):
             self.found = jnp.stack([own_of(self.kept, got), own_of(got, self.kept)])
@@ -700,7 +755,7 @@
         return [whole[:, at : at + width] for at, width in zip(places, splits)]
 
     def ring_of(own):
-        return Gather(own, blocks) if ringed else own
+        return Gather(own) if ringed else own
 
     def step(rings, transfers=(), work=()):
         return phase((list(rings) if ringed else []) + list(transfers), work)
@@ -711,49 +766,50 @@
         jnp.concatenate([block_of(causal_project, 3 * D), block_of(causal_output, D), norms], 1),
         jnp.concatenate([block_of(window_project, 3 * D), block_of(window_output, D), norms], 1),
     )
-    phase([self_shards])
+    cross_shards = Trade(
+        cross_squares(reader_query, reader_pair, reader_output),
+        cross_squares(viewer_query, viewer_pair, viewer_output),
+    )
+    cross_shards.kept, cross_shards.away = phase([self_shards], (cross_shards.kept, cross_shards.away))
     self_ring = ring_of(self_shards.found)
-    later_shards = Trade(
-        jnp.concatenate(
-            [
-                cross_squares(reader_query, reader_pair, reader_output),
-                mlp_squares(question_up, question_down),
-            ]
-        ),
-        jnp.concatenate(
-            [
-                cross_squares(viewer_query, viewer_pair, viewer_output),
-                mlp_squares(visual_up, visual_down),
-            ]
-        ),
-    )
-    step([self_ring], [later_shards])
+    mlp_shards = Trade(mlp_squares(question_up, question_down), mlp_squares(visual_up, visual_down))
+    mlp_shards.kept, mlp_shards.away = step(
+        [self_ring], [cross_shards], (mlp_shards.kept, mlp_shards.away)
+    )
     row_shards = Trade(
         pad_rows(lax.dynamic_slice_in_dim(question_in, first, reach, 0), span),
         pad_rows(visual_in, span),
     )
     marks = Trade(segment_ids[0], jnp.pad(regions, (0, Q_LEN - rows)))
     cot = Trade(
-        pad_rows(lax.dynamic_slice_in_dim(question_cot, seat * share, share, 0), rows), visual_cot
-    )
-    later = step([self_ring], [], later_shards.found)
+        pad_rows(lax.dynamic_slice_in_dim(question_cot, turn * share, share, 0), rows), visual_cot
+    )
+    row_shards.away, later = step([self_ring], [mlp_shards], (row_shards.away, cross_shards.found))
+    row_shards.begin()
+    later = jnp.concatenate([later, mlp_shards.found], 1)
     later = later.transpose(1, 0, 2, 3).reshape(-1, cut, D)
     later = lax.all_gather(later, ("core", "blk"), axis=1, tiled=True).reshape(-1, D, D)
-    bias = window_bias(role, rel_table, rel_index)
-    bias = step([self_ring], [], bias)
-    step([self_ring], [row_shards, marks])
+    bias = window_bias(role, rel_table, rel_index, 0, 2)
+    bias, rel_table = step([self_ring], [marks], (bias, rel_table))
+    bias_rest = window_bias(role, rel_table, rel_index, 1, 2)
+    bias_rest = step([self_ring], [row_shards], bias_rest)
+    bias = jnp.concatenate([bias, bias_rest])[:, :HEADS].transpose(1, 0, 2)
     slots, marks = row_shards.found, marks.found
+
+    def of_slots(values, starts, size):
+        return jnp.stack(
+            [lax.dynamic_slice_in_dim(values[i], start, size, 0) for i, start in enumerate(starts)]
+        )
+
     key_marks = own_of(
         jnp.pad(
-            lax.dynamic_slice_in_dim(marks, first, reach, 1),
-            ((0, 0), (0, span - reach)),
-            constant_values=-2,
+            of_slots(marks, firsts, reach), ((0, 0), (0, span - reach)), constant_values=-2
         ),
         marks[:, :span],
     )[:, None, :]
     row_marks = own_of(
         jnp.pad(
-            lax.dynamic_slice_in_dim(marks, seat * share, share, 1),
+            of_slots(marks, [turn * share for turn in turns], share),
             ((0, 0), (0, rows - share)),
             constant_values=-1,
         ),
@@ -765,7 +821,7 @@
     gains = norm_flat[:, : norm_gains.size].reshape(6, D)
     shifts = norm_flat[:, norm_gains.size :].reshape(6, D)
 
-    own = lax.dynamic_slice_in_dim(slots, inset, rows, 1).astype(jnp.float32)
+    own = of_slots(slots, insets, rows).astype(jnp.float32)
     self_gain, self_shift = own_of(gains[1], gains[0]), own_of(shifts[1], shifts[0])
     self_norm, self_pull = jax.vjp(normalize, own, self_gain, self_shift)
     self_low = low(self_norm).reshape(2 * rows, D)
@@ -816,9 +872,38 @@
     rows_three = rows_two + mlp_out.reshape(2, rows, D)
     back_mlp_in, gain_mlp, shift_mlp = mlp_pull(back_mlp.reshape(2, rows, D))
     back_two = cot.astype(jnp.float32) + back_mlp_in
-    mlp_delta = mlp_delta.reshape(2 * blocks, -1, D)
-    mlp_delta = lax.psum_scatter(mlp_delta, ("core", "blk"), scatter_dimension=0, tiled=True)
-
+    mlp_delta = mlp_delta.reshape(2, blocks, -1, D)
+
+    class Shares:
+        def __init__(self, delta):
+            self.delta = delta
+            self.swap = Once(
+                lambda: swap_core(lax.dynamic_index_in_dim(delta, 1 - core, 0, keepdims=False))
+            )
+
+        def start(self):
+            if ringed:
+                self.ring = Sum(self.chunk)
+            else:
+                kept = lax.dynamic_index_in_dim(self.delta, core, 0, keepdims=False)
+                kept = kept.astype(jnp.float32) + self.swap.found.astype(jnp.float32)
+                self.sum = lax.psum_scatter(kept, "blk", scatter_dimension=0, tiled=True)[0]
+
+        def chunk(self, k):
+            place = ring_place(seat + k, blocks)
+            mine = lax.dynamic_slice(self.delta, (core, place, 0, 0), (1, 1) + self.delta.shape[2:])
+            theirs = lax.dynamic_index_in_dim(self.swap.found, place, 0, keepdims=False)
+            mine = mine.reshape(theirs.shape)
+            return mine.astype(jnp.float32) + theirs.astype(jnp.float32)
+
+        def rings(self):
+            return [self.ring] if ringed else []
+
+        def total(self):
+            found = self.ring.total if ringed else self.sum
+            return found.reshape(-1, 2, cut, D).transpose(1, 0, 2, 3)
+
+    mlp_shares = Shares(mlp_delta)
     class Owners(Once):
         def __init__(self, total):
             self.total = total
@@ -844,63 +929,71 @@
 
     home_out = Home(low(rows_three))
 
-    def by_owner(parts):
-        whole = jnp.stack([part.reshape(2, -1, D) for part in parts], 1)
-        return whole.reshape(2, 4, -1, D).transpose(2, 1, 0, 3).reshape(2 * blocks * cut, 8, D)
-
     cross_branch = low(back_two).reshape(2 * rows, D)
     back_attn = low(times_transposed(cross_branch, cross_exit)).reshape(2, rows, D)
-    back_query, back_keys, back_values = cross_backward(
-        cross_query, cross_keys, cross_values, cross_extra, cross_logs, back_attn
+    back_attn = phase([mlp_shares.swap], back_attn)
+    mlp_shares.start()
+    back_query, back_keys, back_values = phase(
+        mlp_shares.rings(),
+        cross_backward(cross_query, cross_keys, cross_values, cross_extra, cross_logs, back_attn),
     )
     back_query = back_query.reshape(2 * rows, D)
     back_keys, back_values = back_keys.reshape(-1, D), back_values.reshape(-1, D)
     back_sources = times_transposed(back_keys, cross_key_weight)
     back_sources = back_sources + times_transposed(back_values, cross_value_weight)
-    back_sources = back_sources.reshape(2, -1, D)
+    back_sources = phase(mlp_shares.rings(), back_sources.reshape(2, -1, D))
+
+    def owned(delta):
+        delta = delta.reshape(2 * blocks, -1, D)
+        return lax.psum_scatter(delta, ("core", "blk"), scatter_dimension=0, tiled=True)
+
+    cross_pairs = [
+        (cross_low.reshape(2 * rows, D), back_query),
+        (sources, back_keys),
+        (sources, back_values),
+        (cross_attn, cross_branch),
+    ]
     if ringed:
 
         def source_chunk(k):
             at = OFFSETS.index(k) * rows
-            return back_sources[:, at : at + rows]
-
-        back_sent = Sum(source_chunk, blocks)
-        delta_cross_exit = low(transposed_times(cross_attn, cross_branch))
-        delta_cross_query = low(transposed_times(cross_low.reshape(2 * rows, D), back_query))
+            return back_sources[:, at : at + rows].reshape(2 * rows, D)
+
+        back_sent = Sum(source_chunk)
+        cross_delta = weight_gradients(cross_pairs, blocks)
         back_cross = times_transposed(back_query, cross_query_weight).reshape(2, rows, D)
-        works = [
-            (delta_cross_exit, delta_cross_query, back_cross),
-            low(transposed_times(sources, back_keys)),
-            low(transposed_times(sources, back_values)),
-            (),
-        ]
+        works = [back_cross, cross_delta, (), ()]
         extra = [[home_out], [], [], []]
         works = [phase([back_sent] + more, work) for work, more in zip(works, extra)]
-        delta_cross_exit, delta_cross_query, back_cross = works[0]
-        delta_cross_keys, delta_cross_values = works[1:3]
-        back_sent = back_sent.total
+        back_cross, cross_delta = works[:2]
+        cross_delta = owned(cross_delta)
+        back_sent = back_sent.total.reshape(2, rows, D)
     else:
         back_sent = lax.psum_scatter(back_sources, "blk", scatter_dimension=1, tiled=True)
         phase([home_out])
-        delta_cross_exit = low(transposed_times(cross_attn, cross_branch))
-        delta_cross_query = low(transposed_times(cross_low.reshape(2 * rows, D), back_query))
+        cross_delta = owned(weight_gradients(cross_pairs, blocks))
         back_cross = times_transposed(back_query, cross_query_weight).reshape(2, rows, D)
-        delta_cross_keys = low(transposed_times(sources, back_keys))
-        delta_cross_values = low(transposed_times(sources, back_values))
     returned = Once(lambda: swap_far(low(back_sent)))
-    cross_delta = by_owner(
-        [delta_cross_query, delta_cross_keys, delta_cross_values, delta_cross_exit]
-    )
-    cross_delta, mlp_delta = phase([returned], (cross_delta, mlp_delta))
-    cross_delta = lax.psum_scatter(cross_delta, ("core", "blk"), scatter_dimension=0, tiled=True)
+    phase([returned] + mlp_shares.rings())
     back_cross = back_cross + returned.found.astype(jnp.float32)
     back_cross_in, gain_cross, shift_cross = cross_pull(back_cross)
     back_one = back_two + back_cross_in
 
     self_branch = low(back_one).reshape(2 * rows, D)
     back_attn = low(times_transposed(self_branch, self_exit)).reshape(2, rows, D)
-    back_query, back_keys, back_values, back_scores = self_backward(
-        role, self_query, self_keys, self_values, bias, row_marks, key_marks, self_logs, back_attn
+    back_query, back_keys, back_values, back_scores = phase(
+        mlp_shares.rings(),
+        self_backward(
+            role,
+            self_query,
+            self_keys,
+            self_values,
+            bias,
+            row_marks,
+            key_marks,
+            self_logs,
+            back_attn,
+        ),
     )
     back_query = back_query.reshape(2 * rows, D)
     back_keys, back_values = back_keys.reshape(2 * span, D), back_values.reshape(2 * span, D)
@@ -910,68 +1003,58 @@
     back_self = times_transposed(back_query, self_query_weight).reshape(2, rows, D)
 
     def for_earlier(j):
-        at = jnp.maximum(inset - j * share, 0)
-        found = lax.dynamic_slice_in_dim(back_every, at, share, 1)
-        return jnp.where(asks & (seat >= j), found, 0.0)
-
-    order = ring_order(blocks)
-    earlier_hop = [(order[i], order[i - 1]) for i in range(1, blocks)]
-
-    class Chain:
+        parts = []
+        for slot in (0, 1):
+            at = jnp.maximum(insets[slot] - j * share, 0)
+            found = lax.dynamic_slice_in_dim(back_every[slot], at, share, 0)
+            parts.append(jnp.where(asks & (turns[slot] >= j), found, 0.0))
+        return parts
+
+    class Chain(Ring):
         def __init__(self):
-            self.left, self.state = early, low(for_earlier(early))
-
-        def send(self):
-            return lax.ppermute(self.state, "blk", earlier_hop)
+            self.left = early
+            self.set(for_earlier(early))
+
+        def set(self, total):
+            self.total = total
+            self.state = low(total[1]), low(total[0])
 
         def receive(self, found):
             self.left -= 1
-            self.total = found.astype(jnp.float32) + for_earlier(self.left)
-            self.state = low(self.total)
+            own = for_earlier(self.left)
+            self.set([found[1].astype(jnp.float32) + own[0], found[0].astype(jnp.float32) + own[1]])
 
     chain = Chain()
     chain.state, back_query, back_keys, back_values = lax.optimization_barrier(
         (chain.state, back_query, back_keys, back_values)
     )
-    self_parts = [
-        low(transposed_times(self_low, back_query)),
-        low(transposed_times(every_low, back_keys)),
-        low(transposed_times(every_low, back_values)),
-        low(transposed_times(self_attn, self_branch)),
+    self_pairs = [
+        (self_low, back_query),
+        (every_low, back_keys),
+        (every_low, back_values),
+        (self_attn, self_branch),
     ]
+    self_delta = weight_gradients(self_pairs, blocks).reshape(2, blocks, 8 * cut, D)
     question_rows, visual_out = home_out.found
-    out_ring = Circle(question_rows, blocks)
-    outs = [out_ring] if ringed else []
-    self_delta = jnp.stack(self_parts).reshape(4, 2, 2, blocks, cut, D)
-    self_delta = phase([chain] + outs, self_delta)
-    self_other = Once(
-        lambda: swap_core(lax.dynamic_index_in_dim(self_delta, 1 - core, 2, keepdims=False))
-    )
-    table_part = table_sums(role, back_scores, rel_index)
-    table_part = phase([chain, self_other] + outs, table_part)
-    self_other = self_other.found
-    if ringed:
-
-        def self_chunk(k):
-            place = ring_place(seat + k, blocks)
-            mine = lax.dynamic_slice(
-                self_delta, (0, 0, core, place, 0, 0), (4, 2, 1, 1, cut, D)
-            ).reshape(4, 2, cut, D)
-            theirs = lax.dynamic_index_in_dim(self_other, place, 2, keepdims=False)
-            return mine.astype(jnp.float32) + theirs.astype(jnp.float32)
-
-        self_sum = Sum(self_chunk, blocks)
-        sums = [self_sum]
-    else:
-        kept = lax.dynamic_index_in_dim(self_delta, core, 2, keepdims=False)
-        kept = kept.astype(jnp.float32) + self_other.astype(jnp.float32)
-        self_total = lax.psum_scatter(kept, "blk", scatter_dimension=2, tiled=True)[:, :, 0]
-        sums = []
-    mlp_sums = Owners(mlp_delta.reshape(2 * TILES, 2, cut, D).transpose(1, 0, 2, 3))
+    outs = [Gather(question_rows)] if ringed else []
+    score_rows = back_scores.reshape(2 * HEADS, WIN, WIN).transpose(1, 0, 2)
+    table_parts = [table_sums(role, score_rows, rel_index, part, 4) for part in range(4)]
+    self_delta, table_parts[0] = phase([chain] + outs, (self_delta, table_parts[0]))
+    self_shares = Shares(self_delta)
+    table_parts[1], cross_delta = phase(
+        [chain, self_shares.swap] + outs, (table_parts[1], cross_delta)
+    )
+    self_shares.start()
+    sums = self_shares.rings()
     for number in range(early - 2):
-        phase([chain] + outs + (sums if number < 2 else []))
+        work = table_parts[2 + number] if number < 2 else ()
+        work = phase([chain] + (outs + sums if number < 2 else []), work)
+        if number < 2:
+            table_parts[2 + number] = work
+    table_part = sum(table_parts).reshape(HEADS, 2, RELS_PAD)
+    table_part = jnp.sum(table_part, axis=1)[:, :RELS]
     back_self = back_self + own_of(
-        jnp.pad(chain.total, ((0, 0), (0, rows - share), (0, 0))), back_every[:, :rows]
+        jnp.pad(jnp.stack(chain.total), ((0, 0), (0, rows - share), (0, 0))), back_every[:, :rows]
     )
     back_self_in, gain_self, shift_self = self_pull(back_self)
     back_in = back_one + back_self_in
@@ -1000,8 +1083,9 @@
     class Everywhere:
         def __init__(self, total):
             self.total, self.bit = total, 0
-            self.bits = [("core", 1, 2), ("far", 1, 2)]
+            self.bits = [("far", 1, 2)]
             self.bits += [("blk", 1 << i, blocks) for i in range(blocks.bit_length() - 1)]
+            self.bits += [("core", 1, 2)]
 
         def send(self):
             axis, bit, count = self.bits[self.bit]
@@ -1012,27 +1096,27 @@
 
     small = Everywhere(small)
     home_back = Home(low(back_in))
-    cross_delta = phase([home_back, mlp_sums] + outs + sums, cross_delta)
-    cross_sums = Owners(cross_delta.reshape(cut, 4, 2, D).transpose(2, 1, 0, 3))
+    mlp_sums = Owners(mlp_shares.total())
+    phase([home_back, mlp_sums, small] + sums)
+    cross_sums = Owners(cross_delta.reshape(4, 2, cut, D).transpose(1, 0, 2, 3))
     question_back, visual_back = home_back.found
     if ringed:
-        back_ring = Gather(question_back, blocks)
-        phase([back_ring, small] + outs + sums)
-        self_total = self_sum.total
-    self_sums = Owners(self_total.transpose(1, 0, 2, 3))
+        back_ring = Gather(question_back)
+        phase([back_ring, small] + sums)
+    self_sums = Owners(self_shares.total())
     if ringed:
         for number in range(3):
-            more = (outs if out_ring.left else []) + [[], [cross_sums], [self_sums]][number]
-            phase([back_ring, small] + more)
-        found = [(k, 0, back_ring.pieces[k]) for k in OFFSETS[:-1]]
-        found += [(4, 0, back_ring.pieces["first"]), (4, share // 2, back_ring.pieces["second"])]
-        question_delta = seats_in_order(found, seat, blocks, jnp.float32)
-        found = [(-k, 0, piece) for k, piece in enumerate(out_ring.pieces)]
-        question_out = seats_in_order(found, seat, blocks, jnp.bfloat16)
+            phase([back_ring, small] + [[], [cross_sums], [self_sums]][number])
+        question_delta = seats_in_order(back_ring, far, seat, blocks, jnp.float32)
+        question_out = seats_in_order(outs[0], far, seat, blocks, jnp.bfloat16)
     else:
         both = jnp.stack([question_rows, question_back])
         both = lax.all_gather(both, "blk", axis=0)
-        both = jnp.concatenate([both[i] for i in ring_order(blocks)], 1)
+        order = ring_order(blocks)
+        both = own_of(
+            jnp.concatenate([both[i] for i in order], 1),
+            jnp.concatenate([both[i] for i in order[::-1]], 1),
+        )
         question_out, question_delta = both[0], both[1].astype(jnp.float32)
         phase([cross_sums, self_sums])
     while small.bit < len(small.bits):

time: 599 us -> 577 us (0.963)
  starting transfers between devices: 134 us -> 83.2 us
  Pallas kernels: 97.1 us -> 119 us
  matrix products: 53.8 us -> 33.2 us
  local copies, waits for them, and re-layouts: 63.7 us -> 82 us
  other arithmetic: 63.3 us -> 77.9 us
  waiting for transfers between devices: 163 us -> 157 us
    ppermute x12 -> x13, starting transfers between devices: 56.7 us -> 20.5 us  [swap_far(): return lax.ppermute(values, 'far', [(0, 1), (1, 0)])]
    pallas_call x2 -> x8, Pallas kernels: 4.77 us -> 27.2 us  [the longest x2 15.9 us: weight_gradients(): pl.pallas_call(functools.partial(weight_kernel, 2 * blocks), out_shape=ja...]
    dot_general x8 -> x0, matrix products: 17.5 us -> none  [transposed_times(): lax.dot_general(left, right, (((0,), (0,)), ((), ())), preferred_element_...]
    ppermute x51 -> x50, starting transfers between devices: 68.6 us -> 52.7 us  [phase(): lax.ppermute(parts[0] if len(parts) == 1 else jnp.concatenate(parts), 'bl...]
    ppermute x51 -> x50, waiting for transfers between devices: 132 us -> 117 us  [phase(): lax.ppermute(parts[0] if len(parts) == 1 else jnp.concatenate(parts), 'bl...]
    convert_element_type x20 -> x32, other arithmetic: 25.1 us -> 35 us  [low(): return values.astype(jnp.bfloat16)]
    unnamed x267 -> x298, local copies, waits for them, and re-layouts: 20.4 us -> 30.1 us
    ppermute x12 -> x13, waiting for transfers between devices: 27.3 us -> 35.7 us  [swap_far(): return lax.ppermute(values, 'far', [(0, 1), (1, 0)])]
  transfers between devices with their start and end apart: 81 -> 81, of which waited for: 38 -> 44; matrix products, arithmetic and copies ran while one was open for 24% -> 22% of each run, Pallas kernels for 11% -> 15%
where the time goes in v3:
time: 577 us; the launch traced here: 569 us
  waiting for transfers between devices  157 us (27%)
  Pallas kernels  119 us (21%)
  starting transfers between devices  83.2 us (14%)
  local copies, waits for them, and re-layouts  82 us (14%)
  other arithmetic  77.9 us (14%)
  matrix products  33.2 us (6%)
  between operations  16.9 us (3%)
    ppermute x50, waiting for transfers between devices, phase(): lax.ppermute(parts[0] if len(parts) == 1 else jnp.concatenate(parts), 'bl...  117 us
    ppermute x50, starting transfers between devices, phase(): lax.ppermute(parts[0] if len(parts) == 1 else jnp.concatenate(parts), 'bl...  52.7 us
    ppermute x13, waiting for transfers between devices, swap_far(): return lax.ppermute(values, 'far', [(0, 1), (1, 0)])  35.7 us
    convert_element_type x32, other arithmetic, low(): return values.astype(jnp.bfloat16)  35 us
    unnamed x298, local copies, waits for them, and re-layouts  30.1 us
    pallas_call x1, Pallas kernels, cross_backward(): pl.pallas_call(cross_backward_kernel, out_shape=[jax.ShapeDtypeStruct((2,...  24.8 us
    ppermute x13, starting transfers between devices, swap_far(): return lax.ppermute(values, 'far', [(0, 1), (1, 0)])  20.5 us
    dot_general x8, matrix products, product(): return jnp.dot(left, right, preferred_element_type=jnp.float32)  18.8 us
  transfers between devices with their start and end apart: 81, of which 44 were waited for; matrix products, arithmetic and copies ran while one was open for 22% of the time, Pallas kernels for 15%

profile of v3, /device:TPU:0, one launch (start us, length us, event | category | flops | bytes accessed | tf_op | source)
XLA Modules:
  0.0 569.0 jit_solution(16292205000421630974)
XLA Ops:
  36.1 6.3 %collective-permute-done.6 = bf16[8,24,768]{2,0,1:T(8,128)(2,1)S(1)} collective-permute-done((bf16[8,24,768]{2,0,1:T(8,128)(2,1)S(1)}, bf16[8,24,768]{2,0,1:T(8,128)(2,1)S(1)}, u32[]{:S(2)}, u32[]{:S(2)}) %collective-permute-start.6) | collective-permute-done | bytes 294944 | tf_op jit(solution)/shard_map/ppermute | solution.py:82
  50.5 7.5 %collective-permute-start.12 = (bf16[656,768]{1,0:T(8,128)(2,1)}, bf16[656,768]{1,0:T(8,128)(2,1)}, u32[]{:S(2)}, u32[]{:S(2)}) collective-permute-start(bf16[656,768]{1,0:T(8,128)(2,1)} %pad_select_fusion), channel_id=1, source_target_pairs={{0,16},{16,0},{1,17},{17,1},{2,18},{18,2},{3,19},{19,3},{4,20},{20... | collective-permute-start | bytes 3022856 | tf_op jit(solution)/shard_map/ppermute | solution.py:82
  68.1 5.2 collective-permute-done.11.refs_8_
  73.3 7.5 %collective-permute-done.12 = bf16[656,768]{1,0:T(8,128)(2,1)} collective-permute-done((bf16[656,768]{1,0:T(8,128)(2,1)}, bf16[656,768]{1,0:T(8,128)(2,1)}, u32[]{:S(2)}, u32[]{:S(2)}) %collective-permute-start.12) | collective-permute-done | bytes 1007648 | tf_op jit(solution)/shard_map/ppermute | solution.py:82
  104.5 10.5 %shard_map.402 = (bf16[2,144,768]{2,1,0:T(8,128)(2,1)S(1)}, f32[2,144,768]{2,1,0:T(8,128)S(1)}) custom-call(s32[3]{0:T(128)S(1)} %copy-done.54, bf16[2,144,768]{2,1,0:T(8,128)(2,1)S(1)} %bitcast.411, bf16[2,656,768]{2,1,0:T(8,128)(2,1)S(1)} %bitcast.396, bf16[2,656,768]{2,1,0:T(8,128)(2,1)S(1)} %bitcast.394, f32[12,144,144]{2,1,0:T(8,128)S(1)} %fusion.4.bias_ref, ...), custom_call_target="tpu_custom_call" | custom-call | flops 1160773632 | bytes 6045696 | tf_op jit(solution)/shard_map/pallas_call | solution.py:453
  117.3 11.3 %collective-permute-done.22 = bf16[2,144,768]{2,1,0:T(8,128)(2,1)S(1)} collective-permute-done((bf16[2,144,768]{2,1,0:T(8,128)(2,1)S(1)}, bf16[2,144,768]{2,1,0:T(8,128)(2,1)S(1)}, u32[]{:S(2)}, u32[]{:S(2)}) %collective-permute-start.22) | collective-permute-done | bytes 442400 | tf_op jit(solution)/shard_map/ppermute | solution.py:82
  131.1 5.9 %collective-permute-done.25 = bf16[144,768]{1,0:T(8,128)(2,1)S(1)} collective-permute-done((bf16[144,768]{1,0:T(8,128)(2,1)S(1)}, bf16[144,768]{1,0:T(8,128)(2,1)S(1)}, u32[]{:S(2)}, u32[]{:S(2)}) %collective-permute-start.25) | collective-permute-done | bytes 221216 | tf_op jit(solution)/shard_map/ppermute | solution.py:82
  137.0 9.0 %collective-permute-done.23 = bf16[2,144,768]{2,1,0:T(8,128)(2,1)} collective-permute-done((bf16[2,144,768]{2,1,0:T(8,128)(2,1)S(1)}, bf16[2,144,768]{2,1,0:T(8,128)(2,1)}, u32[]{:S(2)}, u32[]{:S(2)}) %collective-permute-start.23) | collective-permute-done | bytes 442400 | tf_op jit(solution)/shard_map/ppermute | solution.py:153
  146.0 11.6 %collective-permute-done.24 = bf16[2,144,768]{2,1,0:T(8,128)(2,1)S(1)} collective-permute-done((bf16[2,144,768]{2,1,0:T(8,128)(2,1)S(1)}, bf16[2,144,768]{2,1,0:T(8,128)(2,1)S(1)}, u32[]{:S(2)}, u32[]{:S(2)}) %collective-permute-start.24) | collective-permute-done | bytes 442400 | tf_op jit(solution)/shard_map/ppermute | solution.py:153
  163.5 6.3 %collective-permute-done.26 = bf16[2,144,768]{2,1,0:T(8,128)(2,1)S(1)} collective-permute-done((bf16[2,144,768]{2,1,0:T(8,128)(2,1)}, bf16[2,144,768]{2,1,0:T(8,128)(2,1)S(1)}, u32[]{:S(2)}, u32[]{:S(2)}) %collective-permute-start.26) | collective-permute-done | bytes 442400 | tf_op jit(solution)/shard_map/ppermute | solution.py:153
  176.9 6.0 %collective-permute-done.28 = bf16[2,144,768]{2,1,0:T(8,128)(2,1)S(1)} collective-permute-done((bf16[2,144,768]{2,1,0:T(8,128)(2,1)S(1)}, bf16[2,144,768]{2,1,0:T(8,128)(2,1)S(1)}, u32[]{:S(2)}, u32[]{:S(2)}) %collective-permute-start.28) | collective-permute-done | bytes 442400 | tf_op jit(solution)/shard_map/ppermute | solution.py:153
  196.1 5.5 convolution_convert_fusion
  201.6 6.2 %convolution_convert_fusion.1 = bf16[2304,768]{1,0:T(8,128)(2,1)S(1)} fusion(bf16[2304,768]{1,0:T(8,128)(2,1)} %bitcast.53.refs_2_.refs_4_, bf16[768,768]{1,0:T(8,128)(2,1)S(1)} %bitcast.475), kind=kOutput, calls=%fused_computation.2 | convolution fusion | flops 2719678464 | bytes 8257536 | tf_op jit(solution)/shard_map/dot_general | solution.py:29
  208.4 14.6 %shard_map.403 = (bf16[2,144,768]{2,1,0:T(8,128)(2,1)S(1)}, f32[2,144,768]{2,1,0:T(8,128)S(1)}) custom-call(bf16[2,144,768]{2,1,0:T(8,128)(2,1)S(1)} %bitcast.431, bf16[2,1152,768]{2,1,0:T(8,128)(2,1)S(1)} %bitcast.425, bf16[2,1152,768]{2,1,0:T(8,128)(2,1)S(1)} %bitcast.423, f32[1,1152]{1,0:T(1,128)S(1)} %broadcast_select_fusion.12.extra_ref), custom_call_target="tpu_custom_call" | custom-call | flops 4076863488 | bytes 7077888 | tf_op jit(solution)/shard_map/pallas_call | solution.py:526
  224.6 18.1 %shard_map.404 = (f32[288,768]{1,0:T(8,128)S(1)}, f32[288,768]{1,0:T(8,128)S(1)}, bf16[16,8,2,24,768]{4,3,2,1,0:T(8,128)(2,1)}) custom-call(bf16[288,768]{1,0:T(8,128)(2,1)S(1)} %bitcast.410, bf16[288,768]{1,0:T(8,128)(2,1)S(1)} %bitcast.407, bf16[12,768,768]{2,1,0:T(8,128)(2,1)} %bitcast.472, bf16[12,768,768]{2,1,0:T(8,128)(2,1)} %bitcast.473), custom_call_target="tpu_custom_call" | custom-call | flops 8153726976 | bytes 18874368 | tf_op jit(solution)/shard_map/pallas_call | solution.py:612
  259.3 24.8 %shard_map.405 = (bf16[2,144,768]{2,1,0:T(8,128)(2,1)S(1)}, bf16[2,1152,768]{2,1,0:T(8,128)(2,1)S(1)}, bf16[2,1152,768]{2,1,0:T(8,128)(2,1)S(1)}) custom-call(bf16[2,144,768]{2,1,0:T(8,128)(2,1)S(1)} %bitcast.432, bf16[2,1152,768]{2,1,0:T(8,128)(2,1)S(1)} %bitcast.426, bf16[2,1152,768]{2,1,0:T(8,128)(2,1)S(1)} %bitcast.424, ...), custom_call_target="tpu_custom_call" | custom-call | flops 10192158720 | bytes 14155776 | tf_op jit(solution)/shard_map/pallas_call | solution.py:545
  296.1 8.0 %collective-permute-done.35 = bf16[384,768]{1,0:T(8,128)(2,1)S(1)} collective-permute-done((bf16[384,768]{1,0:T(8,128)(2,1)S(1)}, bf16[384,768]{1,0:T(8,128)(2,1)S(1)}, u32[]{:S(2)}, u32[]{:S(2)}) %collective-permute-start.35) | collective-permute-done | bytes 589856 | tf_op jit(solution)/shard_map/ppermute | solution.py:153
  314.9 9.8 %shard_map.406 = bf16[16,4,2,24,768]{4,3,2,1,0:T(8,128)(2,1)S(1)} custom-call(bf16[288,768]{1,0:T(8,128)(2,1)S(1)} %bitcast.409, bf16[288,768]{1,0:T(8,128)(2,1)S(1)} %bitcast.406, bf16[2304,768]{1,0:T(8,128)(2,1)} %bitcast.53.refs_2_.refs_4_, bf16[2304,768]{1,0:T(8,128)(2,1)S(1)} %bitcast.428, bf16[2304,768]{1,0:T(8,128)(2,1)} %bitcast.53.refs_2_.refs_4_, ...), custom_call_target="tpu_custom_call" | custom-call | flops 6115295232 | bytes 15925248 | tf_op jit(solution)/shard_map/pallas_call | solution.py:656
  330.1 6.9 %collective-permute-done.44 = bf16[288,768]{1,0:T(8,128)(2,1)S(1)} collective-permute-done((bf16[288,768]{1,0:T(8,128)(2,1)}, bf16[288,768]{1,0:T(8,128)(2,1)S(1)}, u32[]{:S(2)}, u32[]{:S(2)}) %collective-permute-start.44) | collective-permute-done | bytes 442400 | tf_op jit(solution)/shard_map/ppermute | solution.py:153
  355.8 5.9 %collective-permute-done.40 = bf16[384,768]{1,0:T(8,128)(2,1)} collective-permute-done((bf16[384,768]{1,0:T(8,128)(2,1)}, bf16[384,768]{1,0:T(8,128)(2,1)}, u32[]{:S(2)}, u32[]{:S(2)}) %collective-permute-start.40) | collective-permute-done | bytes 589856 | tf_op jit(solution)/shard_map/ppermute | solution.py:153
  373.6 17.3 %shard_map.407 = (bf16[2,144,768]{2,1,0:T(8,128)(2,1)S(1)}, bf16[2,656,768]{2,1,0:T(8,128)(2,1)S(1)}, bf16[2,656,768]{2,1,0:T(8,128)(2,1)S(1)}, bf16[12,2,144,144]{3,2,1,0:T(8,128)(2,1)S(1)}) custom-call(s32[3]{0:T(128)S(1)} %copy-done.54, bf16[2,144,768]{2,1,0:T(8,128)(2,1)S(1)} %bitcast.412, bf16[2,656,768]{2,1,0:T(8,128)(2,1)S(1)} %bitcast.397, ...), custom_call_target="tpu_custom_call" | custom-call | flops 2901934080 | bytes 8060928 | tf_op jit(solution)/shard_map/pallas_call | solution.py:472
  411.0 6.1 %shard_map.408 = bf16[16,4,2,24,768]{4,3,2,1,0:T(8,128)(2,1)S(1)} custom-call(bf16[288,768]{1,0:T(8,128)(2,1)S(1)} %fusion.26.refs_0_, bf16[288,768]{1,0:T(8,128)(2,1)S(1)} %bitcast.403, bf16[1312,768]{1,0:T(8,128)(2,1)S(1)} %copy-done.3, bf16[1312,768]{1,0:T(8,128)(2,1)S(1)} %bitcast.391, bf16[1312,768]{1,0:T(8,128)(2,1)S(1)} %copy-done.3, ...), custom_call_target="tpu_custom_call" | custom-call | flops 3774873600 | bytes 9830400 | tf_op jit(solution)/shard_map/pallas_call | solution.py:656
  426.2 15.1 %collective-permute-done.54.refs_4_ = bf16[256,768]{1,0:T(8,128)(2,1)S(1)} collective-permute-done((bf16[256,768]{1,0:T(8,128)(2,1)S(1)}, bf16[256,768]{1,0:T(8,128)(2,1)S(1)}, u32[]{:S(2)}, u32[]{:S(2)}) %collective-permute-start.54) | collective-permute-done | bytes 393248 | tf_op jit(solution)/shard_map/ppermute | solution.py:153
  451.2 9.2 %collective-permute-done.57.refs_6_ = bf16[352,768]{1,0:T(8,128)(2,1)S(1)} collective-permute-done((bf16[352,768]{1,0:T(8,128)(2,1)}, bf16[352,768]{1,0:T(8,128)(2,1)S(1)}, u32[]{:S(2)}, u32[]{:S(2)}) %collective-permute-start.57) | collective-permute-done | bytes 540704 | tf_op jit(solution)/shard_map/ppermute | solution.py:153
  (700 shorter events, 317.7 us)
Async XLA Ops:
  7.2 185.2 %all-gather.2.cloned.1.call-start = ((), (), s32[]{:S(2)}) async-start(), calls=%async_computation.1 | async-start | bytes 15040512 | tf_op jit(solution)/shard_map/all_gather | solution.py:791
  44.1 397.7 %reduce-scatter.2.cloned.1.call-start = ((), (), s32[]{:S(2)}) async-start(), calls=%async_computation.2 | async-start | bytes 5013504 | tf_op jit(solution)/shard_map/reduce_scatter | solution.py:948
  49.9 36.3 %collective-permute-start.13 = (bf16[2,24,3200]{2,1,0:T(8,128)(2,1)S(1)}, bf16[2,24,3200]{2,1,0:T(8,128)(2,1)S(1)}, u32[]{:S(2)}, u32[]{:S(2)}) collective-permute-start(bf16[2,24,3200]{2,1,0:T(8,128)(2,1)S(1)} %pad_maximum_fusion.14.refs_0_), channel_id=1, source_target_pairs={{0,8},{8,0},{1,9},{9,1},{2,10},{10,2},{3,11},{11,3},{4,12},{12,4},... | collective-permute-start | bytes 921608 | tf_op jit(solution)/shard_map/ppermute | solution.py:86
  50.0 37.5 %collective-permute-start.14 = (bf16[2,24,3200]{2,1,0:T(8,128)(2,1)S(1)}, bf16[2,24,3200]{2,1,0:T(8,128)(2,1)S(1)}, u32[]{:S(2)}, u32[]{:S(2)}) collective-permute-start(bf16[2,24,3200]{2,1,0:T(8,128)(2,1)S(1)} %collective-permute-done.1.refs_1_), channel_id=1, source_target_pairs={{0,8},{8,0},{1,9},{9,1},{2,10},{10,2},{3,11},{11,3},{4,12},{12,4},... | collective-permute-start | bytes 921608 | tf_op jit(solution)/shard_map/ppermute | solution.py:86
  50.5 30.3 %collective-permute-start.12 = (bf16[656,768]{1,0:T(8,128)(2,1)}, bf16[656,768]{1,0:T(8,128)(2,1)}, u32[]{:S(2)}, u32[]{:S(2)}) collective-permute-start(bf16[656,768]{1,0:T(8,128)(2,1)} %pad_select_fusion), channel_id=1, source_target_pairs={{0,16},{16,0},{1,17},{17,1},{2,18},{18,2},{3,19},{19,3},{4,20},{20... | collective-permute-start | bytes 3022856 | tf_op jit(solution)/shard_map/ppermute | solution.py:82
  68.1 20.3 %collective-permute-start.15 = (bf16[2,24,3200]{2,1,0:T(8,128)(2,1)S(1)}, bf16[2,24,3200]{2,1,0:T(8,128)(2,1)S(1)}, u32[]{:S(2)}, u32[]{:S(2)}) collective-permute-start(bf16[2,24,3200]{2,1,0:T(8,128)(2,1)S(1)} %collective-permute-done.2.refs_2_), channel_id=1, source_target_pairs={{0,8},{8,0},{1,9},{9,1},{2,10},{10,2},{3,11},{11,3},{4,12},{12,4},... | collective-permute-start | bytes 921608 | tf_op jit(solution)/shard_map/ppermute | solution.py:86
  73.3 15.6 %collective-permute-start.16 = (bf16[2,24,3200]{2,1,0:T(8,128)(2,1)S(1)}, bf16[2,24,3200]{2,1,0:T(8,128)(2,1)S(1)}, u32[]{:S(2)}, u32[]{:S(2)}) collective-permute-start(bf16[2,24,3200]{2,1,0:T(8,128)(2,1)S(1)} %collective-permute-done.4.refs_3_), channel_id=1, source_target_pairs={{0,8},{8,0},{1,9},{9,1},{2,10},{10,2},{3,11},{11,3},{4,12},{12,4},... | collective-permute-start | bytes 921608 | tf_op jit(solution)/shard_map/ppermute | solution.py:86
  128.6 17.4 %collective-permute-start.23 = (bf16[2,144,768]{2,1,0:T(8,128)(2,1)S(1)}, bf16[2,144,768]{2,1,0:T(8,128)(2,1)}, u32[]{:S(2)}, u32[]{:S(2)}) collective-permute-start(bf16[2,144,768]{2,1,0:T(8,128)(2,1)S(1)} %collective-permute-done.22), channel_id=1, source_target_pairs={{0,2},{2,4},{4,6},{6,7},{7,5},{5,3},{3,1},{1,0},{8,10},{10,12},{12... | collective-permute-start | bytes 1327112 | tf_op jit(solution)/shard_map/ppermute | solution.py:153
  130.2 27.4 %collective-permute-start.24 = (bf16[2,144,768]{2,1,0:T(8,128)(2,1)S(1)}, bf16[2,144,768]{2,1,0:T(8,128)(2,1)S(1)}, u32[]{:S(2)}, u32[]{:S(2)}) collective-permute-start(bf16[2,144,768]{2,1,0:T(8,128)(2,1)S(1)} %collective-permute-done.22), channel_id=1, source_target_pairs={{2,0},{4,2},{6,4},{7,6},{5,7},{3,5},{1,3},{0,1},{10,8},{12,10},{14... | collective-permute-start | bytes 1327112 | tf_op jit(solution)/shard_map/ppermute | solution.py:153
  250.9 59.1 %collective-permute-start.39 = (bf16[144,768]{1,0:T(8,128)(2,1)S(1)}, bf16[144,768]{1,0:T(8,128)(2,1)S(1)}, u32[]{:S(2)}, u32[]{:S(2)}) collective-permute-start(bf16[144,768]{1,0:T(8,128)(2,1)S(1)} %select_bitcast_fusion.5), channel_id=1, source_target_pairs={{0,16},{16,0},{1,17},{17,1},{2,18},{18,2},{3,19},{19,3},{4,20},{20... | collective-permute-start | bytes 663560 | tf_op jit(solution)/shard_map/ppermute | solution.py:82
  257.2 26.9 %collective-permute-start.33 = (bf16[192,768]{1,0:T(8,128)(2,1)S(1)}, bf16[192,768]{1,0:T(8,128)(2,1)S(1)}, u32[]{:S(2)}, u32[]{:S(2)}) collective-permute-start(bf16[192,768]{1,0:T(8,128)(2,1)S(1)} %get-tuple-element.270), channel_id=1, source_target_pairs={{0,2},{2,4},{4,6},{6,7},{7,5},{5,3},{3,1},{1,0},{8,10},{10,12},{12... | collective-permute-start | bytes 884744 | tf_op jit(solution)/shard_map/ppermute | solution.py:153
  257.8 26.3 %collective-permute-start.34 = (bf16[192,768]{1,0:T(8,128)(2,1)S(1)}, bf16[192,768]{1,0:T(8,128)(2,1)S(1)}, u32[]{:S(2)}, u32[]{:S(2)}) collective-permute-start(bf16[192,768]{1,0:T(8,128)(2,1)S(1)} %get-tuple-element.271), channel_id=1, source_target_pairs={{2,0},{4,2},{6,4},{7,6},{5,7},{3,5},{1,3},{0,1},{10,8},{12,10},{14... | collective-permute-start | bytes 884744 | tf_op jit(solution)/shard_map/ppermute | solution.py:153
  289.2 14.9 %collective-permute-start.35 = (bf16[384,768]{1,0:T(8,128)(2,1)S(1)}, bf16[384,768]{1,0:T(8,128)(2,1)S(1)}, u32[]{:S(2)}, u32[]{:S(2)}) collective-permute-start(bf16[384,768]{1,0:T(8,128)(2,1)S(1)} %get-tuple-element.279), channel_id=1, source_target_pairs={{0,2},{2,4},{4,6},{6,7},{7,5},{5,3},{3,1},{1,0},{8,10},{10,12},{12... | collective-permute-start | bytes 1769480 | tf_op jit(solution)/shard_map/ppermute | solution.py:153
  289.9 14.7 %collective-permute-start.36 = (bf16[384,768]{1,0:T(8,128)(2,1)S(1)}, bf16[384,768]{1,0:T(8,128)(2,1)S(1)}, u32[]{:S(2)}, u32[]{:S(2)}) collective-permute-start(bf16[384,768]{1,0:T(8,128)(2,1)S(1)} %get-tuple-element.280), channel_id=1, source_target_pairs={{2,0},{4,2},{6,4},{7,6},{5,7},{3,5},{1,3},{0,1},{10,8},{12,10},{14... | collective-permute-start | bytes 1769480 | tf_op jit(solution)/shard_map/ppermute | solution.py:153
  365.7 25.2 %collective-permute-start.49 = (bf16[384,768]{1,0:T(8,128)(2,1)S(1)}, bf16[384,768]{1,0:T(8,128)(2,1)S(1)}, u32[]{:S(2)}, u32[]{:S(2)}) collective-permute-start(bf16[384,768]{1,0:T(8,128)(2,1)S(1)} %get-tuple-element.309), channel_id=1, source_target_pairs={{0,2},{2,4},{4,6},{6,7},{7,5},{5,3},{3,1},{1,0},{8,10},{10,12},{12... | collective-permute-start | bytes 1769480 | tf_op jit(solution)/shard_map/ppermute | solution.py:153
  366.6 24.4 %collective-permute-start.50 = (bf16[384,768]{1,0:T(8,128)(2,1)S(1)}, bf16[384,768]{1,0:T(8,128)(2,1)S(1)}, u32[]{:S(2)}, u32[]{:S(2)}) collective-permute-start(bf16[384,768]{1,0:T(8,128)(2,1)S(1)} %get-tuple-element.310), channel_id=1, source_target_pairs={{2,0},{4,2},{6,4},{7,6},{5,7},{3,5},{1,3},{0,1},{10,8},{12,10},{14... | collective-permute-start | bytes 1769480 | tf_op jit(solution)/shard_map/ppermute | solution.py:153
  398.3 18.8 %collective-permute-start.52 = (bf16[256,768]{1,0:T(8,128)(2,1)}, bf16[256,768]{1,0:T(8,128)(2,1)S(1)}, u32[]{:S(2)}, u32[]{:S(2)}) collective-permute-start(bf16[256,768]{1,0:T(8,128)(2,1)} %pad_maximum_fusion.11), channel_id=1, source_target_pairs={{2,0},{4,2},{6,4},{7,6},{5,7},{3,5},{1,3},{0,1},{10,8},{12,10},{14... | collective-permute-start | bytes 1179656 | tf_op jit(solution)/shard_map/ppermute | solution.py:153
  399.8 17.3 %collective-permute-start.51 = (bf16[256,768]{1,0:T(8,128)(2,1)}, bf16[256,768]{1,0:T(8,128)(2,1)S(1)}, u32[]{:S(2)}, u32[]{:S(2)}) collective-permute-start(bf16[256,768]{1,0:T(8,128)(2,1)} %pad_maximum_fusion.10), channel_id=1, source_target_pairs={{0,2},{2,4},{4,6},{6,7},{7,5},{5,3},{3,1},{1,0},{8,10},{10,12},{12... | collective-permute-start | bytes 1179656 | tf_op jit(solution)/shard_map/ppermute | solution.py:153
  420.0 21.3 %collective-permute-start.55 = (bf16[8,192,768]{2,1,0:T(8,128)(2,1)}, bf16[8,192,768]{2,1,0:T(8,128)(2,1)}, u32[]{:S(2)}, u32[]{:S(2)}) collective-permute-start(bf16[8,192,768]{2,1,0:T(8,128)(2,1)} %dynamic-slice_bitcast_fusion.1), channel_id=1, source_target_pairs={{0,8},{8,0},{1,9},{9,1},{2,10},{10,2},{3,11},{11,3},{4,12},{12,4},... | collective-permute-start | bytes 7077896 | tf_op jit(solution)/shard_map/ppermute | solution.py:86
  422.3 18.9 %collective-permute-start.54 = (bf16[256,768]{1,0:T(8,128)(2,1)S(1)}, bf16[256,768]{1,0:T(8,128)(2,1)S(1)}, u32[]{:S(2)}, u32[]{:S(2)}) collective-permute-start(bf16[256,768]{1,0:T(8,128)(2,1)S(1)} %pad_maximum_fusion.13), channel_id=1, source_target_pairs={{2,0},{4,2},{6,4},{7,6},{5,7},{3,5},{1,3},{0,1},{10,8},{12,10},{14... | collective-permute-start | bytes 1179656 | tf_op jit(solution)/shard_map/ppermute | solution.py:153
  423.2 18.1 %collective-permute-start.53 = (bf16[256,768]{1,0:T(8,128)(2,1)S(1)}, bf16[256,768]{1,0:T(8,128)(2,1)S(1)}, u32[]{:S(2)}, u32[]{:S(2)}) collective-permute-start(bf16[256,768]{1,0:T(8,128)(2,1)S(1)} %pad_maximum_fusion.12), channel_id=1, source_target_pairs={{0,2},{2,4},{4,6},{6,7},{7,5},{5,3},{3,1},{1,0},{8,10},{10,12},{12... | collective-permute-start | bytes 1179656 | tf_op jit(solution)/shard_map/ppermute | solution.py:153
  446.0 14.4 %collective-permute-start.57 = (bf16[352,768]{1,0:T(8,128)(2,1)}, bf16[352,768]{1,0:T(8,128)(2,1)S(1)}, u32[]{:S(2)}, u32[]{:S(2)}) collective-permute-start(bf16[352,768]{1,0:T(8,128)(2,1)} %pad_maximum_fusion.5), channel_id=1, source_target_pairs={{2,0},{4,2},{6,4},{7,6},{5,7},{3,5},{1,3},{0,1},{10,8},{12,10},{14... | collective-permute-start | bytes 1622024 | tf_op jit(solution)/shard_map/ppermute | solution.py:153
  473.8 28.0 %collective-permute-start.63 = (bf16[8,24,768]{2,0,1:T(8,128)(2,1)}, bf16[8,24,768]{2,0,1:T(8,128)(2,1)}, u32[]{:S(2)}, u32[]{:S(2)}) collective-permute-start(bf16[8,24,768]{2,0,1:T(8,128)(2,1)} %fusion.52), channel_id=1, source_target_pairs={{0,16},{16,0},{1,17},{17,1},{2,18},{18,2},{3,19},{19,3},{4,20},{20... | collective-permute-start | bytes 884744 | tf_op jit(solution)/shard_map/ppermute | solution.py:82
  501.8 36.8 %collective-permute-start.74 = (bf16[4,24,768]{2,0,1:T(4,128)(2,1)}, bf16[4,24,768]{2,0,1:T(4,128)(2,1)}, u32[]{:S(2)}, u32[]{:S(2)}) collective-permute-start(bf16[4,24,768]{2,0,1:T(4,128)(2,1)} %select_bitcast_fusion.10), channel_id=1, source_target_pairs={{0,16},{16,0},{1,17},{17,1},{2,18},{18,2},{3,19},{19,3},{4,20},{20... | collective-permute-start | bytes 442376 | tf_op jit(solution)/shard_map/ppermute | solution.py:82
  (202 other events, 1572.0 us)
Sparse Core Ops, SparseCore 0:
  44.2 122.1 all-gather.1
  355.9 85.8 reduce-scatter.1

commit v4 on v3

--- a/solution.py
+++ b/solution.py
@@ -320,61 +320,51 @@
     )(role, rows, rel_index)
 
 
-def head_lanes(side):
-    lane = lax.broadcasted_iota(jnp.int32, (1, LANES), 1)
-    return (lane < HEAD_DIM) if side == 0 else (lane >= HEAD_DIM)
-
-
-def attend_pair(query, keys, values, extras):
-    result, logs = None, None
-    for side in (0, 1):
-        mine = head_lanes(side)
-        one = jnp.where(mine, query * SCALE, 0).astype(jnp.bfloat16)
-        scores = times_transposed(one, keys) + extras[side]
-        top = jnp.max(scores, axis=-1, keepdims=True)
-        expo = jnp.exp(scores - top)
-        total = jnp.sum(expo, axis=-1, keepdims=True)
-        found = product(low(expo), values) / total
-        log_total = jnp.broadcast_to(top + jnp.log(total), found.shape)
-        result = found if side == 0 else jnp.where(mine, found, result)
-        logs = log_total if side == 0 else jnp.where(mine, log_total, logs)
-    return low(result), logs
-
-
-def pair_backward(query, keys, values, extras, logs, back_out):
-    back_query, back_keys, back_values, kept = None, None, None, []
-    for side in (0, 1):
-        mine = head_lanes(side)
-        one = jnp.where(mine, query * SCALE, 0).astype(jnp.bfloat16)
-        back_one = jnp.where(mine, back_out, 0).astype(jnp.bfloat16)
-        scores = times_transposed(one, keys) + extras[side]
-        first = side * HEAD_DIM
-        shares = jnp.exp(scores - logs[:, first : first + 1])
-        back_shares = times_transposed(back_one, values)
-        inner = jnp.sum(shares * back_shares, axis=-1, keepdims=True)
-        back_scores = low(shares * (back_shares - inner))
-        found = product(back_scores, keys) * SCALE
-        found_keys = transposed_times(back_scores, one)
-        found_values = transposed_times(low(shares), back_one)
-        kept.append(back_scores)
-        if side == 0:
-            back_query, back_keys, back_values = found, found_keys, found_values
-        else:
-            back_query = jnp.where(mine, found, back_query)
-            back_keys, back_values = back_keys + found_keys, back_values + found_values
-    return low(back_query), low(back_keys), low(back_values), kept
+def both_heads(rows):
+    first = lax.broadcasted_iota(jnp.int32, (1, LANES), 1) < HEAD_DIM
+    blank = jnp.zeros_like(rows)
+    return jnp.concatenate([jnp.where(first, rows, blank), jnp.where(first, blank, rows)])
+
+
+def own_lanes(stacked):
+    rows = stacked.shape[0] // 2
+    first = lax.broadcasted_iota(jnp.int32, (1, LANES), 1) < HEAD_DIM
+    return jnp.where(first, stacked[:rows], stacked[rows:])
+
+
+def attend_pair(query, keys, values, extra):
+    scores = times_transposed(both_heads(query * SCALE), keys) + extra
+    top = jnp.max(scores, axis=-1, keepdims=True)
+    expo = jnp.exp(scores - top)
+    total = jnp.sum(expo, axis=-1, keepdims=True)
+    found = product(low(expo), values) / total
+    return low(own_lanes(found)), own_lanes(jnp.broadcast_to(top + jnp.log(total), found.shape))
+
+
+def pair_backward(query, keys, values, extra, logs, back_out):
+    query, back_out = both_heads(query * SCALE), both_heads(back_out)
+    logs = jnp.concatenate([logs[:, :1], logs[:, HEAD_DIM : HEAD_DIM + 1]])
+    shares = jnp.exp(times_transposed(query, keys) + extra - logs)
+    back_shares = times_transposed(back_out, values)
+    inner = jnp.sum(shares * back_shares, axis=-1, keepdims=True)
+    back_scores = low(shares * (back_shares - inner))
+    back_query = own_lanes(product(back_scores, keys) * SCALE)
+    back_keys = transposed_times(back_scores, query)
+    back_values = transposed_times(low(shares), back_out)
+    return low(back_query), low(back_keys), low(back_values), back_scores
 
 
 def question_extra(slot, role_ref, qid, kid):
     shape = (qid.shape[0], kid.shape[1])
     row = lax.broadcasted_iota(jnp.int32, shape, 0) + role_ref[1 + slot]
     column = lax.broadcasted_iota(jnp.int32, shape, 1)
-    return jnp.where((qid == kid) & (column <= row), 0.0, NEG)
-
-
-def window_extras(bias_ref, qid, kid):
+    extra = jnp.where((qid == kid) & (column <= row), 0.0, NEG)
+    return jnp.concatenate([extra, extra])
+
+
+def window_extra(bias_ref, qid, kid):
     same = jnp.where(qid == kid, 0.0, NEG)
-    return [bias_ref[0] + same, bias_ref[1] + same]
+    return jnp.concatenate([bias_ref[0] + same, bias_ref[1] + same])
 
 
 def self_forward_kernel(
@@ -386,14 +376,14 @@
     def question():
         for s in (0, 1):
             extra = question_extra(s, role_ref, qid_ref[s], kid_ref[s])
-            o_ref[s], log_ref[s] = attend_pair(q_ref[s], k_ref[s], v_ref[s], [extra, extra])
+            o_ref[s], log_ref[s] = attend_pair(q_ref[s], k_ref[s], v_ref[s], extra)
 
     @pl.when(role_ref[0] != 0)
     def visual():
         for s in (0, 1):
-            extras = window_extras(bias_ref, qid_ref[s], kid_ref[s, :, :rows])
+            extra = window_extra(bias_ref, qid_ref[s], kid_ref[s, :, :rows])
             o_ref[s], log_ref[s] = attend_pair(
-                q_ref[s], k_ref[s, :rows], v_ref[s, :rows], extras
+                q_ref[s], k_ref[s, :rows], v_ref[s, :rows], extra
             )
 
 
@@ -420,7 +410,7 @@
         for s in (0, 1):
             extra = question_extra(s, role_ref, qid_ref[s], kid_ref[s])
             dq_ref[s], dk_ref[s], dv_ref[s], unused = pair_backward(
-                q_ref[s], k_ref[s], v_ref[s], [extra, extra], log_ref[s], back_ref[s]
+                q_ref[s], k_ref[s], v_ref[s], extra, log_ref[s], back_ref[s]
             )
 
     @pl.when(role_ref[0] != 0)
@@ -428,14 +418,14 @@
         dk_ref[...] = jnp.zeros_like(dk_ref)
         dv_ref[...] = jnp.zeros_like(dv_ref)
         for s in (0, 1):
-            extras = window_extras(bias_ref, qid_ref[s], kid_ref[s, :, :rows])
+            extra = window_extra(bias_ref, qid_ref[s], kid_ref[s, :, :rows])
             dq_ref[s], found_keys, found_values, kept = pair_backward(
-                q_ref[s], k_ref[s, :rows], v_ref[s, :rows], extras, log_ref[s], back_ref[s]
+                q_ref[s], k_ref[s, :rows], v_ref[s, :rows], extra, log_ref[s], back_ref[s]
             )
             dk_ref[s, :rows] = found_keys
             dv_ref[s, :rows] = found_values
-            ds_ref[0, s] = kept[0]
-            ds_ref[1, s] = kept[1]
+            ds_ref[0, s] = kept[:rows]
+            ds_ref[1, s] = kept[rows:]
 
 
 def self_specs(rows, span):
@@ -497,7 +487,7 @@
 
 def cross_forward_kernel(q_ref, k_ref, v_ref, extra_ref, o_ref, log_ref):
     extra = extra_ref[...]
-    o_ref[0], log_ref[0] = attend_pair(q_ref[0], k_ref[0], v_ref[0], [extra, extra])
+    o_ref[0], log_ref[0] = attend_pair(q_ref[0], k_ref[0], v_ref[0], extra)
 
 
 def cross_backward_kernel(
@@ -505,7 +495,7 @@
 ):
     extra = extra_ref[...]
     dq_ref[0], dk_ref[0], dv_ref[0], unused = pair_backward(
-        q_ref[0], k_ref[0], v_ref[0], [extra, extra], log_ref[0], back_ref[0]
+        q_ref[0], k_ref[0], v_ref[0], extra, log_ref[0], back_ref[0]
     )
 
 
@@ -789,11 +779,9 @@
     later = jnp.concatenate([later, mlp_shards.found], 1)
     later = later.transpose(1, 0, 2, 3).reshape(-1, cut, D)
     later = lax.all_gather(later, ("core", "blk"), axis=1, tiled=True).reshape(-1, D, D)
-    bias = window_bias(role, rel_table, rel_index, 0, 2)
-    bias, rel_table = step([self_ring], [marks], (bias, rel_table))
-    bias_rest = window_bias(role, rel_table, rel_index, 1, 2)
-    bias_rest = step([self_ring], [row_shards], bias_rest)
-    bias = jnp.concatenate([bias, bias_rest])[:, :HEADS].transpose(1, 0, 2)
+    row_shards.away = step([self_ring], [marks], row_shards.away)
+    bias = window_bias(role, rel_table, rel_index, 0, 1)
+    bias = step([self_ring], [row_shards], bias)[:, :HEADS].transpose(1, 0, 2)
     slots, marks = row_shards.found, marks.found
 
     def of_slots(values, starts, size):
@@ -962,10 +950,11 @@
         back_sent = Sum(source_chunk)
         cross_delta = weight_gradients(cross_pairs, blocks)
         back_cross = times_transposed(back_query, cross_query_weight).reshape(2, rows, D)
-        works = [back_cross, cross_delta, (), ()]
+        ready = mlp_shares.ring
+        works = [back_cross, cross_delta, ready.state, ()]
         extra = [[home_out], [], [], []]
         works = [phase([back_sent] + more, work) for work, more in zip(works, extra)]
-        back_cross, cross_delta = works[:2]
+        back_cross, cross_delta, ready.state = works[:3]
         cross_delta = owned(cross_delta)
         back_sent = back_sent.total.reshape(2, rows, D)
     else:

time: 577 us -> 571 us (0.990)
  Pallas kernels: 119 us -> 109 us
  waiting for transfers between devices: 157 us -> 166 us
    ppermute x50, waiting for transfers between devices: 117 us -> 131 us  [phase(): lax.ppermute(parts[0] if len(parts) == 1 else jnp.concatenate(parts), 'bl...]
    ppermute x13, waiting for transfers between devices: 35.7 us -> 29.8 us  [swap_far(): return lax.ppermute(values, 'far', [(0, 1), (1, 0)])]
    unnamed x298 -> x294, local copies, waits for them, and re-layouts: 30.1 us -> 32.4 us
  transfers between devices with their start and end apart: 81 -> 81, of which waited for: 44 -> 48; matrix products, arithmetic and copies ran while one was open for 22% -> 21% of each run, Pallas kernels for 15% -> 13%
where the time goes in v4:
time: 571 us; the launch traced here: 564 us
  waiting for transfers between devices  166 us (29%)
  Pallas kernels  109 us (19%)
  starting transfers between devices  83.2 us (15%)
  local copies, waits for them, and re-layouts  82.2 us (14%)
  other arithmetic  73.9 us (13%)
  matrix products  33.2 us (6%)
  between operations  16.8 us (3%)
    ppermute x50, waiting for transfers between devices, phase(): lax.ppermute(parts[0] if len(parts) == 1 else jnp.concatenate(parts), 'bl...  131 us
    ppermute x50, starting transfers between devices, phase(): lax.ppermute(parts[0] if len(parts) == 1 else jnp.concatenate(parts), 'bl...  53.8 us
    convert_element_type x32, other arithmetic, low(): return values.astype(jnp.bfloat16)  32.7 us
    unnamed x294, local copies, waits for them, and re-layouts  32.4 us
    ppermute x13, waiting for transfers between devices, swap_far(): return lax.ppermute(values, 'far', [(0, 1), (1, 0)])  29.8 us
    ppermute x13, starting transfers between devices, swap_far(): return lax.ppermute(values, 'far', [(0, 1), (1, 0)])  22.7 us
    pallas_call x1, Pallas kernels, cross_backward(): pl.pallas_call(cross_backward_kernel, out_shape=[jax.ShapeDtypeStruct((2,...  20.2 us
    dot_general x8, matrix products, product(): return jnp.dot(left, right, preferred_element_type=jnp.float32)  18.8 us
  transfers between devices with their start and end apart: 81, of which 48 were waited for; matrix products, arithmetic and copies ran while one was open for 21% of the time, Pallas kernels for 13%

profile of v4, /device:TPU:0, one launch (start us, length us, event | category | flops | bytes accessed | tf_op | source)
XLA Modules:
  0.0 564.0 jit_solution(738690383856824110)
XLA Ops:
  34.6 6.3 %collective-permute-done.6 = bf16[8,24,768]{2,0,1:T(8,128)(2,1)S(1)} collective-permute-done((bf16[8,24,768]{2,0,1:T(8,128)(2,1)S(1)}, bf16[8,24,768]{2,0,1:T(8,128)(2,1)S(1)}, u32[]{:S(2)}, u32[]{:S(2)}) %collective-permute-start.6) | collective-permute-done | bytes 294944 | tf_op jit(solution)/shard_map/ppermute | solution.py:82
  55.3 7.3 %collective-permute-done.10.refs_7_ = bf16[1,24,3200]{2,1,0:T(8,128)(2,1)S(1)} collective-permute-done((bf16[1,24,3200]{2,1,0:T(8,128)(2,1)}, bf16[1,24,3200]{2,1,0:T(8,128)(2,1)S(1)}, u32[]{:S(2)}, u32[]{:S(2)}) %collective-permute-start.10) | collective-permute-done | bytes 153632 | tf_op jit(solution)/shard_map/ppermute | solution.py:153
  62.6 5.3 collective-permute-done.11.refs_8_
  95.0 8.2 %shard_map.401 = (bf16[2,144,768]{2,1,0:T(8,128)(2,1)S(1)}, f32[2,144,768]{2,1,0:T(8,128)S(1)}) custom-call(s32[3]{0:T(128)S(1)} %copy-done.52, bf16[2,144,768]{2,1,0:T(8,128)(2,1)S(1)} %bitcast.411, bf16[2,656,768]{2,1,0:T(8,128)(2,1)S(1)} %bitcast.396, bf16[2,656,768]{2,1,0:T(8,128)(2,1)S(1)} %bitcast.394, f32[12,144,144]{2,1,0:T(8,128)S(1)} %slice_bitcast_fusion.bias_ref, ...), custom_call_target="tpu_custom_call" | custom-call | flops 1160773632 | bytes 6045696 | tf_op jit(solution)/shard_map/pallas_call | solution.py:443
  104.4 9.5 %collective-permute-start.22 = (bf16[2,144,768]{2,1,0:T(8,128)(2,1)S(1)}, bf16[2,144,768]{2,1,0:T(8,128)(2,1)S(1)}, u32[]{:S(2)}, u32[]{:S(2)}) collective-permute-start(bf16[2,144,768]{2,1,0:T(8,128)(2,1)S(1)} %add_convert_fusion.4), channel_id=1, source_target_pairs={{0,16},{16,0},{1,17},{17,1},{2,18},{18,2},{3,19},{19,3},{4,20},{20... | collective-permute-start | bytes 1327112 | tf_op jit(solution)/shard_map/ppermute | solution.py:82
  114.9 9.8 %collective-permute-done.22 = bf16[2,144,768]{2,1,0:T(8,128)(2,1)S(1)} collective-permute-done((bf16[2,144,768]{2,1,0:T(8,128)(2,1)S(1)}, bf16[2,144,768]{2,1,0:T(8,128)(2,1)S(1)}, u32[]{:S(2)}, u32[]{:S(2)}) %collective-permute-start.22) | collective-permute-done | bytes 442400 | tf_op jit(solution)/shard_map/ppermute | solution.py:82
  128.8 5.0 collective-permute-done.25
  133.8 8.4 %collective-permute-done.23 = bf16[2,144,768]{2,1,0:T(8,128)(2,1)} collective-permute-done((bf16[2,144,768]{2,1,0:T(8,128)(2,1)S(1)}, bf16[2,144,768]{2,1,0:T(8,128)(2,1)}, u32[]{:S(2)}, u32[]{:S(2)}) %collective-permute-start.23) | collective-permute-done | bytes 442400 | tf_op jit(solution)/shard_map/ppermute | solution.py:153
  142.2 12.2 %collective-permute-done.24 = bf16[2,144,768]{2,1,0:T(8,128)(2,1)S(1)} collective-permute-done((bf16[2,144,768]{2,1,0:T(8,128)(2,1)S(1)}, bf16[2,144,768]{2,1,0:T(8,128)(2,1)S(1)}, u32[]{:S(2)}, u32[]{:S(2)}) %collective-permute-start.24) | collective-permute-done | bytes 442400 | tf_op jit(solution)/shard_map/ppermute | solution.py:153
  161.6 6.8 %collective-permute-done.26 = bf16[2,144,768]{2,1,0:T(8,128)(2,1)S(1)} collective-permute-done((bf16[2,144,768]{2,1,0:T(8,128)(2,1)}, bf16[2,144,768]{2,1,0:T(8,128)(2,1)S(1)}, u32[]{:S(2)}, u32[]{:S(2)}) %collective-permute-start.26) | collective-permute-done | bytes 442400 | tf_op jit(solution)/shard_map/ppermute | solution.py:153
  175.6 6.3 %collective-permute-done.28 = bf16[2,144,768]{2,1,0:T(8,128)(2,1)S(1)} collective-permute-done((bf16[2,144,768]{2,1,0:T(8,128)(2,1)S(1)}, bf16[2,144,768]{2,1,0:T(8,128)(2,1)S(1)}, u32[]{:S(2)}, u32[]{:S(2)}) %collective-permute-start.28) | collective-permute-done | bytes 442400 | tf_op jit(solution)/shard_map/ppermute | solution.py:153
  195.3 5.5 convolution_convert_fusion
  200.8 6.2 %convolution_convert_fusion.1 = bf16[2304,768]{1,0:T(8,128)(2,1)S(1)} fusion(bf16[2304,768]{1,0:T(8,128)(2,1)} %bitcast.53.refs_2_.refs_4_, bf16[768,768]{1,0:T(8,128)(2,1)S(1)} %bitcast.475), kind=kOutput, calls=%fused_computation.2 | convolution fusion | flops 2719678464 | bytes 8257536 | tf_op jit(solution)/shard_map/dot_general | solution.py:29
  207.6 15.3 %shard_map.402 = (bf16[2,144,768]{2,1,0:T(8,128)(2,1)S(1)}, f32[2,144,768]{2,1,0:T(8,128)S(1)}) custom-call(bf16[2,144,768]{2,1,0:T(8,128)(2,1)S(1)} %bitcast.431, bf16[2,1152,768]{2,1,0:T(8,128)(2,1)S(1)} %bitcast.425, bf16[2,1152,768]{2,1,0:T(8,128)(2,1)S(1)} %bitcast.423, f32[1,1152]{1,0:T(1,128)S(1)} %broadcast_select_fusion.12.extra_ref), custom_call_target="tpu_custom_call" | custom-call | flops 4076863488 | bytes 7077888 | tf_op jit(solution)/shard_map/pallas_call | solution.py:516
  224.6 18.1 %shard_map.403 = (f32[288,768]{1,0:T(8,128)S(1)}, f32[288,768]{1,0:T(8,128)S(1)}, bf16[16,8,2,24,768]{4,3,2,1,0:T(8,128)(2,1)}) custom-call(bf16[288,768]{1,0:T(8,128)(2,1)S(1)} %bitcast.410, bf16[288,768]{1,0:T(8,128)(2,1)S(1)} %bitcast.407, bf16[12,768,768]{2,1,0:T(8,128)(2,1)} %bitcast.472, bf16[12,768,768]{2,1,0:T(8,128)(2,1)} %bitcast.473), custom_call_target="tpu_custom_call" | custom-call | flops 8153726976 | bytes 18874368 | tf_op jit(solution)/shard_map/pallas_call | solution.py:602
  242.6 4.8 dynamic-slice_bitcast_fusion
  259.2 20.2 %shard_map.404 = (bf16[2,144,768]{2,1,0:T(8,128)(2,1)S(1)}, bf16[2,1152,768]{2,1,0:T(8,128)(2,1)S(1)}, bf16[2,1152,768]{2,1,0:T(8,128)(2,1)S(1)}) custom-call(bf16[2,144,768]{2,1,0:T(8,128)(2,1)S(1)} %bitcast.432, bf16[2,1152,768]{2,1,0:T(8,128)(2,1)S(1)} %bitcast.426, bf16[2,1152,768]{2,1,0:T(8,128)(2,1)S(1)} %bitcast.424, ...), custom_call_target="tpu_custom_call" | custom-call | flops 10192158720 | bytes 14155776 | tf_op jit(solution)/shard_map/pallas_call | solution.py:535
  291.5 8.0 %collective-permute-done.35 = bf16[384,768]{1,0:T(8,128)(2,1)S(1)} collective-permute-done((bf16[384,768]{1,0:T(8,128)(2,1)S(1)}, bf16[384,768]{1,0:T(8,128)(2,1)S(1)}, u32[]{:S(2)}, u32[]{:S(2)}) %collective-permute-start.35) | collective-permute-done | bytes 589856 | tf_op jit(solution)/shard_map/ppermute | solution.py:153
  310.5 9.7 %shard_map.405 = bf16[16,4,2,24,768]{4,3,2,1,0:T(8,128)(2,1)S(1)} custom-call(bf16[288,768]{1,0:T(8,128)(2,1)S(1)} %bitcast.409, bf16[288,768]{1,0:T(8,128)(2,1)S(1)} %bitcast.406, bf16[2304,768]{1,0:T(8,128)(2,1)} %bitcast.53.refs_2_.refs_4_, bf16[2304,768]{1,0:T(8,128)(2,1)S(1)} %bitcast.428, bf16[2304,768]{1,0:T(8,128)(2,1)} %bitcast.53.refs_2_.refs_4_, ...), custom_call_target="tpu_custom_call" | custom-call | flops 6115295232 | bytes 15925248 | tf_op jit(solution)/shard_map/pallas_call | solution.py:646
  341.5 6.5 %collective-permute-done.46 = bf16[288,768]{1,0:T(8,128)(2,1)S(1)} collective-permute-done((bf16[288,768]{1,0:T(8,128)(2,1)S(1)}, bf16[288,768]{1,0:T(8,128)(2,1)S(1)}, u32[]{:S(2)}, u32[]{:S(2)}) %collective-permute-start.46) | collective-permute-done | bytes 442400 | tf_op jit(solution)/shard_map/ppermute | solution.py:153
  369.4 15.9 %shard_map.406 = (bf16[2,144,768]{2,1,0:T(8,128)(2,1)S(1)}, bf16[2,656,768]{2,1,0:T(8,128)(2,1)S(1)}, bf16[2,656,768]{2,1,0:T(8,128)(2,1)S(1)}, bf16[12,2,144,144]{3,2,1,0:T(8,128)(2,1)S(1)}) custom-call(s32[3]{0:T(128)S(1)} %copy-done.52, bf16[2,144,768]{2,1,0:T(8,128)(2,1)S(1)} %bitcast.412, bf16[2,656,768]{2,1,0:T(8,128)(2,1)S(1)} %bitcast.397, ...), custom_call_target="tpu_custom_call" | custom-call | flops 2901934080 | bytes 8060928 | tf_op jit(solution)/shard_map/pallas_call | solution.py:462
  405.3 6.1 %shard_map.407 = bf16[16,4,2,24,768]{4,3,2,1,0:T(8,128)(2,1)S(1)} custom-call(bf16[288,768]{1,0:T(8,128)(2,1)S(1)} %fusion.25.refs_0_, bf16[288,768]{1,0:T(8,128)(2,1)S(1)} %bitcast.403, bf16[1312,768]{1,0:T(8,128)(2,1)S(1)} %copy-done.3, bf16[1312,768]{1,0:T(8,128)(2,1)S(1)} %bitcast.391, bf16[1312,768]{1,0:T(8,128)(2,1)S(1)} %copy-done.3, ...), custom_call_target="tpu_custom_call" | custom-call | flops 3774873600 | bytes 9830400 | tf_op jit(solution)/shard_map/pallas_call | solution.py:646
  420.4 16.9 %collective-permute-done.54.refs_4_ = bf16[256,768]{1,0:T(8,128)(2,1)S(1)} collective-permute-done((bf16[256,768]{1,0:T(8,128)(2,1)S(1)}, bf16[256,768]{1,0:T(8,128)(2,1)S(1)}, u32[]{:S(2)}, u32[]{:S(2)}) %collective-permute-start.54) | collective-permute-done | bytes 393248 | tf_op jit(solution)/shard_map/ppermute | solution.py:153
  447.2 9.5 %collective-permute-done.57.refs_6_ = bf16[352,768]{1,0:T(8,128)(2,1)S(1)} collective-permute-done((bf16[352,768]{1,0:T(8,128)(2,1)}, bf16[352,768]{1,0:T(8,128)(2,1)S(1)}, u32[]{:S(2)}, u32[]{:S(2)}) %collective-permute-start.57) | collective-permute-done | bytes 540704 | tf_op jit(solution)/shard_map/ppermute | solution.py:153
  (692 shorter events, 319.5 us)
Async XLA Ops:
  7.2 184.4 %all-gather.2.cloned.1.call-start = ((), (), s32[]{:S(2)}) async-start(), calls=%async_computation.1 | async-start | bytes 15040512 | tf_op jit(solution)/shard_map/all_gather | solution.py:781
  42.8 395.6 %reduce-scatter.2.cloned.1.call-start = ((), (), s32[]{:S(2)}) async-start(), calls=%async_computation.2 | async-start | bytes 5013504 | tf_op jit(solution)/shard_map/reduce_scatter | solution.py:936
  45.5 22.4 %collective-permute-start.12 = (bf16[656,768]{1,0:T(8,128)(2,1)}, bf16[656,768]{1,0:T(8,128)(2,1)}, u32[]{:S(2)}, u32[]{:S(2)}) collective-permute-start(bf16[656,768]{1,0:T(8,128)(2,1)} %pad_select_fusion), channel_id=1, source_target_pairs={{0,16},{16,0},{1,17},{17,1},{2,18},{18,2},{3,19},{19,3},{4,20},{20... | collective-permute-start | bytes 3022856 | tf_op jit(solution)/shard_map/ppermute | solution.py:82
  50.7 24.0 %collective-permute-start.13 = (bf16[2,24,3200]{2,1,0:T(8,128)(2,1)}, bf16[2,24,3200]{2,1,0:T(8,128)(2,1)S(1)}, u32[]{:S(2)}, u32[]{:S(2)}) collective-permute-start(bf16[2,24,3200]{2,1,0:T(8,128)(2,1)} %pad_maximum_fusion.13.refs_0_), channel_id=1, source_target_pairs={{0,8},{8,0},{1,9},{9,1},{2,10},{10,2},{3,11},{11,3},{4,12},{12,4},... | collective-permute-start | bytes 921608 | tf_op jit(solution)/shard_map/ppermute | solution.py:86
  50.8 24.8 %collective-permute-start.14 = (bf16[2,24,3200]{2,1,0:T(8,128)(2,1)}, bf16[2,24,3200]{2,1,0:T(8,128)(2,1)}, u32[]{:S(2)}, u32[]{:S(2)}) collective-permute-start(bf16[2,24,3200]{2,1,0:T(8,128)(2,1)} %collective-permute-done.1.refs_1_), channel_id=1, source_target_pairs={{0,8},{8,0},{1,9},{9,1},{2,10},{10,2},{3,11},{11,3},{4,12},{12,4},... | collective-permute-start | bytes 921608 | tf_op jit(solution)/shard_map/ppermute | solution.py:86
  104.4 20.3 %collective-permute-start.22 = (bf16[2,144,768]{2,1,0:T(8,128)(2,1)S(1)}, bf16[2,144,768]{2,1,0:T(8,128)(2,1)S(1)}, u32[]{:S(2)}, u32[]{:S(2)}) collective-permute-start(bf16[2,144,768]{2,1,0:T(8,128)(2,1)S(1)} %add_convert_fusion.4), channel_id=1, source_target_pairs={{0,16},{16,0},{1,17},{17,1},{2,18},{18,2},{3,19},{19,3},{4,20},{20... | collective-permute-start | bytes 1327112 | tf_op jit(solution)/shard_map/ppermute | solution.py:82
  124.7 17.5 %collective-permute-start.23 = (bf16[2,144,768]{2,1,0:T(8,128)(2,1)S(1)}, bf16[2,144,768]{2,1,0:T(8,128)(2,1)}, u32[]{:S(2)}, u32[]{:S(2)}) collective-permute-start(bf16[2,144,768]{2,1,0:T(8,128)(2,1)S(1)} %collective-permute-done.22), channel_id=1, source_target_pairs={{0,2},{2,4},{4,6},{6,7},{7,5},{5,3},{3,1},{1,0},{8,10},{10,12},{12... | collective-permute-start | bytes 1327112 | tf_op jit(solution)/shard_map/ppermute | solution.py:153
  125.5 28.8 %collective-permute-start.24 = (bf16[2,144,768]{2,1,0:T(8,128)(2,1)S(1)}, bf16[2,144,768]{2,1,0:T(8,128)(2,1)S(1)}, u32[]{:S(2)}, u32[]{:S(2)}) collective-permute-start(bf16[2,144,768]{2,1,0:T(8,128)(2,1)S(1)} %collective-permute-done.22), channel_id=1, source_target_pairs={{2,0},{4,2},{6,4},{7,6},{5,7},{3,5},{1,3},{0,1},{10,8},{12,10},{14... | collective-permute-start | bytes 1327112 | tf_op jit(solution)/shard_map/ppermute | solution.py:153
  250.8 54.5 %collective-permute-start.39 = (bf16[144,768]{1,0:T(8,128)(2,1)S(1)}, bf16[144,768]{1,0:T(8,128)(2,1)S(1)}, u32[]{:S(2)}, u32[]{:S(2)}) collective-permute-start(bf16[144,768]{1,0:T(8,128)(2,1)S(1)} %select_bitcast_fusion.5), channel_id=1, source_target_pairs={{0,16},{16,0},{1,17},{17,1},{2,18},{18,2},{3,19},{19,3},{4,20},{20... | collective-permute-start | bytes 663560 | tf_op jit(solution)/shard_map/ppermute | solution.py:82
  257.1 22.3 %collective-permute-start.33 = (bf16[192,768]{1,0:T(8,128)(2,1)S(1)}, bf16[192,768]{1,0:T(8,128)(2,1)S(1)}, u32[]{:S(2)}, u32[]{:S(2)}) collective-permute-start(bf16[192,768]{1,0:T(8,128)(2,1)S(1)} %get-tuple-element.268), channel_id=1, source_target_pairs={{0,2},{2,4},{4,6},{6,7},{7,5},{5,3},{3,1},{1,0},{8,10},{10,12},{12... | collective-permute-start | bytes 884744 | tf_op jit(solution)/shard_map/ppermute | solution.py:153
  257.7 21.8 %collective-permute-start.34 = (bf16[192,768]{1,0:T(8,128)(2,1)S(1)}, bf16[192,768]{1,0:T(8,128)(2,1)S(1)}, u32[]{:S(2)}, u32[]{:S(2)}) collective-permute-start(bf16[192,768]{1,0:T(8,128)(2,1)S(1)} %get-tuple-element.269), channel_id=1, source_target_pairs={{2,0},{4,2},{6,4},{7,6},{5,7},{3,5},{1,3},{0,1},{10,8},{12,10},{14... | collective-permute-start | bytes 884744 | tf_op jit(solution)/shard_map/ppermute | solution.py:153
  284.6 14.9 %collective-permute-start.35 = (bf16[384,768]{1,0:T(8,128)(2,1)S(1)}, bf16[384,768]{1,0:T(8,128)(2,1)S(1)}, u32[]{:S(2)}, u32[]{:S(2)}) collective-permute-start(bf16[384,768]{1,0:T(8,128)(2,1)S(1)} %get-tuple-element.277), channel_id=1, source_target_pairs={{0,2},{2,4},{4,6},{6,7},{7,5},{5,3},{3,1},{1,0},{8,10},{10,12},{12... | collective-permute-start | bytes 1769480 | tf_op jit(solution)/shard_map/ppermute | solution.py:153
  285.1 14.7 %collective-permute-start.36 = (bf16[384,768]{1,0:T(8,128)(2,1)S(1)}, bf16[384,768]{1,0:T(8,128)(2,1)S(1)}, u32[]{:S(2)}, u32[]{:S(2)}) collective-permute-start(bf16[384,768]{1,0:T(8,128)(2,1)S(1)} %get-tuple-element.278), channel_id=1, source_target_pairs={{2,0},{4,2},{6,4},{7,6},{5,7},{3,5},{1,3},{0,1},{10,8},{12,10},{14... | collective-permute-start | bytes 1769480 | tf_op jit(solution)/shard_map/ppermute | solution.py:153
  339.4 15.8 %collective-permute-start.44 = (bf16[384,768]{1,0:T(8,128)(2,1)}, bf16[384,768]{1,0:T(8,128)(2,1)}, u32[]{:S(2)}, u32[]{:S(2)}) collective-permute-start(bf16[384,768]{1,0:T(8,128)(2,1)} %get-tuple-element.299), channel_id=1, source_target_pairs={{0,2},{2,4},{4,6},{6,7},{7,5},{5,3},{3,1},{1,0},{8,10},{10,12},{12... | collective-permute-start | bytes 1769480 | tf_op jit(solution)/shard_map/ppermute | solution.py:153
  340.7 15.8 %collective-permute-start.45 = (bf16[384,768]{1,0:T(8,128)(2,1)}, bf16[384,768]{1,0:T(8,128)(2,1)}, u32[]{:S(2)}, u32[]{:S(2)}) collective-permute-start(bf16[384,768]{1,0:T(8,128)(2,1)} %get-tuple-element.300), channel_id=1, source_target_pairs={{2,0},{4,2},{6,4},{7,6},{5,7},{3,5},{1,3},{0,1},{10,8},{12,10},{14... | collective-permute-start | bytes 1769480 | tf_op jit(solution)/shard_map/ppermute | solution.py:153
  361.5 23.9 %collective-permute-start.49 = (bf16[384,768]{1,0:T(8,128)(2,1)S(1)}, bf16[384,768]{1,0:T(8,128)(2,1)S(1)}, u32[]{:S(2)}, u32[]{:S(2)}) collective-permute-start(bf16[384,768]{1,0:T(8,128)(2,1)S(1)} %get-tuple-element.309), channel_id=1, source_target_pairs={{0,2},{2,4},{4,6},{6,7},{7,5},{5,3},{3,1},{1,0},{8,10},{10,12},{12... | collective-permute-start | bytes 1769480 | tf_op jit(solution)/shard_map/ppermute | solution.py:153
  362.4 23.0 %collective-permute-start.50 = (bf16[384,768]{1,0:T(8,128)(2,1)S(1)}, bf16[384,768]{1,0:T(8,128)(2,1)S(1)}, u32[]{:S(2)}, u32[]{:S(2)}) collective-permute-start(bf16[384,768]{1,0:T(8,128)(2,1)S(1)} %get-tuple-element.310), channel_id=1, source_target_pairs={{2,0},{4,2},{6,4},{7,6},{5,7},{3,5},{1,3},{0,1},{10,8},{12,10},{14... | collective-permute-start | bytes 1769480 | tf_op jit(solution)/shard_map/ppermute | solution.py:153
  392.7 18.7 %collective-permute-start.52 = (bf16[256,768]{1,0:T(8,128)(2,1)}, bf16[256,768]{1,0:T(8,128)(2,1)S(1)}, u32[]{:S(2)}, u32[]{:S(2)}) collective-permute-start(bf16[256,768]{1,0:T(8,128)(2,1)} %pad_maximum_fusion.10), channel_id=1, source_target_pairs={{2,0},{4,2},{6,4},{7,6},{5,7},{3,5},{1,3},{0,1},{10,8},{12,10},{14... | collective-permute-start | bytes 1179656 | tf_op jit(solution)/shard_map/ppermute | solution.py:153
  394.2 17.2 %collective-permute-start.51 = (bf16[256,768]{1,0:T(8,128)(2,1)}, bf16[256,768]{1,0:T(8,128)(2,1)S(1)}, u32[]{:S(2)}, u32[]{:S(2)}) collective-permute-start(bf16[256,768]{1,0:T(8,128)(2,1)} %pad_maximum_fusion.9), channel_id=1, source_target_pairs={{0,2},{2,4},{4,6},{6,7},{7,5},{5,3},{3,1},{1,0},{8,10},{10,12},{12... | collective-permute-start | bytes 1179656 | tf_op jit(solution)/shard_map/ppermute | solution.py:153
  414.3 23.0 %collective-permute-start.55 = (bf16[8,192,768]{2,1,0:T(8,128)(2,1)}, bf16[8,192,768]{2,1,0:T(8,128)(2,1)}, u32[]{:S(2)}, u32[]{:S(2)}) collective-permute-start(bf16[8,192,768]{2,1,0:T(8,128)(2,1)} %dynamic-slice_bitcast_fusion.1), channel_id=1, source_target_pairs={{0,8},{8,0},{1,9},{9,1},{2,10},{10,2},{3,11},{11,3},{4,12},{12,4},... | collective-permute-start | bytes 7077896 | tf_op jit(solution)/shard_map/ppermute | solution.py:86
  416.6 20.7 %collective-permute-start.54 = (bf16[256,768]{1,0:T(8,128)(2,1)S(1)}, bf16[256,768]{1,0:T(8,128)(2,1)S(1)}, u32[]{:S(2)}, u32[]{:S(2)}) collective-permute-start(bf16[256,768]{1,0:T(8,128)(2,1)S(1)} %pad_maximum_fusion.12), channel_id=1, source_target_pairs={{2,0},{4,2},{6,4},{7,6},{5,7},{3,5},{1,3},{0,1},{10,8},{12,10},{14... | collective-permute-start | bytes 1179656 | tf_op jit(solution)/shard_map/ppermute | solution.py:153
  417.5 19.8 %collective-permute-start.53 = (bf16[256,768]{1,0:T(8,128)(2,1)S(1)}, bf16[256,768]{1,0:T(8,128)(2,1)S(1)}, u32[]{:S(2)}, u32[]{:S(2)}) collective-permute-start(bf16[256,768]{1,0:T(8,128)(2,1)S(1)} %pad_maximum_fusion.11), channel_id=1, source_target_pairs={{0,2},{2,4},{4,6},{6,7},{7,5},{5,3},{3,1},{1,0},{8,10},{10,12},{12... | collective-permute-start | bytes 1179656 | tf_op jit(solution)/shard_map/ppermute | solution.py:153
  470.7 27.1 %collective-permute-start.63 = (bf16[8,24,768]{2,0,1:T(8,128)(2,1)}, bf16[8,24,768]{2,0,1:T(8,128)(2,1)}, u32[]{:S(2)}, u32[]{:S(2)}) collective-permute-start(bf16[8,24,768]{2,0,1:T(8,128)(2,1)} %fusion.51), channel_id=1, source_target_pairs={{0,16},{16,0},{1,17},{17,1},{2,18},{18,2},{3,19},{19,3},{4,20},{20... | collective-permute-start | bytes 884744 | tf_op jit(solution)/shard_map/ppermute | solution.py:82
  497.8 35.9 %collective-permute-start.74 = (bf16[4,24,768]{2,0,1:T(4,128)(2,1)}, bf16[4,24,768]{2,0,1:T(4,128)(2,1)}, u32[]{:S(2)}, u32[]{:S(2)}) collective-permute-start(bf16[4,24,768]{2,0,1:T(4,128)(2,1)} %select_bitcast_fusion.10), channel_id=1, source_target_pairs={{0,16},{16,0},{1,17},{17,1},{2,18},{18,2},{3,19},{19,3},{4,20},{20... | collective-permute-start | bytes 442376 | tf_op jit(solution)/shard_map/ppermute | solution.py:82
  (200 other events, 1491.1 us)
Sparse Core Ops, SparseCore 0:
  42.9 122.9 all-gather.1
  352.4 85.9 reduce-scatter.1

commit v5 on v4

--- a/solution.py
+++ b/solution.py
@@ -1030,13 +1030,13 @@
     table_parts = [table_sums(role, score_rows, rel_index, part, 4) for part in range(4)]
     self_delta, table_parts[0] = phase([chain] + outs, (self_delta, table_parts[0]))
     self_shares = Shares(self_delta)
-    table_parts[1], cross_delta = phase(
-        [chain, self_shares.swap] + outs, (table_parts[1], cross_delta)
-    )
+    table_parts[1] = phase([chain, self_shares.swap] + outs, table_parts[1])
     self_shares.start()
     sums = self_shares.rings()
     for number in range(early - 2):
         work = table_parts[2 + number] if number < 2 else ()
+        if number == 0:
+            work, cross_delta = lax.optimization_barrier((work, cross_delta))
         work = phase([chain] + (outs + sums if number < 2 else []), work)
         if number < 2:
             table_parts[2 + number] = work

time: 571 us -> 571 us (level)
    unnamed x294 -> x296, local copies, waits for them, and re-layouts: 32.4 us -> 33 us
  transfers between devices with their start and end apart: 81 -> 81, of which waited for: 48 -> 47; matrix products, arithmetic and copies ran while one was open for 21% -> 22% of each run, Pallas kernels for 13% -> 13%
where the time goes in v5:
time: 571 us; the launch traced here: 563 us
  waiting for transfers between devices  165 us (29%)
  Pallas kernels  109 us (19%)
  local copies, waits for them, and re-layouts  82.8 us (15%)
  starting transfers between devices  82.6 us (14%)
  other arithmetic  74.2 us (13%)
  matrix products  33.1 us (6%)
  between operations  16.8 us (3%)
    ppermute x50, waiting for transfers between devices, phase(): lax.ppermute(parts[0] if len(parts) == 1 else jnp.concatenate(parts), 'bl...  131 us
    ppermute x50, starting transfers between devices, phase(): lax.ppermute(parts[0] if len(parts) == 1 else jnp.concatenate(parts), 'bl...  53.8 us
    unnamed x296, local copies, waits for them, and re-layouts  33 us
    convert_element_type x32, other arithmetic, low(): return values.astype(jnp.bfloat16)  31.5 us
    ppermute x13, waiting for transfers between devices, swap_far(): return lax.ppermute(values, 'far', [(0, 1), (1, 0)])  29.8 us
    ppermute x13, starting transfers between devices, swap_far(): return lax.ppermute(values, 'far', [(0, 1), (1, 0)])  22.5 us
    pallas_call x1, Pallas kernels, cross_backward(): pl.pallas_call(cross_backward_kernel, out_shape=[jax.ShapeDtypeStruct((2,...  20.2 us
    dot_general x8, matrix products, product(): return jnp.dot(left, right, preferred_element_type=jnp.float32)  18.8 us
  transfers between devices with their start and end apart: 81, of which 47 were waited for; matrix products, arithmetic and copies ran while one was open for 22% of the time, Pallas kernels for 13%

profile of v5, /device:TPU:0, one launch (start us, length us, event | category | flops | bytes accessed | tf_op | source)
XLA Modules:
  0.0 563.4 jit_solution(10338539234052646281)
XLA Ops:
  34.6 6.3 %collective-permute-done.6 = bf16[8,24,768]{2,0,1:T(8,128)(2,1)S(1)} collective-permute-done((bf16[8,24,768]{2,0,1:T(8,128)(2,1)S(1)}, bf16[8,24,768]{2,0,1:T(8,128)(2,1)S(1)}, u32[]{:S(2)}, u32[]{:S(2)}) %collective-permute-start.6) | collective-permute-done | bytes 294944 | tf_op jit(solution)/shard_map/ppermute | solution.py:82
  55.3 7.3 %collective-permute-done.10.refs_7_ = bf16[1,24,3200]{2,1,0:T(8,128)(2,1)S(1)} collective-permute-done((bf16[1,24,3200]{2,1,0:T(8,128)(2,1)}, bf16[1,24,3200]{2,1,0:T(8,128)(2,1)S(1)}, u32[]{:S(2)}, u32[]{:S(2)}) %collective-permute-start.10) | collective-permute-done | bytes 153632 | tf_op jit(solution)/shard_map/ppermute | solution.py:153
  62.6 5.3 collective-permute-done.11.refs_8_
  95.0 8.2 %shard_map.401 = (bf16[2,144,768]{2,1,0:T(8,128)(2,1)S(1)}, f32[2,144,768]{2,1,0:T(8,128)S(1)}) custom-call(s32[3]{0:T(128)S(1)} %copy-done.52, bf16[2,144,768]{2,1,0:T(8,128)(2,1)S(1)} %bitcast.411, bf16[2,656,768]{2,1,0:T(8,128)(2,1)S(1)} %bitcast.396, bf16[2,656,768]{2,1,0:T(8,128)(2,1)S(1)} %bitcast.394, f32[12,144,144]{2,1,0:T(8,128)S(1)} %slice_bitcast_fusion.bias_ref, ...), custom_call_target="tpu_custom_call" | custom-call | flops 1160773632 | bytes 6045696 | tf_op jit(solution)/shard_map/pallas_call | solution.py:443
  104.4 9.5 %collective-permute-start.22 = (bf16[2,144,768]{2,1,0:T(8,128)(2,1)S(1)}, bf16[2,144,768]{2,1,0:T(8,128)(2,1)S(1)}, u32[]{:S(2)}, u32[]{:S(2)}) collective-permute-start(bf16[2,144,768]{2,1,0:T(8,128)(2,1)S(1)} %add_convert_fusion.4), channel_id=1, source_target_pairs={{0,16},{16,0},{1,17},{17,1},{2,18},{18,2},{3,19},{19,3},{4,20},{20... | collective-permute-start | bytes 1327112 | tf_op jit(solution)/shard_map/ppermute | solution.py:82
  114.9 9.8 %collective-permute-done.22 = bf16[2,144,768]{2,1,0:T(8,128)(2,1)S(1)} collective-permute-done((bf16[2,144,768]{2,1,0:T(8,128)(2,1)S(1)}, bf16[2,144,768]{2,1,0:T(8,128)(2,1)S(1)}, u32[]{:S(2)}, u32[]{:S(2)}) %collective-permute-start.22) | collective-permute-done | bytes 442400 | tf_op jit(solution)/shard_map/ppermute | solution.py:82
  128.8 5.0 collective-permute-done.25
  133.8 8.4 %collective-permute-done.23 = bf16[2,144,768]{2,1,0:T(8,128)(2,1)} collective-permute-done((bf16[2,144,768]{2,1,0:T(8,128)(2,1)S(1)}, bf16[2,144,768]{2,1,0:T(8,128)(2,1)}, u32[]{:S(2)}, u32[]{:S(2)}) %collective-permute-start.23) | collective-permute-done | bytes 442400 | tf_op jit(solution)/shard_map/ppermute | solution.py:153
  142.2 12.2 %collective-permute-done.24 = bf16[2,144,768]{2,1,0:T(8,128)(2,1)S(1)} collective-permute-done((bf16[2,144,768]{2,1,0:T(8,128)(2,1)S(1)}, bf16[2,144,768]{2,1,0:T(8,128)(2,1)S(1)}, u32[]{:S(2)}, u32[]{:S(2)}) %collective-permute-start.24) | collective-permute-done | bytes 442400 | tf_op jit(solution)/shard_map/ppermute | solution.py:153
  161.6 6.8 %collective-permute-done.26 = bf16[2,144,768]{2,1,0:T(8,128)(2,1)S(1)} collective-permute-done((bf16[2,144,768]{2,1,0:T(8,128)(2,1)}, bf16[2,144,768]{2,1,0:T(8,128)(2,1)S(1)}, u32[]{:S(2)}, u32[]{:S(2)}) %collective-permute-start.26) | collective-permute-done | bytes 442400 | tf_op jit(solution)/shard_map/ppermute | solution.py:153
  175.6 6.3 %collective-permute-done.28 = bf16[2,144,768]{2,1,0:T(8,128)(2,1)S(1)} collective-permute-done((bf16[2,144,768]{2,1,0:T(8,128)(2,1)S(1)}, bf16[2,144,768]{2,1,0:T(8,128)(2,1)S(1)}, u32[]{:S(2)}, u32[]{:S(2)}) %collective-permute-start.28) | collective-permute-done | bytes 442400 | tf_op jit(solution)/shard_map/ppermute | solution.py:153
  195.3 5.5 convolution_convert_fusion
  200.8 6.2 %convolution_convert_fusion.1 = bf16[2304,768]{1,0:T(8,128)(2,1)S(1)} fusion(bf16[2304,768]{1,0:T(8,128)(2,1)} %bitcast.53.refs_2_.refs_4_, bf16[768,768]{1,0:T(8,128)(2,1)S(1)} %bitcast.475), kind=kOutput, calls=%fused_computation.2 | convolution fusion | flops 2719678464 | bytes 8257536 | tf_op jit(solution)/shard_map/dot_general | solution.py:29
  207.6 15.3 %shard_map.402 = (bf16[2,144,768]{2,1,0:T(8,128)(2,1)S(1)}, f32[2,144,768]{2,1,0:T(8,128)S(1)}) custom-call(bf16[2,144,768]{2,1,0:T(8,128)(2,1)S(1)} %bitcast.431, bf16[2,1152,768]{2,1,0:T(8,128)(2,1)S(1)} %bitcast.425, bf16[2,1152,768]{2,1,0:T(8,128)(2,1)S(1)} %bitcast.423, f32[1,1152]{1,0:T(1,128)S(1)} %broadcast_select_fusion.12.extra_ref), custom_call_target="tpu_custom_call" | custom-call | flops 4076863488 | bytes 7077888 | tf_op jit(solution)/shard_map/pallas_call | solution.py:516
  224.5 18.1 %shard_map.403 = (f32[288,768]{1,0:T(8,128)S(1)}, f32[288,768]{1,0:T(8,128)S(1)}, bf16[16,8,2,24,768]{4,3,2,1,0:T(8,128)(2,1)}) custom-call(bf16[288,768]{1,0:T(8,128)(2,1)S(1)} %bitcast.410, bf16[288,768]{1,0:T(8,128)(2,1)S(1)} %bitcast.407, bf16[12,768,768]{2,1,0:T(8,128)(2,1)} %bitcast.472, bf16[12,768,768]{2,1,0:T(8,128)(2,1)} %bitcast.473), custom_call_target="tpu_custom_call" | custom-call | flops 8153726976 | bytes 18874368 | tf_op jit(solution)/shard_map/pallas_call | solution.py:602
  242.6 4.8 dynamic-slice_bitcast_fusion
  259.2 20.2 %shard_map.404 = (bf16[2,144,768]{2,1,0:T(8,128)(2,1)S(1)}, bf16[2,1152,768]{2,1,0:T(8,128)(2,1)S(1)}, bf16[2,1152,768]{2,1,0:T(8,128)(2,1)S(1)}) custom-call(bf16[2,144,768]{2,1,0:T(8,128)(2,1)S(1)} %bitcast.432, bf16[2,1152,768]{2,1,0:T(8,128)(2,1)S(1)} %bitcast.426, bf16[2,1152,768]{2,1,0:T(8,128)(2,1)S(1)} %bitcast.424, ...), custom_call_target="tpu_custom_call" | custom-call | flops 10192158720 | bytes 14155776 | tf_op jit(solution)/shard_map/pallas_call | solution.py:535
  291.4 8.0 %collective-permute-done.35 = bf16[384,768]{1,0:T(8,128)(2,1)S(1)} collective-permute-done((bf16[384,768]{1,0:T(8,128)(2,1)S(1)}, bf16[384,768]{1,0:T(8,128)(2,1)S(1)}, u32[]{:S(2)}, u32[]{:S(2)}) %collective-permute-start.35) | collective-permute-done | bytes 589856 | tf_op jit(solution)/shard_map/ppermute | solution.py:153
  310.5 9.5 %shard_map.405 = bf16[16,4,2,24,768]{4,3,2,1,0:T(8,128)(2,1)S(1)} custom-call(bf16[288,768]{1,0:T(8,128)(2,1)S(1)} %bitcast.409, bf16[288,768]{1,0:T(8,128)(2,1)S(1)} %bitcast.406, bf16[2304,768]{1,0:T(8,128)(2,1)} %bitcast.53.refs_2_.refs_4_, bf16[2304,768]{1,0:T(8,128)(2,1)S(1)} %bitcast.428, bf16[2304,768]{1,0:T(8,128)(2,1)} %bitcast.53.refs_2_.refs_4_, ...), custom_call_target="tpu_custom_call" | custom-call | flops 6115295232 | bytes 15925248 | tf_op jit(solution)/shard_map/pallas_call | solution.py:646
  341.2 6.6 %collective-permute-done.46 = bf16[288,768]{1,0:T(8,128)(2,1)S(1)} collective-permute-done((bf16[288,768]{1,0:T(8,128)(2,1)S(1)}, bf16[288,768]{1,0:T(8,128)(2,1)S(1)}, u32[]{:S(2)}, u32[]{:S(2)}) %collective-permute-start.46) | collective-permute-done | bytes 442400 | tf_op jit(solution)/shard_map/ppermute | solution.py:153
  370.0 15.9 %shard_map.406 = (bf16[2,144,768]{2,1,0:T(8,128)(2,1)S(1)}, bf16[2,656,768]{2,1,0:T(8,128)(2,1)S(1)}, bf16[2,656,768]{2,1,0:T(8,128)(2,1)S(1)}, bf16[12,2,144,144]{3,2,1,0:T(8,128)(2,1)S(1)}) custom-call(s32[3]{0:T(128)S(1)} %copy-done.52, bf16[2,144,768]{2,1,0:T(8,128)(2,1)S(1)} %bitcast.412, bf16[2,656,768]{2,1,0:T(8,128)(2,1)S(1)} %bitcast.397, ...), custom_call_target="tpu_custom_call" | custom-call | flops 2901934080 | bytes 8060928 | tf_op jit(solution)/shard_map/pallas_call | solution.py:462
  405.9 6.1 %shard_map.407 = bf16[16,4,2,24,768]{4,3,2,1,0:T(8,128)(2,1)S(1)} custom-call(bf16[288,768]{1,0:T(8,128)(2,1)S(1)} %fusion.25.refs_0_, bf16[288,768]{1,0:T(8,128)(2,1)S(1)} %bitcast.403, bf16[1312,768]{1,0:T(8,128)(2,1)S(1)} %copy-done.3, bf16[1312,768]{1,0:T(8,128)(2,1)S(1)} %bitcast.391, bf16[1312,768]{1,0:T(8,128)(2,1)S(1)} %copy-done.3, ...), custom_call_target="tpu_custom_call" | custom-call | flops 3774873600 | bytes 9830400 | tf_op jit(solution)/shard_map/pallas_call | solution.py:646
  421.0 16.4 %collective-permute-done.54.refs_4_ = bf16[256,768]{1,0:T(8,128)(2,1)S(1)} collective-permute-done((bf16[256,768]{1,0:T(8,128)(2,1)S(1)}, bf16[256,768]{1,0:T(8,128)(2,1)S(1)}, u32[]{:S(2)}, u32[]{:S(2)}) %collective-permute-start.54) | collective-permute-done | bytes 393248 | tf_op jit(solution)/shard_map/ppermute | solution.py:153
  446.5 9.9 %collective-permute-done.57.refs_6_ = bf16[352,768]{1,0:T(8,128)(2,1)S(1)} collective-permute-done((bf16[352,768]{1,0:T(8,128)(2,1)}, bf16[352,768]{1,0:T(8,128)(2,1)S(1)}, u32[]{:S(2)}, u32[]{:S(2)}) %collective-permute-start.57) | collective-permute-done | bytes 540704 | tf_op jit(solution)/shard_map/ppermute | solution.py:153
  (694 shorter events, 319.0 us)
Async XLA Ops:
  7.2 184.4 %all-gather.2.cloned.1.call-start = ((), (), s32[]{:S(2)}) async-start(), calls=%async_computation.1 | async-start | bytes 15040512 | tf_op jit(solution)/shard_map/all_gather | solution.py:781
  42.8 403.7 %reduce-scatter.2.cloned.1.call-start = ((), (), s32[]{:S(2)}) async-start(), calls=%async_computation.2 | async-start | bytes 5013504 | tf_op jit(solution)/shard_map/reduce_scatter | solution.py:936
  45.5 22.4 %collective-permute-start.12 = (bf16[656,768]{1,0:T(8,128)(2,1)}, bf16[656,768]{1,0:T(8,128)(2,1)}, u32[]{:S(2)}, u32[]{:S(2)}) collective-permute-start(bf16[656,768]{1,0:T(8,128)(2,1)} %pad_select_fusion), channel_id=1, source_target_pairs={{0,16},{16,0},{1,17},{17,1},{2,18},{18,2},{3,19},{19,3},{4,20},{20... | collective-permute-start | bytes 3022856 | tf_op jit(solution)/shard_map/ppermute | solution.py:82
  50.7 24.0 %collective-permute-start.13 = (bf16[2,24,3200]{2,1,0:T(8,128)(2,1)}, bf16[2,24,3200]{2,1,0:T(8,128)(2,1)S(1)}, u32[]{:S(2)}, u32[]{:S(2)}) collective-permute-start(bf16[2,24,3200]{2,1,0:T(8,128)(2,1)} %pad_maximum_fusion.13.refs_0_), channel_id=1, source_target_pairs={{0,8},{8,0},{1,9},{9,1},{2,10},{10,2},{3,11},{11,3},{4,12},{12,4},... | collective-permute-start | bytes 921608 | tf_op jit(solution)/shard_map/ppermute | solution.py:86
  50.8 24.8 %collective-permute-start.14 = (bf16[2,24,3200]{2,1,0:T(8,128)(2,1)}, bf16[2,24,3200]{2,1,0:T(8,128)(2,1)}, u32[]{:S(2)}, u32[]{:S(2)}) collective-permute-start(bf16[2,24,3200]{2,1,0:T(8,128)(2,1)} %collective-permute-done.1.refs_1_), channel_id=1, source_target_pairs={{0,8},{8,0},{1,9},{9,1},{2,10},{10,2},{3,11},{11,3},{4,12},{12,4},... | collective-permute-start | bytes 921608 | tf_op jit(solution)/shard_map/ppermute | solution.py:86
  104.4 20.3 %collective-permute-start.22 = (bf16[2,144,768]{2,1,0:T(8,128)(2,1)S(1)}, bf16[2,144,768]{2,1,0:T(8,128)(2,1)S(1)}, u32[]{:S(2)}, u32[]{:S(2)}) collective-permute-start(bf16[2,144,768]{2,1,0:T(8,128)(2,1)S(1)} %add_convert_fusion.4), channel_id=1, source_target_pairs={{0,16},{16,0},{1,17},{17,1},{2,18},{18,2},{3,19},{19,3},{4,20},{20... | collective-permute-start | bytes 1327112 | tf_op jit(solution)/shard_map/ppermute | solution.py:82
  124.7 17.5 %collective-permute-start.23 = (bf16[2,144,768]{2,1,0:T(8,128)(2,1)S(1)}, bf16[2,144,768]{2,1,0:T(8,128)(2,1)}, u32[]{:S(2)}, u32[]{:S(2)}) collective-permute-start(bf16[2,144,768]{2,1,0:T(8,128)(2,1)S(1)} %collective-permute-done.22), channel_id=1, source_target_pairs={{0,2},{2,4},{4,6},{6,7},{7,5},{5,3},{3,1},{1,0},{8,10},{10,12},{12... | collective-permute-start | bytes 1327112 | tf_op jit(solution)/shard_map/ppermute | solution.py:153
  125.5 28.8 %collective-permute-start.24 = (bf16[2,144,768]{2,1,0:T(8,128)(2,1)S(1)}, bf16[2,144,768]{2,1,0:T(8,128)(2,1)S(1)}, u32[]{:S(2)}, u32[]{:S(2)}) collective-permute-start(bf16[2,144,768]{2,1,0:T(8,128)(2,1)S(1)} %collective-permute-done.22), channel_id=1, source_target_pairs={{2,0},{4,2},{6,4},{7,6},{5,7},{3,5},{1,3},{0,1},{10,8},{12,10},{14... | collective-permute-start | bytes 1327112 | tf_op jit(solution)/shard_map/ppermute | solution.py:153
  250.8 54.5 %collective-permute-start.39 = (bf16[144,768]{1,0:T(8,128)(2,1)S(1)}, bf16[144,768]{1,0:T(8,128)(2,1)S(1)}, u32[]{:S(2)}, u32[]{:S(2)}) collective-permute-start(bf16[144,768]{1,0:T(8,128)(2,1)S(1)} %select_bitcast_fusion.5), channel_id=1, source_target_pairs={{0,16},{16,0},{1,17},{17,1},{2,18},{18,2},{3,19},{19,3},{4,20},{20... | collective-permute-start | bytes 663560 | tf_op jit(solution)/shard_map/ppermute | solution.py:82
  257.1 22.3 %collective-permute-start.33 = (bf16[192,768]{1,0:T(8,128)(2,1)S(1)}, bf16[192,768]{1,0:T(8,128)(2,1)S(1)}, u32[]{:S(2)}, u32[]{:S(2)}) collective-permute-start(bf16[192,768]{1,0:T(8,128)(2,1)S(1)} %get-tuple-element.269), channel_id=1, source_target_pairs={{0,2},{2,4},{4,6},{6,7},{7,5},{5,3},{3,1},{1,0},{8,10},{10,12},{12... | collective-permute-start | bytes 884744 | tf_op jit(solution)/shard_map/ppermute | solution.py:153
  257.7 21.8 %collective-permute-start.34 = (bf16[192,768]{1,0:T(8,128)(2,1)S(1)}, bf16[192,768]{1,0:T(8,128)(2,1)S(1)}, u32[]{:S(2)}, u32[]{:S(2)}) collective-permute-start(bf16[192,768]{1,0:T(8,128)(2,1)S(1)} %get-tuple-element.270), channel_id=1, source_target_pairs={{2,0},{4,2},{6,4},{7,6},{5,7},{3,5},{1,3},{0,1},{10,8},{12,10},{14... | collective-permute-start | bytes 884744 | tf_op jit(solution)/shard_map/ppermute | solution.py:153
  284.5 14.9 %collective-permute-start.35 = (bf16[384,768]{1,0:T(8,128)(2,1)S(1)}, bf16[384,768]{1,0:T(8,128)(2,1)S(1)}, u32[]{:S(2)}, u32[]{:S(2)}) collective-permute-start(bf16[384,768]{1,0:T(8,128)(2,1)S(1)} %get-tuple-element.278), channel_id=1, source_target_pairs={{0,2},{2,4},{4,6},{6,7},{7,5},{5,3},{3,1},{1,0},{8,10},{10,12},{12... | collective-permute-start | bytes 1769480 | tf_op jit(solution)/shard_map/ppermute | solution.py:153
  285.1 14.7 %collective-permute-start.36 = (bf16[384,768]{1,0:T(8,128)(2,1)S(1)}, bf16[384,768]{1,0:T(8,128)(2,1)S(1)}, u32[]{:S(2)}, u32[]{:S(2)}) collective-permute-start(bf16[384,768]{1,0:T(8,128)(2,1)S(1)} %get-tuple-element.279), channel_id=1, source_target_pairs={{2,0},{4,2},{6,4},{7,6},{5,7},{3,5},{1,3},{0,1},{10,8},{12,10},{14... | collective-permute-start | bytes 1769480 | tf_op jit(solution)/shard_map/ppermute | solution.py:153
  339.2 15.8 %collective-permute-start.44 = (bf16[384,768]{1,0:T(8,128)(2,1)}, bf16[384,768]{1,0:T(8,128)(2,1)}, u32[]{:S(2)}, u32[]{:S(2)}) collective-permute-start(bf16[384,768]{1,0:T(8,128)(2,1)} %get-tuple-element.300), channel_id=1, source_target_pairs={{0,2},{2,4},{4,6},{6,7},{7,5},{5,3},{3,1},{1,0},{8,10},{10,12},{12... | collective-permute-start | bytes 1769480 | tf_op jit(solution)/shard_map/ppermute | solution.py:153
  340.5 15.8 %collective-permute-start.45 = (bf16[384,768]{1,0:T(8,128)(2,1)}, bf16[384,768]{1,0:T(8,128)(2,1)}, u32[]{:S(2)}, u32[]{:S(2)}) collective-permute-start(bf16[384,768]{1,0:T(8,128)(2,1)} %get-tuple-element.301), channel_id=1, source_target_pairs={{2,0},{4,2},{6,4},{7,6},{5,7},{3,5},{1,3},{0,1},{10,8},{12,10},{14... | collective-permute-start | bytes 1769480 | tf_op jit(solution)/shard_map/ppermute | solution.py:153
  364.0 22.0 %collective-permute-start.49 = (bf16[384,768]{1,0:T(8,128)(2,1)S(1)}, bf16[384,768]{1,0:T(8,128)(2,1)S(1)}, u32[]{:S(2)}, u32[]{:S(2)}) collective-permute-start(bf16[384,768]{1,0:T(8,128)(2,1)S(1)} %get-tuple-element.310), channel_id=1, source_target_pairs={{0,2},{2,4},{4,6},{6,7},{7,5},{5,3},{3,1},{1,0},{8,10},{10,12},{12... | collective-permute-start | bytes 1769480 | tf_op jit(solution)/shard_map/ppermute | solution.py:153
  365.0 21.0 %collective-permute-start.50 = (bf16[384,768]{1,0:T(8,128)(2,1)S(1)}, bf16[384,768]{1,0:T(8,128)(2,1)S(1)}, u32[]{:S(2)}, u32[]{:S(2)}) collective-permute-start(bf16[384,768]{1,0:T(8,128)(2,1)S(1)} %get-tuple-element.311), channel_id=1, source_target_pairs={{2,0},{4,2},{6,4},{7,6},{5,7},{3,5},{1,3},{0,1},{10,8},{12,10},{14... | collective-permute-start | bytes 1769480 | tf_op jit(solution)/shard_map/ppermute | solution.py:153
  393.3 18.7 %collective-permute-start.52 = (bf16[256,768]{1,0:T(8,128)(2,1)}, bf16[256,768]{1,0:T(8,128)(2,1)S(1)}, u32[]{:S(2)}, u32[]{:S(2)}) collective-permute-start(bf16[256,768]{1,0:T(8,128)(2,1)} %pad_maximum_fusion.10), channel_id=1, source_target_pairs={{2,0},{4,2},{6,4},{7,6},{5,7},{3,5},{1,3},{0,1},{10,8},{12,10},{14... | collective-permute-start | bytes 1179656 | tf_op jit(solution)/shard_map/ppermute | solution.py:153
  394.8 17.2 %collective-permute-start.51 = (bf16[256,768]{1,0:T(8,128)(2,1)}, bf16[256,768]{1,0:T(8,128)(2,1)S(1)}, u32[]{:S(2)}, u32[]{:S(2)}) collective-permute-start(bf16[256,768]{1,0:T(8,128)(2,1)} %pad_maximum_fusion.9), channel_id=1, source_target_pairs={{0,2},{2,4},{4,6},{6,7},{7,5},{5,3},{3,1},{1,0},{8,10},{10,12},{12... | collective-permute-start | bytes 1179656 | tf_op jit(solution)/shard_map/ppermute | solution.py:153
  414.9 22.6 %collective-permute-start.55 = (bf16[8,192,768]{2,1,0:T(8,128)(2,1)}, bf16[8,192,768]{2,1,0:T(8,128)(2,1)}, u32[]{:S(2)}, u32[]{:S(2)}) collective-permute-start(bf16[8,192,768]{2,1,0:T(8,128)(2,1)} %dynamic-slice_bitcast_fusion.1), channel_id=1, source_target_pairs={{0,8},{8,0},{1,9},{9,1},{2,10},{10,2},{3,11},{11,3},{4,12},{12,4},... | collective-permute-start | bytes 7077896 | tf_op jit(solution)/shard_map/ppermute | solution.py:86
  417.2 20.3 %collective-permute-start.54 = (bf16[256,768]{1,0:T(8,128)(2,1)S(1)}, bf16[256,768]{1,0:T(8,128)(2,1)S(1)}, u32[]{:S(2)}, u32[]{:S(2)}) collective-permute-start(bf16[256,768]{1,0:T(8,128)(2,1)S(1)} %pad_maximum_fusion.12), channel_id=1, source_target_pairs={{2,0},{4,2},{6,4},{7,6},{5,7},{3,5},{1,3},{0,1},{10,8},{12,10},{14... | collective-permute-start | bytes 1179656 | tf_op jit(solution)/shard_map/ppermute | solution.py:153
  418.0 19.5 %collective-permute-start.53 = (bf16[256,768]{1,0:T(8,128)(2,1)S(1)}, bf16[256,768]{1,0:T(8,128)(2,1)S(1)}, u32[]{:S(2)}, u32[]{:S(2)}) collective-permute-start(bf16[256,768]{1,0:T(8,128)(2,1)S(1)} %pad_maximum_fusion.11), channel_id=1, source_target_pairs={{0,2},{2,4},{4,6},{6,7},{7,5},{5,3},{3,1},{1,0},{8,10},{10,12},{12... | collective-permute-start | bytes 1179656 | tf_op jit(solution)/shard_map/ppermute | solution.py:153
  470.0 27.1 %collective-permute-start.63 = (bf16[8,24,768]{2,0,1:T(8,128)(2,1)}, bf16[8,24,768]{2,0,1:T(8,128)(2,1)}, u32[]{:S(2)}, u32[]{:S(2)}) collective-permute-start(bf16[8,24,768]{2,0,1:T(8,128)(2,1)} %fusion.51), channel_id=1, source_target_pairs={{0,16},{16,0},{1,17},{17,1},{2,18},{18,2},{3,19},{19,3},{4,20},{20... | collective-permute-start | bytes 884744 | tf_op jit(solution)/shard_map/ppermute | solution.py:82
  497.0 35.7 %collective-permute-start.74 = (bf16[4,24,768]{2,0,1:T(4,128)(2,1)}, bf16[4,24,768]{2,0,1:T(4,128)(2,1)}, u32[]{:S(2)}, u32[]{:S(2)}) collective-permute-start(bf16[4,24,768]{2,0,1:T(4,128)(2,1)} %select_bitcast_fusion.10), channel_id=1, source_target_pairs={{0,16},{16,0},{1,17},{17,1},{2,18},{18,2},{3,19},{19,3},{4,20},{20... | collective-permute-start | bytes 442376 | tf_op jit(solution)/shard_map/ppermute | solution.py:82
  (201 other events, 1490.0 us)
Sparse Core Ops, SparseCore 0:
  42.9 122.9 all-gather.1
  352.2 86.0 reduce-scatter.1
